TPU v7x, 32 devices: a whole 2x2x4 slice. The times are simulated.
32 devices in a mesh: groups: 2 (over x), tok: 16 (over z, y, core).
Axes of the slice: x: 2, y: 2, z: 4, core: 2. Of those that a mesh axis runs over, the one named last changes fastest.
Arguments:
- tokens: bfloat16 [8192, 1024], P(('groups', 'tok')), parts along dimension 0, may hold values from -6 to 6
- norm_gain: float32 [1024], replicated, may hold values from 0.1 to 1.9
- w_qk: bfloat16 [1024, 1024], replicated, may hold values from -0.1875 to 0.1875
- w_v: bfloat16 [1024, 1024], replicated, may hold values from -0.1875 to 0.1875
- cotangent: bfloat16 [8192, 1024], P(('groups', 'tok')), parts along dimension 0, may hold values from -48 to 48
- log_sums: float32 [2, 8, 8192], P(None, None, ('groups', 'tok')), parts along dimension 2, may hold values from 7 to 8
- bucket_order: int32 [2, 8192], P(None, 'groups'), parts along dimension 1, may hold values from 0 to 4095, as said below
- token_position: int32 [2, 8192], P(None, ('groups', 'tok')), parts along dimension 1, may hold values from 0 to 4095, as said below
Outputs:
- d_tokens: bfloat16 [8192, 1024], P(('groups', 'tok')), parts along dimension 0
- d_gain: float32 [2048], P(('groups', 'tok')), parts along dimension 0
- d_wqk: float32 [2048, 1024], P(('groups', 'tok')), parts along dimension 0
- d_wv: float32 [2048, 1024], P(('groups', 'tok')), parts along dimension 0
There are 2 independent parts, one for each index of `groups`. A program takes and returns all parts, laid end to end along the dimension named above; an argument that names none is the same for every part. Nothing has to cross between parts.
Inputs may be any that keep to these rules, and one draw needn't show every extreme that they name: `bucket_order`: each row is a permutation; the 256 hash-sorted positions of one device hold at most 20 tokens of any one device's 256 tokens, and exactly 20 of at least one. token_position[r, bucket_order[r, p]] = p.
All inputs are finite; a program needn't handle non-finite values.
Results may differ from a plain program's by a relative error of at most 0.025.
Values may be sent and summed in bfloat16 or wider, within the bound.
No kernel may reach another device: no remote copies, remote signals or barrier semaphores. Data moves between devices by JAX's collectives and lax.ppermute only.
A program may use at most 128 MiB of HBM per device.

v0:
```python
import math
from functools import partial

import jax
import jax.numpy as jnp
from jax import lax
from jax.experimental import pallas as pl
from jax.experimental.pallas import tpu as pltpu
from jax.sharding import PartitionSpec as P

BLOCK = 256
EPS = 1e-06
F32 = jnp.float32
BF16 = jnp.bfloat16
TILE = 8
NN = (((1,), (0,)), ((), ()))
NT = (((1,), (1,)), ((), ()))
TN = (((0,), (0,)), ((), ()))
VMEM_BYTES = 60 * 1024 * 1024


def dot(a, b, dims):
    return lax.dot_general(a, b, dims, preferred_element_type=F32)


def every(lead, size):
    return pl.ds(lead, size, stride=TILE)


def attention_kernel(
    per, parts, blocks, rounds, ids, order, log_sums, *refs
):
    qv_refs = refs[:per]
    cot_refs = refs[per : 2 * per]
    out_refs = refs[2 * per : 3 * per]
    table, picked, packed, keys, values, queries, dq, dk, dv = refs[3 * per :]
    chips = qv_refs[0].shape[0]
    size = qv_refs[0].shape[1]
    head_dim = cot_refs[0].shape[-1]
    total = table.shape[0] // TILE
    block_total = total // BLOCK
    first_block = ids[4, 0]

    for m in range(per):

        def fill(n, carry):
            base = (ids[0, n] * per + ids[3, m]) * (size * TILE)
            table[every(base, size), :] = qv_refs[m][n, :, :head_dim].astype(F32)
            table[every(base + 1, size), :] = qv_refs[m][n, :, head_dim:].astype(F32)
            base = (ids[1, n] * per + ids[3, m]) * (size * TILE)
            table[every(base + 2, size), :] = cot_refs[m][n].astype(F32)
            if parts > 1:
                zero = jnp.zeros((size, head_dim), F32)
                table[every(base + 3, size), :] = zero
                table[every(base + 4, size), :] = zero
            return carry

        lax.fori_loop(0, chips, fill, 0)

    def gather(block):
        start = block * BLOCK

        def body(step, carry):
            for u in range(32):
                p = step * 32 + u
                row = pl.multiple_of(order[start + p] * TILE, TILE)
                picked[pl.ds(pl.multiple_of(p * TILE, TILE), TILE), :] = table[pl.ds(row, TILE), :]
            return carry

        lax.fori_loop(0, BLOCK // 32, body, 0)

    def scatter(block):
        start = block * BLOCK

        def body(step, carry):
            for u in range(32):
                p = step * 32 + u
                row = pl.multiple_of(order[start + p] * TILE, TILE)
                table[pl.ds(row, TILE), :] = packed[pl.ds(pl.multiple_of(p * TILE, TILE), TILE), :]
            return carry

        lax.fori_loop(0, BLOCK // 32, body, 0)

    def load(slot):
        q = picked[every(0, BLOCK), :]
        scale = lax.rsqrt(jnp.mean(q * q, axis=-1, keepdims=True) + EPS) * (1.0 / math.sqrt(head_dim))
        queries[slot] = q
        keys[slot] = (q * scale).astype(BF16)
        values[slot] = picked[every(1, BLOCK), :].astype(BF16)

    def finish(slot, block):
        q = queries[slot]
        d_key = dk[slot]
        scale = lax.rsqrt(jnp.mean(q * q, axis=-1, keepdims=True) + EPS)
        inner = jnp.mean(q * d_key, axis=-1, keepdims=True)
        pulled = (scale * (1.0 / math.sqrt(head_dim))) * (d_key - q * (scale * scale * inner))
        packed[every(3, BLOCK), :] = dq[slot] + pulled
        packed[every(4, BLOCK), :] = dv[slot]
        scatter(block)

    halo_block = lax.rem(first_block + block_total - 1, block_total)
    gather(halo_block)
    load(2)
    dk[2] = jnp.zeros_like(dk[2])
    dv[2] = jnp.zeros_like(dv[2])
    dq[2] = jnp.zeros_like(dq[2])

    row_id = lax.broadcasted_iota(jnp.int32, (BLOCK, BLOCK), 0)
    col_id = lax.broadcasted_iota(jnp.int32, (BLOCK, BLOCK), 1)
    diagonal = row_id == col_id

    def step(b, carry):
        block = first_block + b
        cur = lax.rem(b, 2)
        prev = jnp.where(b == 0, 2, 1 - cur)
        gather(block)
        load(cur)
        log_sum = log_sums[pl.ds(block, 1), :]
        cot = picked[every(2, BLOCK), :].astype(BF16)
        query = queries[cur].astype(BF16)
        key_a, key_b = keys[prev], keys[cur]
        w_a = jnp.exp(dot(key_a, query, NT) - log_sum)
        w_b = jnp.where(diagonal, 0.0, jnp.exp(dot(key_b, query, NT) - log_sum))
        dw_a = dot(values[prev], cot, NT)
        dw_b = dot(values[cur], cot, NT)
        delta = jnp.sum(w_a * dw_a + w_b * dw_b, axis=0, keepdims=True)
        ds_a = (w_a * (dw_a - delta)).astype(BF16)
        ds_b = (w_b * (dw_b - delta)).astype(BF16)
        dv[prev] = dv[prev] + dot(w_a.astype(BF16), cot, NN)
        dv[cur] = dot(w_b.astype(BF16), cot, NN)
        dk[prev] = dk[prev] + dot(ds_a, query, NN)
        dk[cur] = dot(ds_b, query, NN)
        dq[cur] = (dot(key_a, ds_a, TN) + dot(key_b, ds_b, TN)).T

        @pl.when(b > 0)
        def _():
            finish(prev, block - 1)

        return carry

    lax.fori_loop(0, blocks, step, 0)
    last = (blocks - 1) % 2
    if parts == 1:
        dk[last] = dk[last] + dk[2]
        dv[last] = dv[last] + dv[2]
    else:
        finish(2, halo_block)
    finish(last, first_block + blocks - 1)

    for m in range(per):

        def drain(n, carry):
            base = (ids[2, n] * per + ids[3, m]) * (size * TILE)
            out_refs[m][n, :, :head_dim] = table[every(base + 3, size), :].astype(BF16)
            out_refs[m][n, :, head_dim:] = table[every(base + 4, size), :].astype(BF16)
            return carry

        lax.fori_loop(0, chips, drain, 0)


def attention(per, parts, rounds, ids, order, log_sums, qv, cot):
    chips, size, width = qv[0].shape
    head_dim = width // 2
    total = order.shape[0]
    blocks = total // BLOCK // parts
    smem = pl.BlockSpec(memory_space=pltpu.SMEM)
    vmem = pl.BlockSpec(memory_space=pltpu.VMEM)
    return pl.pallas_call(
        partial(attention_kernel, per, parts, blocks, rounds),
        out_shape=[jax.ShapeDtypeStruct((chips, size, width), BF16)] * per,
        in_specs=[smem, smem, vmem] + [vmem] * (2 * per),
        out_specs=[vmem] * per,
        scratch_shapes=[
            pltpu.VMEM((total * TILE, head_dim), F32),
            pltpu.VMEM((BLOCK * TILE, head_dim), F32),
            pltpu.VMEM((BLOCK * TILE, head_dim), F32),
            pltpu.VMEM((3, BLOCK, head_dim), BF16),
            pltpu.VMEM((3, BLOCK, head_dim), BF16),
            pltpu.VMEM((3, BLOCK, head_dim), F32),
            pltpu.VMEM((3, BLOCK, head_dim), F32),
            pltpu.VMEM((3, BLOCK, head_dim), F32),
            pltpu.VMEM((3, BLOCK, head_dim), F32),
        ],
        compiler_params=pltpu.CompilerParams(vmem_limit_bytes=VMEM_BYTES),
        name="attention",
    )(ids, order, log_sums, *qv, *cot)


def home_kernel(grads, weights, tokens, gain, out):
    total = jnp.zeros(tokens.shape, F32)
    for head in range(grads.shape[0]):
        total = total + dot(grads[head], weights[head], NT)
    x = tokens[...].astype(F32)
    scale = lax.rsqrt(jnp.mean(x * x, axis=-1, keepdims=True) + EPS)
    scaled = total * gain[...]
    inner = jnp.mean(x * scaled, axis=-1, keepdims=True)
    out[...] = (scale * (scaled - x * (scale * scale * inner))).astype(BF16)


def home(grads, weights, tokens, gain):
    return pl.pallas_call(
        home_kernel,
        out_shape=jax.ShapeDtypeStruct(tokens.shape, BF16),
        compiler_params=pltpu.CompilerParams(vmem_limit_bytes=VMEM_BYTES),
        name="home",
    )(grads, weights, tokens, gain)


def per_device(tokens, norm_gain, w_qk, w_v, cotangent, log_sums, bucket_order, token_position):
    devices = lax.axis_size("tok")
    me = lax.axis_index("tok")
    size, width = tokens.shape
    rounds, heads, _ = log_sums.shape
    head_dim = width // heads
    total = bucket_order.shape[1]
    per = devices // heads
    parts = per // rounds
    chips = heads
    chip, lane = me // per, me % per
    hashing, part = lane % rounds, lane // rounds
    groups = [[c * per + j for c in range(chips)] for j in range(per)]
    ring = list(range(0, chips, 2)) + list(range(chips - 1, 0, -2))
    place = [ring.index(c) for c in range(chips)]

    def hop(x, distance):
        route = [
            (ring[p] * per + j, ring[(p + distance) % chips] * per + j)
            for p in range(chips)
            for j in range(per)
        ]
        return lax.ppermute(x, "tok", route)

    def swap(x, shift):
        route = [
            (c * per + j, c * per + (j + shift) % per) for c in range(chips) for j in range(per)
        ]
        return lax.ppermute(x, "tok", route)

    def exchange(x):
        return lax.all_to_all(x, "tok", 0, 0, tiled=True, axis_index_groups=groups)

    def by_head(x):
        return x.reshape(x.shape[0], heads, head_dim).transpose(1, 0, 2)

    sums_all = lax.all_gather(log_sums, "tok", axis=2, tiled=True)
    my_sums = lax.dynamic_slice(sums_all, (hashing, chip, 0), (1, 1, total)).reshape(-1, BLOCK)
    my_order = lax.dynamic_index_in_dim(bucket_order, hashing, 0, keepdims=False)

    x = tokens.astype(F32)
    normal = (
        x * lax.rsqrt(jnp.mean(x * x, axis=-1, keepdims=True) + EPS) * norm_gain
    ).astype(BF16)
    cot = exchange(by_head(cotangent))

    ring_ids = jnp.array(ring, jnp.int32)
    my_place = jnp.array(place, jnp.int32)[chip]
    shards, places = [normal], [my_place]
    ahead = behind = normal
    half = chips // 2
    for s in range(1, half):
        ahead, behind = hop(ahead, 1), hop(behind, -1)
        shards += [ahead, behind]
        places += [my_place - s, my_place + s]
    shards.append(
        jnp.concatenate([hop(ahead[: size // 2], 1), hop(behind[size // 2 :], -1)], axis=0)
    )
    places.append(my_place + half)
    shard_chips = ring_ids[jnp.stack(places) % chips]

    weights = jnp.concatenate(
        [
            w_qk.reshape(width, heads, head_dim).transpose(1, 0, 2),
            w_v.reshape(width, heads, head_dim).transpose(1, 0, 2),
        ],
        axis=2,
    )
    my_weights = lax.dynamic_index_in_dim(weights, chip, 0, keepdims=False)
    qv = jnp.stack(
        [jnp.dot(n, my_weights, preferred_element_type=F32).astype(BF16) for n in shards]
    )
    qv_all = [qv] + [swap(qv, shift) for shift in range(1, per)]
    cot_all = [cot] + [swap(cot, shift) for shift in range(1, per)]
    lanes = jnp.stack([(lane - shift) % per for shift in range(per)])

    def padded(v):
        return jnp.zeros((chips,), jnp.int32).at[: v.shape[0]].set(v.astype(jnp.int32))

    own_chips = jnp.arange(chips, dtype=jnp.int32)
    ids = jnp.stack(
        [
            shard_chips,
            own_chips,
            own_chips,
            padded(lanes),
            jnp.broadcast_to(part * (total // BLOCK // parts), (chips,)).astype(jnp.int32),
        ]
    )
    sent = attention(per, parts, rounds, ids, my_order, my_sums, qv_all, cot_all)
    grads = sent[0].astype(F32)
    for shift in range(1, per):
        grads = grads + swap(sent[shift], per - shift).astype(F32)
    grads = grads.astype(BF16)

    inbound = exchange(grads)
    normal_all = jnp.concatenate(shards, axis=0)
    grads_ring = grads[shard_chips].reshape(chips * size, 2 * head_dim)
    d_weights = jnp.einsum("td,te->de", normal_all, grads_ring, preferred_element_type=F32)
    rows = width // devices
    d_weights = d_weights.astype(BF16).reshape(chips, per, rows, 2 * head_dim)
    mine = lax.dynamic_index_in_dim(d_weights, lane, 1, keepdims=False).astype(F32)
    for shift in range(1, per):
        out = lax.dynamic_index_in_dim(d_weights, (lane + shift) % per, 1, keepdims=False)
        mine = mine + swap(out, shift).astype(F32)
    d_rows = exchange(mine.astype(BF16)).astype(F32) * (1.0 / math.sqrt(total))
    d_rows = d_rows.transpose(1, 0, 2)
    d_wqk = d_rows[:, :, :head_dim].reshape(rows, width)
    d_wv = d_rows[:, :, head_dim:].reshape(rows, width)

    d_tokens = home(inbound, weights, tokens, norm_gain[None, :])

    def own(v):
        return lax.dynamic_slice_in_dim(v, me * rows, rows, 0)

    weighted = d_wqk * own(w_qk).astype(F32) + d_wv * own(w_v).astype(F32)
    d_gain = jnp.sum(weighted, axis=1) / own(norm_gain)
    return d_tokens, d_gain, d_wqk, d_wv


def solution(mesh):
    in_specs = (
        P(("groups", "tok"), None),
        P(),
        P(),
        P(),
        P(("groups", "tok"), None),
        P(None, None, ("groups", "tok")),
        P(None, "groups"),
        P(None, ("groups", "tok")),
    )
    out_specs = (
        P(("groups", "tok"), None),
        P(("groups", "tok")),
        P(("groups", "tok"), None),
        P(("groups", "tok"), None),
    )
    return jax.shard_map(
        per_device, mesh=mesh, in_specs=in_specs, out_specs=out_specs, check_vma=False
    )
```

profile of v0, /device:TPU:0, one launch (start us, length us, event | category | flops | bytes accessed | tf_op | source)
XLA Modules:
  0.0 199.1 jit_solution(2568750085535648358)
XLA Ops:
  0.7 1.4 fusion.16
  2.0 2.2 %constant_dynamic-update-slice_fusion.8 = (bf16[2048,1024]{1,0:T(8,128)(2,1)}, bf16[256,1024]{1,0:T(8,128)(2,1)}) fusion(f32[1024]{0:T(1024)} %param.13, f32[256]{0:T(256)S(1)} %add_rsqrt_fusion, bf16[256,1024]{1,0:T(8,128)(2,1)} %tokens.1), kind=kLoop, calls=%fused_computation.65 | loop fusion | flops 1048575 | bytes 1577984
  4.3 3.0 %collective-permute-start = (bf16[256,1024]{1,0:T(8,128)(2,1)}, bf16[256,1024]{1,0:T(8,128)(2,1)S(1)}, u32[]{:S(2)}, u32[]{:S(2)}) collective-permute-start(bf16[256,1024]{1,0:T(8,128)(2,1)} %get-tuple-element.24), channel_id=1, source_target_pairs={{0,4},{1,5},{4,8},{5,9},{8,12},{9,13},{12,14},{13,15},{14,10},{15,... | collective-permute-start | bytes 1572872 | tf_op jit(solution)/shard_map/ppermute | solution.py:231
  9.5 6.3 %all-to-all-start = ((bf16[8,256,128]{2,1,0:T(8,128)(2,1)}), bf16[8,256,128]{2,1,0:T(8,128)(2,1)}, u32[]{:S(2)}, u32[]{:S(2)}) async-start(bf16[8,256,128]{2,1,0:T(8,128)(2,1)} %bitcast.28), calls=%async_computation | async-start | bytes 1048576 | tf_op jit(solution)/shard_map/all_to_all | solution.py:240
  15.8 2.6 %copy.15 = bf16[1024,1024]{0,1:T(8,128)(2,1)} copy(bf16[1024,1024]{1,0:T(8,128)(2,1)S(1)} %copy-done.5) | data formatting | bytes 4194304 | tf_op args[2]
  18.4 3.0 %copy.16 = bf16[1024,8,128]{2,0,1:T(8,128)(2,1)S(1)} copy(bf16[1024,8,128]{0,2,1:T(8,128)(2,1)} %bitcast.108) | data formatting | bytes 4194304 | tf_op jit(solution)/shard_map/reshape | solution.py:272
  21.4 4.0 %copy.17 = bf16[1024,1024]{0,1:T(8,128)(2,1)} copy(bf16[1024,1024]{1,0:T(8,128)(2,1)} %param.15) | data formatting | bytes 4194304 | tf_op args[3]
  25.5 3.9 %copy.18 = bf16[1024,8,128]{2,0,1:T(8,128)(2,1)} copy(bf16[1024,8,128]{0,2,1:T(8,128)(2,1)} %bitcast.109) | data formatting | bytes 4194304 | tf_op jit(solution)/shard_map/reshape | solution.py:273
  30.4 2.0 %collective-permute-start.2 = (bf16[256,1024]{1,0:T(8,128)(2,1)S(1)}, bf16[256,1024]{1,0:T(8,128)(2,1)}, u32[]{:S(2)}, u32[]{:S(2)}) collective-permute-start(bf16[256,1024]{1,0:T(8,128)(2,1)S(1)} %collective-permute-done), channel_id=1, source_target_pairs={{0,4},{1,5},{4,8},{5,9},{8,12},{9,13},{12,14},{13,15},{14,10},{15,... | collective-permute-start | bytes 1572872 | tf_op jit(solution)/shard_map/ppermute | solution.py:231
  32.6 26.6 %all_gather.3 = f32[2,8,4096]{2,1,0:T(8,128)S(1)} all-gather(f32[2,8,256]{2,1,0:T(8,128)S(1)} %copy-done.12), channel_id=1, replica_groups=mesh['groups'=2,'tok'=16] {'tok'}, dimensions={2}, use_global_device_ids=true | all-gather | bytes 278528 | tf_op jit(solution)/shard_map/all_gather | solution.py:245
  65.7 2.0 %fusion.1 = bf16[8,256,256]{2,1,0:T(8,128)(2,1)} fusion(bf16[256,1024]{1,0:T(8,128)(2,1)} %get-tuple-element.24, bf16[1,1024,256]{2,1,0:T(8,128)(2,1)S(1)} %fusion.19), kind=kOutput, calls=%fused_computation.18 | convolution fusion | flops 134283264 | bytes 1179648 | tf_op jit(solution)/shard_map/dot_general | solution.py:279
  68.7 2.0 %collective-permute-start.5 = (bf16[256,1024]{1,0:T(8,128)(2,1)}, bf16[256,1024]{1,0:T(8,128)(2,1)S(1)}, u32[]{:S(2)}, u32[]{:S(2)}) collective-permute-start(bf16[256,1024]{1,0:T(8,128)(2,1)} %collective-permute-done.3), channel_id=1, source_target_pairs={{0,2},{1,3},{4,0},{5,1},{8,4},{9,5},{12,8},{13,9},{14,12},{15,13},... | collective-permute-start | bytes 1572872 | tf_op jit(solution)/shard_map/ppermute | solution.py:231
  70.7 2.0 %fusion.5 = bf16[8,256,256]{2,1,0:T(8,128)(2,1)} fusion(bf16[8,256,256]{2,1,0:T(8,128)(2,1)} %fusion.3, bf16[256,1024]{1,0:T(8,128)(2,1)} %collective-permute-done.1, bf16[1,1024,256]{2,1,0:T(8,128)(2,1)S(1)} %fusion.19), kind=kOutput, calls=%fused_computation.22 | convolution fusion | flops 134283264 | bytes 1179648 | tf_op jit(solution)/shard_map/dot_general | solution.py:279
  72.7 2.0 %fusion.7 = bf16[8,256,256]{2,1,0:T(8,128)(2,1)} fusion(bf16[8,256,256]{2,1,0:T(8,128)(2,1)} %fusion.5, bf16[256,1024]{1,0:T(8,128)(2,1)} %collective-permute-done.2, bf16[1,1024,256]{2,1,0:T(8,128)(2,1)S(1)} %fusion.19), kind=kOutput, calls=%fused_computation.24 | convolution fusion | flops 134283264 | bytes 1179648 | tf_op jit(solution)/shard_map/dot_general | solution.py:279
  74.7 2.0 fusion.9
  76.7 6.4 %collective-permute-done.4 = bf16[256,1024]{1,0:T(8,128)(2,1)S(1)} collective-permute-done((bf16[256,1024]{1,0:T(8,128)(2,1)}, bf16[256,1024]{1,0:T(8,128)(2,1)S(1)}, u32[]{:S(2)}, u32[]{:S(2)}) %collective-permute-start.4) | collective-permute-done | bytes 524320 | tf_op jit(solution)/shard_map/ppermute | solution.py:231
  83.4 1.8 collective-permute-start.7
  87.1 3.7 %collective-permute-done.6 = bf16[128,1024]{1,0:T(8,128)(2,1)S(1)} collective-permute-done((bf16[128,1024]{1,0:T(8,128)(2,1)S(1)}, bf16[128,1024]{1,0:T(8,128)(2,1)S(1)}, u32[]{:S(2)}, u32[]{:S(2)}) %collective-permute-start.6) | collective-permute-done | bytes 262176 | tf_op jit(solution)/shard_map/ppermute | solution.py:231
  96.7 34.1 %attention.1 = (bf16[8,256,256]{2,1,0:T(8,128)(2,1)}, bf16[8,256,256]{2,1,0:T(8,128)(2,1)}) custom-call(s32[5,8]{1,0:T(8,128)} %stack.87.ids, s32[4096]{0:T(1024)} %bitcast.114, f32[16,256]{1,0:T(8,128)} %reshape.447.log_sums, bf16[8,256,256]{2,1,0:T(8,128)(2,1)} %fusion.15.refs_0_, bf16[8,256,256]{2,1,0:T(8,128)(2,1)} %collective-permute-done.8.refs_1_, ...), custom_call_target="tpu_custom_call" | custom-call | tf_op jit(solution)/shard_map/attention/pallas_call | solution.py:168
  130.9 2.0 constant_dynamic-update-slice_fusion.7
  132.9 1.9 constant_dynamic-update-slice_fusion.6
  134.7 1.9 constant_dynamic-update-slice_fusion.5
  136.6 1.9 constant_dynamic-update-slice_fusion.4
  142.8 1.8 gather_fusion.1
  144.6 3.5 %convolution_convert_fusion = bf16[1024,256]{1,0:T(8,128)(2,1)S(1)} fusion(bf16[2048,1024]{1,0:T(8,128)(2,1)} %constant_dynamic-update-slice_fusion, bf16[2048,256]{1,0:T(8,128)(2,1)S(1)} %bitcast.111), kind=kOutput, calls=%fused_computation.8 | convolution fusion | flops 1074003968 | bytes 5767168 | tf_op jit(solution)/shard_map/td,te->de/dot_general | solution.py:307
  151.6 12.1 %all_to_all.15 = bf16[8,64,256]{2,1,0:T(8,128)(2,1)S(1)} all-to-all(bf16[8,64,256]{2,1,0:T(8,128)(2,1)S(1)} %fusion.23), channel_id=1, replica_groups={{0,2,4,6,8,10,12,14},{1,3,5,7,9,11,13,15},{16,18,20,22,24,26,28,30},{17..., dimensions={0} | all-to-all | bytes 524288 | tf_op jit(solution)/shard_map/all_to_all | solution.py:240
  163.7 3.6 %all-to-all-start.1 = ((bf16[8,256,256]{2,1,0:T(8,128)(2,1)}), bf16[8,256,256]{2,1,0:T(8,128)(2,1)S(1)}, u32[]{:S(2)}, u32[]{:S(2)}) async-start(bf16[8,256,256]{2,1,0:T(8,128)(2,1)} %add_convert_fusion), calls=%async_computation.1 | async-start | bytes 2097152 | tf_op jit(solution)/shard_map/all_to_all | solution.py:240
  167.3 4.0 %pad_maximum_fusion.weights = bf16[8,1024,256]{2,1,0:T(8,128)(2,1)} fusion(bf16[8,1024,128]{2,1,0:T(8,128)(2,1)} %bitcast.107, bf16[8,1024,128]{2,1,0:T(8,128)(2,1)S(1)} %bitcast.105), kind=kLoop, calls=%fused_computation.3 | loop fusion | flops 8388608 | bytes 8388608 | tf_op jit(solution)/shard_map/concatenate | solution.py:270
  171.4 1.9 add_reduce_fusion
  173.3 1.3 dynamic-slice_divide_fusion
  174.6 18.7 %all-to-all-done.1.grads = bf16[8,256,256]{2,1,0:T(8,128)(2,1)S(1)} async-done(((bf16[8,256,256]{2,1,0:T(8,128)(2,1)}), bf16[8,256,256]{2,1,0:T(8,128)(2,1)S(1)}, u32[]{:S(2)}, u32[]{:S(2)}) %all-to-all-start.1) | async-done | bytes 1048608 | tf_op jit(solution)/shard_map/all_to_all | solution.py:240
  194.2 4.9 %home.1 = bf16[256,1024]{1,0:T(8,128)(2,1)} custom-call(bf16[8,256,256]{2,1,0:T(8,128)(2,1)} %copy-done.2, bf16[8,1024,256]{2,1,0:T(8,128)(2,1)} %pad_maximum_fusion.weights, bf16[256,1024]{1,0:T(8,128)(2,1)} %tokens.1, f32[1,1024]{1,0:T(1,128)} %bitcast.115), custom_call_target="tpu_custom_call" | custom-call | tf_op jit(solution)/shard_map/home/pallas_call | solution.py:201
  (81 shorter events, 23.4 us)
Async XLA Ops:
  0.6 93.6 %copy-start = (s32[2,4096]{1,0:T(2,128)S(1)}, s32[2,4096]{1,0:T(2,128)}, u32[]{:S(2)}) copy-start(s32[2,4096]{1,0:T(2,128)} %param.18) | copy-start | bytes 98308
  0.6 15.2 %copy-start.5 = (bf16[1024,1024]{1,0:T(8,128)(2,1)S(1)}, bf16[1024,1024]{1,0:T(8,128)(2,1)}, u32[]{:S(2)}) copy-start(bf16[1024,1024]{1,0:T(8,128)(2,1)} %param.14) | copy-start | bytes 6291460
  4.3 26.1 %collective-permute-start = (bf16[256,1024]{1,0:T(8,128)(2,1)}, bf16[256,1024]{1,0:T(8,128)(2,1)S(1)}, u32[]{:S(2)}, u32[]{:S(2)}) collective-permute-start(bf16[256,1024]{1,0:T(8,128)(2,1)} %get-tuple-element.24), channel_id=1, source_target_pairs={{0,4},{1,5},{4,8},{5,9},{8,12},{9,13},{12,14},{13,15},{14,10},{15,... | collective-permute-start | bytes 1572872 | tf_op jit(solution)/shard_map/ppermute | solution.py:231
  7.3 25.2 %collective-permute-start.1 = (bf16[256,1024]{1,0:T(8,128)(2,1)}, bf16[256,1024]{1,0:T(8,128)(2,1)}, u32[]{:S(2)}, u32[]{:S(2)}) collective-permute-start(bf16[256,1024]{1,0:T(8,128)(2,1)} %get-tuple-element.24), channel_id=1, source_target_pairs={{0,2},{1,3},{4,0},{5,1},{8,4},{9,5},{12,8},{13,9},{14,12},{15,13},... | collective-permute-start | bytes 1572872 | tf_op jit(solution)/shard_map/ppermute | solution.py:231
  9.5 83.4 %all-to-all-start = ((bf16[8,256,128]{2,1,0:T(8,128)(2,1)}), bf16[8,256,128]{2,1,0:T(8,128)(2,1)}, u32[]{:S(2)}, u32[]{:S(2)}) async-start(bf16[8,256,128]{2,1,0:T(8,128)(2,1)} %bitcast.28), calls=%async_computation | async-start | bytes 1048576 | tf_op jit(solution)/shard_map/all_to_all | solution.py:240
  25.4 7.1 %copy-start.12 = (f32[2,8,256]{2,1,0:T(8,128)S(1)}, f32[2,8,256]{2,1,0:T(8,128)}, u32[]{:S(2)}) copy-start(f32[2,8,256]{2,1,0:T(8,128)} %param.17) | copy-start | bytes 49156
  25.5 34.3 %copy-start.13 = (s32[8]{0:T(128)S(1)}, s32[8]{0:T(128)}, u32[]{:S(2)}) copy-start(s32[8]{0:T(128)} %constant.145.clone) | copy-start | bytes 100
  30.4 38.2 %copy-start.6 = (bf16[256,1024]{1,0:T(8,128)(2,1)}, bf16[256,1024]{1,0:T(8,128)(2,1)S(1)}, u32[]{:S(2)}) copy-start(bf16[256,1024]{1,0:T(8,128)(2,1)S(1)} %collective-permute-done) | copy-start | bytes 1572868
  30.4 38.2 %collective-permute-start.2 = (bf16[256,1024]{1,0:T(8,128)(2,1)S(1)}, bf16[256,1024]{1,0:T(8,128)(2,1)}, u32[]{:S(2)}, u32[]{:S(2)}) collective-permute-start(bf16[256,1024]{1,0:T(8,128)(2,1)S(1)} %collective-permute-done), channel_id=1, source_target_pairs={{0,4},{1,5},{4,8},{5,9},{8,12},{9,13},{12,14},{13,15},{14,10},{15,... | collective-permute-start | bytes 1572872 | tf_op jit(solution)/shard_map/ppermute | solution.py:231
  32.5 36.2 %collective-permute-start.3 = (bf16[256,1024]{1,0:T(8,128)(2,1)}, bf16[256,1024]{1,0:T(8,128)(2,1)}, u32[]{:S(2)}, u32[]{:S(2)}) collective-permute-start(bf16[256,1024]{1,0:T(8,128)(2,1)} %collective-permute-done.1), channel_id=1, source_target_pairs={{0,2},{1,3},{4,0},{5,1},{8,4},{9,5},{12,8},{13,9},{14,12},{15,13},... | collective-permute-start | bytes 1572872 | tf_op jit(solution)/shard_map/ppermute | solution.py:231
  68.6 23.7 %copy-start.1 = (s32[8]{0:T(128)S(1)}, s32[8]{0:T(128)}, u32[]{:S(2)}) copy-start(s32[8]{0:T(128)} %constant.144.clone) | copy-start | bytes 100
  68.6 14.4 %collective-permute-start.4 = (bf16[256,1024]{1,0:T(8,128)(2,1)}, bf16[256,1024]{1,0:T(8,128)(2,1)S(1)}, u32[]{:S(2)}, u32[]{:S(2)}) collective-permute-start(bf16[256,1024]{1,0:T(8,128)(2,1)} %collective-permute-done.2), channel_id=1, source_target_pairs={{0,4},{1,5},{4,8},{5,9},{8,12},{9,13},{12,14},{13,15},{14,10},{15,... | collective-permute-start | bytes 1572872 | tf_op jit(solution)/shard_map/ppermute | solution.py:231
  68.7 14.7 %collective-permute-start.5 = (bf16[256,1024]{1,0:T(8,128)(2,1)}, bf16[256,1024]{1,0:T(8,128)(2,1)S(1)}, u32[]{:S(2)}, u32[]{:S(2)}) collective-permute-start(bf16[256,1024]{1,0:T(8,128)(2,1)} %collective-permute-done.3), channel_id=1, source_target_pairs={{0,2},{1,3},{4,0},{5,1},{8,4},{9,5},{12,8},{13,9},{14,12},{15,13},... | collective-permute-start | bytes 1572872 | tf_op jit(solution)/shard_map/ppermute | solution.py:231
  83.1 7.8 %collective-permute-start.6 = (bf16[128,1024]{1,0:T(8,128)(2,1)S(1)}, bf16[128,1024]{1,0:T(8,128)(2,1)S(1)}, u32[]{:S(2)}, u32[]{:S(2)}) collective-permute-start(bf16[128,1024]{1,0:T(8,128)(2,1)S(1)} %slice.31), channel_id=1, source_target_pairs={{0,4},{1,5},{4,8},{5,9},{8,12},{9,13},{12,14},{13,15},{14,10},{15,... | collective-permute-start | bytes 786440 | tf_op jit(solution)/shard_map/ppermute | solution.py:231
  83.4 8.8 %copy-start.3 = (bf16[256,1024]{1,0:T(8,128)(2,1)}, bf16[256,1024]{1,0:T(8,128)(2,1)S(1)}, u32[]{:S(2)}) copy-start(bf16[256,1024]{1,0:T(8,128)(2,1)S(1)} %collective-permute-done.5) | copy-start | bytes 1572868
  83.4 7.8 %collective-permute-start.7 = (bf16[128,1024]{1,0:T(8,128)(2,1)S(1)}, bf16[128,1024]{1,0:T(8,128)(2,1)S(1)}, u32[]{:S(2)}, u32[]{:S(2)}) collective-permute-start(bf16[128,1024]{1,0:T(8,128)(2,1)S(1)} %slice.32), channel_id=1, source_target_pairs={{0,2},{1,3},{4,0},{5,1},{8,4},{9,5},{12,8},{13,9},{14,12},{15,13},... | collective-permute-start | bytes 786440 | tf_op jit(solution)/shard_map/ppermute | solution.py:231
  91.3 1.0 copy-start.10
  92.2 3.6 %collective-permute-start.8 = (bf16[8,256,256]{2,1,0:T(8,128)(2,1)}, bf16[8,256,256]{2,1,0:T(8,128)(2,1)}, u32[]{:S(2)}, u32[]{:S(2)}) collective-permute-start(bf16[8,256,256]{2,1,0:T(8,128)(2,1)} %fusion.15.refs_0_), channel_id=1, source_target_pairs={{0,1},{1,0},{2,3},{3,2},{4,5},{5,4},{6,7},{7,6},{8,9},{9,8},{10,11... | collective-permute-start | bytes 3145736 | tf_op jit(solution)/shard_map/ppermute | solution.py:237
  93.0 2.9 %collective-permute-start.9 = (bf16[8,256,128]{2,1,0:T(8,128)(2,1)}, bf16[8,256,128]{2,1,0:T(8,128)(2,1)S(1)}, u32[]{:S(2)}, u32[]{:S(2)}) collective-permute-start(bf16[8,256,128]{2,1,0:T(8,128)(2,1)} %all-to-all-done.refs_2_), channel_id=1, source_target_pairs={{0,1},{1,0},{2,3},{3,2},{4,5},{5,4},{6,7},{7,6},{8,9},{9,8},{10,11... | collective-permute-start | bytes 1572872 | tf_op jit(solution)/shard_map/ppermute | solution.py:237
  95.9 0.8 copy-start.8
  96.7 42.6 %copy-start.4 = (bf16[256,1024]{1,0:T(8,128)(2,1)S(1)}, bf16[256,1024]{1,0:T(8,128)(2,1)}, u32[]{:S(2)}) copy-start(bf16[256,1024]{1,0:T(8,128)(2,1)} %copy-done.3) | copy-start | bytes 1572868
  130.8 10.1 %copy-start.11 = (bf16[128,1024]{1,0:T(8,128)(2,1)S(1)}, bf16[128,1024]{1,0:T(8,128)(2,1)}, u32[]{:S(2)}) copy-start(bf16[128,1024]{1,0:T(8,128)(2,1)} %copy-done.10) | copy-start | bytes 786436
  130.8 10.8 %copy-start.7 = (bf16[8,256,256]{2,1,0:T(8,128)(2,1)S(1)}, bf16[8,256,256]{2,1,0:T(8,128)(2,1)}, u32[]{:S(2)}) copy-start(bf16[8,256,256]{2,1,0:T(8,128)(2,1)} %get-tuple-element.18) | copy-start | bytes 3145732
  130.8 10.8 %collective-permute-start.10 = (bf16[8,256,256]{2,1,0:T(8,128)(2,1)}, bf16[8,256,256]{2,1,0:T(8,128)(2,1)S(1)}, u32[]{:S(2)}, u32[]{:S(2)}) collective-permute-start(bf16[8,256,256]{2,1,0:T(8,128)(2,1)} %get-tuple-element.19), channel_id=1, source_target_pairs={{0,1},{1,0},{2,3},{3,2},{4,5},{5,4},{6,7},{7,6},{8,9},{9,8},{10,11... | collective-permute-start | bytes 3145736 | tf_op jit(solution)/shard_map/ppermute | solution.py:237
  148.1 0.8 copy-start.9
  148.9 1.6 collective-permute-start.11
  163.7 29.5 %all-to-all-start.1 = ((bf16[8,256,256]{2,1,0:T(8,128)(2,1)}), bf16[8,256,256]{2,1,0:T(8,128)(2,1)S(1)}, u32[]{:S(2)}, u32[]{:S(2)}) async-start(bf16[8,256,256]{2,1,0:T(8,128)(2,1)} %add_convert_fusion), calls=%async_computation.1 | async-start | bytes 2097152 | tf_op jit(solution)/shard_map/all_to_all | solution.py:240
  193.2 1.0 copy-start.2
where the time goes:
time: 200 us; the launch traced here: 199 us
  Pallas kernels  39 us (20%)
  blocking collectives  38.7 us (19%)
  local copies, waits for them, and re-layouts  34.9 us (17%)
  waiting for transfers between devices  31.4 us (16%)
  starting transfers between devices  20.3 us (10%)
  matrix products  15.3 us (8%)
  other arithmetic  14.2 us (7%)
  between operations  5.36 us (3%)
    pallas_call x1, Pallas kernels, attention(): pl.pallas_call(partial(attention_kernel, per, parts, blocks, rounds), out...  34.1 us
    all_gather x1, blocking collectives, per_device(): sums_all = lax.all_gather(log_sums, 'tok', axis=2, tiled=True)  26.6 us
    unnamed x39, local copies, waits for them, and re-layouts  20.4 us
    all_to_all x2, waiting for transfers between devices, exchange(): return lax.all_to_all(x, 'tok', 0, 0, tiled=True, axis_index_groups=groups)  18.7 us
    all_to_all x1, blocking collectives, exchange(): return lax.all_to_all(x, 'tok', 0, 0, tiled=True, axis_index_groups=groups)  12.1 us
    dot_general x8, matrix products, per_device(): jnp.dot(n, my_weights, preferred_element_type=F32).astype(BF16)  11.8 us
    ppermute x8, waiting for transfers between devices, hop(): return lax.ppermute(x, 'tok', route)  10.5 us
    all_to_all x2, starting transfers between devices, exchange(): return lax.all_to_all(x, 'tok', 0, 0, tiled=True, axis_index_groups=groups)  9.85 us
  transfers between devices with their start and end apart: 14, of which 6 were waited for; matrix products, arithmetic and copies ran while one was open for 25% of the time, Pallas kernels for 0%

commit v1 on v0

v1 whole, which is shorter than its diff:
```python
import math
from functools import partial

import jax
import jax.numpy as jnp
import numpy as np
from jax import lax
from jax.experimental import pallas as pl
from jax.experimental.pallas import tpu as pltpu
from jax.sharding import PartitionSpec as P

BLOCK = 256
EPS = 1e-06
F32 = jnp.float32
BF16 = jnp.bfloat16
TILE = 8
NN = (((1,), (0,)), ((), ()))
NT = (((1,), (1,)), ((), ()))
TN = (((0,), (0,)), ((), ()))
VMEM_BYTES = 60 * 1024 * 1024
SMALL_VMEM_BYTES = 24 * 1024 * 1024
SHARDS, LANES = 0, 1


def dot(a, b, dims):
    return lax.dot_general(a, b, dims, preferred_element_type=F32)


def every(lead, size):
    return pl.ds(lead, size, stride=TILE)


def attention_kernel(per, parts, blocks, rounds, pieces, ids, order, *refs):
    qv_refs = [refs[m * pieces : (m + 1) * pieces] for m in range(per)]
    refs = refs[per * pieces :]
    cot_refs = refs[:per]
    out_refs = refs[per : 2 * per]
    table, picked, packed, log_sums, keys, values, queries, dq, dk, dv = refs[2 * per :]
    chips, size, width = out_refs[0].shape
    head_dim = width // 2
    total = table.shape[0] // TILE
    block_total = total // BLOCK
    sum_rows = size // head_dim
    lo_start = rounds * sum_rows
    hashing = ids[LANES, per]
    first_block = ids[LANES, per + 1]

    for m in range(per):
        n = 0
        for ref in qv_refs[m]:
            for row in range(ref.shape[0]):
                base = (ids[SHARDS, n] * per + ids[LANES, m]) * (size * TILE)
                table[every(base, size), :] = ref[row, :, :head_dim].astype(F32)
                table[every(base + 1, size), :] = ref[row, :, head_dim:].astype(F32)
                n += 1

        def fill(n, carry):
            device = n * per + ids[LANES, m]
            base = device * (size * TILE)
            table[every(base + 2, size), :] = cot_refs[m][n, :size, :].astype(F32)
            if parts > 1:
                zero = jnp.zeros((size, head_dim), F32)
                table[every(base + 3, size), :] = zero
                table[every(base + 4, size), :] = zero
            sums = cot_refs[m][n, size:, :].astype(F32)
            sums = sums[:lo_start] + sums[lo_start : 2 * lo_start]
            chosen = sums[:sum_rows]
            for r in range(1, rounds):
                chosen = jnp.where(hashing == r, sums[r * sum_rows : (r + 1) * sum_rows], chosen)
            log_sums[device, :sum_rows, :] = chosen
            return carry

        lax.fori_loop(0, chips, fill, 0)

    def gather(block):
        start = block * BLOCK

        def body(step, carry):
            for u in range(32):
                p = step * 32 + u
                row = pl.multiple_of(order[start + p] * TILE, TILE)
                picked[pl.ds(pl.multiple_of(p * TILE, TILE), TILE), :] = table[pl.ds(row, TILE), :]
            return carry

        lax.fori_loop(0, BLOCK // 32, body, 0)

    def scatter(block):
        start = block * BLOCK

        def body(step, carry):
            for u in range(32):
                p = step * 32 + u
                row = pl.multiple_of(order[start + p] * TILE, TILE)
                table[pl.ds(row, TILE), :] = packed[pl.ds(pl.multiple_of(p * TILE, TILE), TILE), :]
            return carry

        lax.fori_loop(0, BLOCK // 32, body, 0)

    def load(slot):
        q = picked[every(0, BLOCK), :]
        scale = lax.rsqrt(jnp.mean(q * q, axis=-1, keepdims=True) + EPS) * (1.0 / math.sqrt(head_dim))
        queries[slot] = q
        keys[slot] = (q * scale).astype(BF16)
        values[slot] = picked[every(1, BLOCK), :].astype(BF16)

    def finish(slot, block):
        q = queries[slot]
        d_key = dk[slot]
        scale = lax.rsqrt(jnp.mean(q * q, axis=-1, keepdims=True) + EPS)
        inner = jnp.mean(q * d_key, axis=-1, keepdims=True)
        pulled = (scale * (1.0 / math.sqrt(head_dim))) * (d_key - q * (scale * scale * inner))
        packed[every(3, BLOCK), :] = dq[slot] + pulled
        packed[every(4, BLOCK), :] = dv[slot]
        scatter(block)

    halo_block = lax.rem(first_block + block_total - 1, block_total)
    gather(halo_block)
    load(2)
    dk[2] = jnp.zeros_like(dk[2])
    dv[2] = jnp.zeros_like(dv[2])
    dq[2] = jnp.zeros_like(dq[2])

    row_id = lax.broadcasted_iota(jnp.int32, (BLOCK, BLOCK), 0)
    col_id = lax.broadcasted_iota(jnp.int32, (BLOCK, BLOCK), 1)
    diagonal = row_id == col_id

    def step(b, carry):
        block = first_block + b
        cur = lax.rem(b, 2)
        prev = jnp.where(b == 0, 2, 1 - cur)
        gather(block)
        load(cur)
        log_sum = jnp.concatenate(
            [log_sums[block, k : k + 1, :] for k in range(BLOCK // head_dim)], axis=1
        )
        cot = picked[every(2, BLOCK), :].astype(BF16)
        query = queries[cur].astype(BF16)
        key_a, key_b = keys[prev], keys[cur]
        w_a = jnp.exp(dot(key_a, query, NT) - log_sum)
        w_b = jnp.where(diagonal, 0.0, jnp.exp(dot(key_b, query, NT) - log_sum))
        dw_a = dot(values[prev], cot, NT)
        dw_b = dot(values[cur], cot, NT)
        delta = jnp.sum(w_a * dw_a + w_b * dw_b, axis=0, keepdims=True)
        ds_a = (w_a * (dw_a - delta)).astype(BF16)
        ds_b = (w_b * (dw_b - delta)).astype(BF16)
        dv[prev] = dv[prev] + dot(w_a.astype(BF16), cot, NN)
        dv[cur] = dot(w_b.astype(BF16), cot, NN)
        dk[prev] = dk[prev] + dot(ds_a, query, NN)
        dk[cur] = dot(ds_b, query, NN)
        dq[cur] = (dot(key_a, ds_a, TN) + dot(key_b, ds_b, TN)).T

        @pl.when(b > 0)
        def _():
            finish(prev, block - 1)

        return carry

    lax.fori_loop(0, blocks, step, 0)
    last = (blocks - 1) % 2
    if parts == 1:
        dk[last] = dk[last] + dk[2]
        dv[last] = dv[last] + dv[2]
    else:
        finish(2, halo_block)
    finish(last, first_block + blocks - 1)

    for m in range(per):

        def drain(n, carry):
            base = (n * per + ids[LANES, m]) * (size * TILE)
            out_refs[m][n, :, :head_dim] = table[every(base + 3, size), :].astype(BF16)
            out_refs[m][n, :, head_dim:] = table[every(base + 4, size), :].astype(BF16)
            return carry

        lax.fori_loop(0, chips, drain, 0)


def attention(per, parts, rounds, ids, order, qv, cot):
    chips = cot[0].shape[0]
    size, width = qv[0][0].shape[1:]
    head_dim = width // 2
    total = order.shape[0]
    blocks = total // BLOCK // parts
    smem = pl.BlockSpec(memory_space=pltpu.SMEM)
    vmem = pl.BlockSpec(memory_space=pltpu.VMEM)
    flat = [piece for lane in qv for piece in lane] + list(cot)
    return pl.pallas_call(
        partial(attention_kernel, per, parts, blocks, rounds, len(qv[0])),
        out_shape=[jax.ShapeDtypeStruct((chips, size, width), BF16)] * per,
        in_specs=[smem, smem] + [vmem] * len(flat),
        out_specs=[vmem] * per,
        scratch_shapes=[
            pltpu.VMEM((total * TILE, head_dim), F32),
            pltpu.VMEM((BLOCK * TILE, head_dim), F32),
            pltpu.VMEM((BLOCK * TILE, head_dim), F32),
            pltpu.VMEM((total // BLOCK, TILE, head_dim), F32),
            pltpu.VMEM((3, BLOCK, head_dim), BF16),
            pltpu.VMEM((3, BLOCK, head_dim), BF16),
            pltpu.VMEM((3, BLOCK, head_dim), F32),
            pltpu.VMEM((3, BLOCK, head_dim), F32),
            pltpu.VMEM((3, BLOCK, head_dim), F32),
            pltpu.VMEM((3, BLOCK, head_dim), F32),
        ],
        compiler_params=pltpu.CompilerParams(vmem_limit_bytes=VMEM_BYTES),
        name="attention",
    )(ids, order, *flat)


def prepare_kernel(tokens, gain, cot, log_sums, normal, chunks):
    heads, _, head_dim = chunks.shape
    size = tokens.shape[0]
    rounds = log_sums.shape[0]
    x = tokens[...].astype(F32)
    scale = lax.rsqrt(jnp.mean(x * x, axis=-1, keepdims=True) + EPS)
    normal[...] = (x * scale * gain[...]).astype(BF16)
    for h in range(heads):
        chunks[h, :size, :] = cot[:, h * head_dim : (h + 1) * head_dim]
        rows = [
            log_sums[r, h : h + 1, k * head_dim : (k + 1) * head_dim]
            for r in range(rounds)
            for k in range(size // head_dim)
        ]
        exact = jnp.concatenate(rows, axis=0)
        high = exact.astype(BF16).astype(F32)
        spare = jnp.zeros((chunks.shape[1] - size - 2 * len(rows), head_dim), F32)
        chunks[h, size:, :] = jnp.concatenate([high, exact - high, spare], axis=0).astype(BF16)


def prepare(tokens, gain, cot, log_sums):
    size, width = tokens.shape
    rounds, heads, _ = log_sums.shape
    head_dim = width // heads
    extra = 2 * rounds * size // head_dim
    extra = (extra + 15) // 16 * 16
    return pl.pallas_call(
        prepare_kernel,
        out_shape=[
            jax.ShapeDtypeStruct(tokens.shape, BF16),
            jax.ShapeDtypeStruct((heads, size + extra, head_dim), BF16),
        ],
        compiler_params=pltpu.CompilerParams(vmem_limit_bytes=SMALL_VMEM_BYTES),
        name="prepare",
    )(tokens, gain, cot, log_sums)


def weight_grad_kernel(per, count, ids, grads, *refs):
    shards = refs[:count]
    outs = refs[count : count + per]
    total = refs[count + per]
    chips, rows, _ = outs[0].shape
    grad_t = jnp.zeros((grads.shape[-1], shards[0].shape[-1]), F32)
    n = 0
    for shard in shards:
        grad_t = grad_t + dot(grads[ids[SHARDS, n]], shard[...], TN)
        n += 1
    total[...] = grad_t.T
    for m in range(per):
        for c in range(chips):
            start = pl.multiple_of((c * per + ids[LANES, m]) * rows, rows)
            outs[m][c] = total[pl.ds(start, rows), :].astype(BF16)


def weight_grad(per, rows, ids, grads, shards):
    chips, _, both = grads.shape
    smem = pl.BlockSpec(memory_space=pltpu.SMEM)
    vmem = pl.BlockSpec(memory_space=pltpu.VMEM)
    return pl.pallas_call(
        partial(weight_grad_kernel, per, len(shards)),
        out_shape=[jax.ShapeDtypeStruct((chips, rows, both), BF16)] * per,
        in_specs=[smem, vmem] + [vmem] * len(shards),
        out_specs=[vmem] * per,
        scratch_shapes=[pltpu.VMEM((shards[0].shape[1], both), F32)],
        compiler_params=pltpu.CompilerParams(vmem_limit_bytes=SMALL_VMEM_BYTES),
        name="weight_grad",
    )(ids, grads, *shards)


def home_kernel(scale_out, ids, grads, d_rows, w_qk, w_v, tokens, gain, out, d_wqk, d_wv, d_gain):
    heads, rows, both = d_rows.shape
    head_dim = both // 2
    total = jnp.zeros(tokens.shape, F32)
    start = pl.multiple_of(ids[LANES, ids.shape[1] - 1] * rows, rows)
    gains = jnp.zeros((rows, 1), F32)
    for head in range(heads):
        columns = slice(head * head_dim, (head + 1) * head_dim)
        weights = jnp.concatenate([w_qk[:, columns], w_v[:, columns]], axis=1)
        total = total + dot(grads[head], weights, NT)
        qk_rows = d_rows[head, :, :head_dim].astype(F32) * scale_out
        v_rows = d_rows[head, :, head_dim:].astype(F32) * scale_out
        d_wqk[:, columns] = qk_rows
        d_wv[:, columns] = v_rows
        own = qk_rows * w_qk[pl.ds(start, rows), columns].astype(F32)
        own = own + v_rows * w_v[pl.ds(start, rows), columns].astype(F32)
        gains = gains + jnp.sum(own, axis=1, keepdims=True)
    d_gain[...] = gains
    x = tokens[...].astype(F32)
    scale = lax.rsqrt(jnp.mean(x * x, axis=-1, keepdims=True) + EPS)
    scaled = total * gain[...]
    inner = jnp.mean(x * scaled, axis=-1, keepdims=True)
    out[...] = (scale * (scaled - x * (scale * scale * inner))).astype(BF16)


def home(scale_out, ids, grads, d_rows, w_qk, w_v, tokens, gain):
    rows = d_rows.shape[1]
    width = tokens.shape[1]
    smem = pl.BlockSpec(memory_space=pltpu.SMEM)
    vmem = pl.BlockSpec(memory_space=pltpu.VMEM)
    return pl.pallas_call(
        partial(home_kernel, scale_out),
        out_shape=[
            jax.ShapeDtypeStruct(tokens.shape, BF16),
            jax.ShapeDtypeStruct((rows, width), F32),
            jax.ShapeDtypeStruct((rows, width), F32),
            jax.ShapeDtypeStruct((rows, 1), F32),
        ],
        in_specs=[smem] + [vmem] * 6,
        out_specs=[vmem] * 4,
        compiler_params=pltpu.CompilerParams(vmem_limit_bytes=SMALL_VMEM_BYTES),
        name="home",
    )(ids, grads, d_rows, w_qk, w_v, tokens, gain)


def tables(devices, per, rounds, ring, block_total):
    chips = len(ring)
    place = [ring.index(c) for c in range(chips)]
    steps = [0]
    for s in range(1, chips // 2):
        steps += [-s, s]
    steps.append(chips // 2)
    out = np.zeros((devices, 2, max(chips, per + 3)), np.int32)
    for me in range(devices):
        chip, lane = me // per, me % per
        out[me, SHARDS, :chips] = [ring[(place[chip] + s) % chips] for s in steps]
        out[me, LANES, :per] = [(lane - m) % per for m in range(per)]
        out[me, LANES, per] = lane % rounds
        out[me, LANES, per + 1] = lane // rounds * (block_total * rounds // per)
        out[me, LANES, -1] = me
    return out


def per_device(tokens, norm_gain, w_qk, w_v, cotangent, log_sums, bucket_order, token_position):
    devices = lax.axis_size("tok")
    me = lax.axis_index("tok")
    size, width = tokens.shape
    rounds, heads, _ = log_sums.shape
    head_dim = width // heads
    total = bucket_order.shape[1]
    per = devices // heads
    parts = per // rounds
    chips = heads
    chip, lane = me // per, me % per
    groups = [[c * per + j for c in range(chips)] for j in range(per)]
    ring = list(range(0, chips, 2)) + list(range(chips - 1, 0, -2))

    def hop(x, distance):
        route = [
            (ring[p] * per + j, ring[(p + distance) % chips] * per + j)
            for p in range(chips)
            for j in range(per)
        ]
        return lax.ppermute(x, "tok", route)

    def swap(x, shift):
        route = [
            (c * per + j, c * per + (j + shift) % per) for c in range(chips) for j in range(per)
        ]
        return lax.ppermute(x, "tok", route)

    def exchange(x):
        return lax.all_to_all(x, "tok", 0, 0, tiled=True, axis_index_groups=groups)

    ids = lax.dynamic_index_in_dim(
        jnp.asarray(tables(devices, per, rounds, ring, total // BLOCK)), me, 0, keepdims=False
    )
    my_order = lax.dynamic_index_in_dim(bucket_order, lane % rounds, 0, keepdims=False)
    gain_row = norm_gain[None, :]
    normal, chunks = prepare(tokens, gain_row, cotangent, log_sums)

    shards = [normal]
    ahead = behind = normal
    half = chips // 2
    for s in range(1, half):
        ahead, behind = hop(ahead, 1), hop(behind, -1)
        shards += [ahead, behind]
    shards.append(
        jnp.concatenate([hop(ahead[: size // 2], 1), hop(behind[size // 2 :], -1)], axis=0)
    )
    cot = exchange(chunks)

    def my_columns(w):
        return lax.dynamic_slice_in_dim(w, chip * head_dim, head_dim, 1)

    my_weights = jnp.concatenate([my_columns(w_qk), my_columns(w_v)], axis=1)

    def project(some):
        return jnp.stack(
            [jnp.dot(n, my_weights, preferred_element_type=F32).astype(BF16) for n in some]
        )

    early = chips - 3
    qv = [project(shards[:early]), project(shards[early:])]
    qv_all = [qv] + [[swap(x, shift) for x in qv] for shift in range(1, per)]
    cot_all = [cot] + [swap(cot, shift) for shift in range(1, per)]
    sent = attention(per, parts, rounds, ids, my_order, qv_all, cot_all)
    grads = sent[0].astype(F32)
    for shift in range(1, per):
        grads = grads + swap(sent[shift], per - shift).astype(F32)
    grads = grads.astype(BF16)

    inbound = exchange(grads)
    rows = width // devices
    partials = weight_grad(per, rows, ids, grads, shards)
    mine = partials[0].astype(F32)
    for shift in range(1, per):
        mine = mine + swap(partials[shift], per - shift).astype(F32)
    d_rows = exchange(mine.astype(BF16))
    d_tokens, d_wqk, d_wv, gains = home(
        1.0 / math.sqrt(total), ids, inbound, d_rows, w_qk, w_v, tokens, gain_row
    )
    d_gain = gains[:, 0] / lax.dynamic_slice_in_dim(norm_gain, me * rows, rows, 0)
    return d_tokens, d_gain, d_wqk, d_wv


def solution(mesh):
    in_specs = (
        P(("groups", "tok"), None),
        P(),
        P(),
        P(),
        P(("groups", "tok"), None),
        P(None, None, ("groups", "tok")),
        P(None, "groups"),
        P(None, ("groups", "tok")),
    )
    out_specs = (
        P(("groups", "tok"), None),
        P(("groups", "tok")),
        P(("groups", "tok"), None),
        P(("groups", "tok"), None),
    )
    return jax.shard_map(
        per_device, mesh=mesh, in_specs=in_specs, out_specs=out_specs, check_vma=False
    )
```

time: 200 us -> 163 us (0.81)
  blocking collectives: 38.7 us -> 13.9 us
  waiting for transfers between devices: 31.4 us -> 55.9 us
  local copies, waits for them, and re-layouts: 34.9 us -> 11.5 us
  other arithmetic: 14.2 us -> 3.27 us
  between operations: 5.36 us -> 0.81 us
  matrix products: 15.3 us -> 11.1 us
  starting transfers between devices: 20.3 us -> 24.1 us
  Pallas kernels: 39 us -> 41.2 us
    all_gather x1 -> x0, blocking collectives: 26.6 us -> none  [per_device(): sums_all = lax.all_gather(log_sums, 'tok', axis=2, tiled=True)]
    ppermute x8, waiting for transfers between devices: 10.5 us -> 25.3 us  [hop(): return lax.ppermute(x, 'tok', route)]
    unnamed x39 -> x41, local copies, waits for them, and re-layouts: 20.4 us -> 7.83 us
    reshape x4 -> x0, local copies, waits for them, and re-layouts: 8.58 us -> none  [the longest x1 3.94 us: per_device(): w_v.reshape(width, heads, head_dim).transpose(1, 0, 2)]
    all_to_all x2, waiting for transfers between devices: 18.7 us -> 25.9 us  [exchange(): return lax.all_to_all(x, 'tok', 0, 0, tiled=True, axis_index_groups=groups)]
    concatenate x2 -> x0, other arithmetic: 5 us -> none  [per_device(): jnp.concatenate([w_qk.reshape(width, heads, head_dim).transpose(1, 0, 2),...]
    dot_general x9 -> x8, matrix products: 15.3 us -> 11.1 us  [project(): jnp.dot(n, my_weights, preferred_element_type=F32).astype(BF16)]
    ppermute x8, starting transfers between devices: 9.34 us -> 12.8 us  [hop(): return lax.ppermute(x, 'tok', route)]
  transfers between devices with their start and end apart: 14 -> 15, of which waited for: 6 -> 9; matrix products, arithmetic and copies ran while one was open for 25% -> 9% of each run, Pallas kernels for 0% -> 0%
where the time goes in v1:
time: 163 us; the launch traced here: 162 us
  waiting for transfers between devices  55.9 us (34%)
  Pallas kernels  41.2 us (25%)
  starting transfers between devices  24.1 us (15%)
  blocking collectives  13.9 us (9%)
  local copies, waits for them, and re-layouts  11.5 us (7%)
  matrix products  11.1 us (7%)
  other arithmetic  3.27 us (2%)
    pallas_call x1, Pallas kernels, attention(): pl.pallas_call(partial(attention_kernel, per, parts, blocks, rounds, len(...  34.1 us
    all_to_all x2, waiting for transfers between devices, exchange(): return lax.all_to_all(x, 'tok', 0, 0, tiled=True, axis_index_groups=groups)  25.9 us
    ppermute x8, waiting for transfers between devices, hop(): return lax.ppermute(x, 'tok', route)  25.3 us
    all_to_all x1, blocking collectives, exchange(): return lax.all_to_all(x, 'tok', 0, 0, tiled=True, axis_index_groups=groups)  13.9 us
    ppermute x8, starting transfers between devices, hop(): return lax.ppermute(x, 'tok', route)  12.8 us
    dot_general x8, matrix products, project(): jnp.dot(n, my_weights, preferred_element_type=F32).astype(BF16)  11.1 us
    all_to_all x2, starting transfers between devices, exchange(): return lax.all_to_all(x, 'tok', 0, 0, tiled=True, axis_index_groups=groups)  9.87 us
    unnamed x41, local copies, waits for them, and re-layouts  7.83 us
  transfers between devices with their start and end apart: 15, of which 9 were waited for; matrix products, arithmetic and copies ran while one was open for 9% of the time, Pallas kernels for 0%

profile of v1, /device:TPU:0, one launch (start us, length us, event | category | flops | bytes accessed | tf_op | source)
XLA Modules:
  0.0 161.7 jit_solution(5442486806991057424)
XLA Ops:
  0.7 1.2 copy-done.3
  1.9 1.0 copy-done.5
  4.3 1.1 prepare.1
  5.4 3.0 %collective-permute-start.1 = (bf16[256,1024]{1,0:T(8,128)(2,1)S(1)}, bf16[256,1024]{1,0:T(8,128)(2,1)S(1)}, u32[]{:S(2)}, u32[]{:S(2)}) collective-permute-start(bf16[256,1024]{1,0:T(8,128)(2,1)S(1)} %get-tuple-element.14.refs_0_), channel_id=1, source_target_pairs={{0,2},{1,3},{4,0},{5,1},{8,4},{9,5},{12,8},{13,9},{14,12},{15,13},... | collective-permute-start | bytes 1572872 | tf_op jit(solution)/shard_map/ppermute | solution.py:361
  8.4 6.3 %all-to-all-start = ((bf16[8,272,128]{2,1,0:T(8,128)(2,1)}), bf16[8,272,128]{2,1,0:T(8,128)(2,1)}, u32[]{:S(2)}, u32[]{:S(2)}) async-start(bf16[8,272,128]{2,1,0:T(8,128)(2,1)} %get-tuple-element.15), calls=%async_computation | async-start | bytes 1114112 | tf_op jit(solution)/shard_map/all_to_all | solution.py:370
  14.7 1.7 %constant_dynamic-slice_fusion = (bf16[1024,128]{1,0:T(8,128)(2,1)S(1)}, bf16[1024,128]{1,0:T(8,128)(2,1)}) fusion(bf16[1024,1024]{1,0:T(8,128)(2,1)S(1)} %copy-done.1, s32[]{:T(128)S(6)} %select_n.35, bf16[1024,1024]{1,0:T(8,128)(2,1)} %w_qk.1), kind=kLoop, calls=%fused_computation.28 | loop fusion | bytes 1048580 | tf_op jit(solution)/shard_map/dynamic_slice | solution.py:391
  16.4 5.5 %collective-permute-done.1.refs_2_ = bf16[256,1024]{1,0:T(8,128)(2,1)S(1)} collective-permute-done((bf16[256,1024]{1,0:T(8,128)(2,1)S(1)}, bf16[256,1024]{1,0:T(8,128)(2,1)S(1)}, u32[]{:S(2)}, u32[]{:S(2)}) %collective-permute-start.1) | collective-permute-done | bytes 524320 | tf_op jit(solution)/shard_map/ppermute | solution.py:361
  21.9 2.8 %collective-permute-start.3 = (bf16[256,1024]{1,0:T(8,128)(2,1)S(1)}, bf16[256,1024]{1,0:T(8,128)(2,1)}, u32[]{:S(2)}, u32[]{:S(2)}) collective-permute-start(bf16[256,1024]{1,0:T(8,128)(2,1)S(1)} %collective-permute-done.1.refs_2_), channel_id=1, source_target_pairs={{0,2},{1,3},{4,0},{5,1},{8,4},{9,5},{12,8},{13,9},{14,12},{15,13},... | collective-permute-start | bytes 1572872 | tf_op jit(solution)/shard_map/ppermute | solution.py:361
  24.9 1.2 dynamic-slice_bitcast_fusion.ids
  26.1 2.0 %fusion.1 = bf16[5,256,256]{2,1,0:T(8,128)(2,1)} fusion(bf16[256,1024]{1,0:T(8,128)(2,1)S(1)} %get-tuple-element.14.refs_0_, bf16[1024,128]{1,0:T(8,128)(2,1)S(1)} %get-tuple-element.24, bf16[1024,128]{1,0:T(8,128)(2,1)} %get-tuple-element.25), kind=kOutput, calls=%fused_computation.10 | convolution fusion | flops 135331840 | bytes 1179648 | tf_op jit(solution)/shard_map/dot_general | solution.py:397
  28.1 2.1 %fusion.3 = bf16[5,256,256]{2,1,0:T(8,128)(2,1)} fusion(bf16[5,256,256]{2,1,0:T(8,128)(2,1)} %fusion.1, bf16[256,1024]{1,0:T(8,128)(2,1)} %collective-permute-done.refs_1_, bf16[1024,128]{1,0:T(8,128)(2,1)S(1)} %get-tuple-element.24, bf16[1024,128]{1,0:T(8,128)(2,1)} %get-tuple-element.25), kind=kOutput, calls=%fused_computation.12 | convolution fusion | flops 135331840 | bytes 1179648 | tf_op jit(solution)/shard_map/dot_general | solution.py:397
  30.2 10.4 %collective-permute-done.3.refs_4_ = bf16[256,1024]{1,0:T(8,128)(2,1)} collective-permute-done((bf16[256,1024]{1,0:T(8,128)(2,1)S(1)}, bf16[256,1024]{1,0:T(8,128)(2,1)}, u32[]{:S(2)}, u32[]{:S(2)}) %collective-permute-start.3) | collective-permute-done | bytes 524320 | tf_op jit(solution)/shard_map/ppermute | solution.py:361
  41.3 4.1 %collective-permute-start.4 = (bf16[256,1024]{1,0:T(8,128)(2,1)}, bf16[256,1024]{1,0:T(8,128)(2,1)S(1)}, u32[]{:S(2)}, u32[]{:S(2)}) collective-permute-start(bf16[256,1024]{1,0:T(8,128)(2,1)} %collective-permute-done.2.refs_3_), channel_id=1, source_target_pairs={{0,4},{1,5},{4,8},{5,9},{8,12},{9,13},{12,14},{13,15},{14,10},{15,... | collective-permute-start | bytes 1572872 | tf_op jit(solution)/shard_map/ppermute | solution.py:361
  45.4 2.0 %fusion.5 = bf16[5,256,256]{2,1,0:T(8,128)(2,1)} fusion(bf16[5,256,256]{2,1,0:T(8,128)(2,1)} %fusion.3, bf16[256,1024]{1,0:T(8,128)(2,1)} %copy-done.8, bf16[1024,128]{1,0:T(8,128)(2,1)S(1)} %get-tuple-element.24, bf16[1024,128]{1,0:T(8,128)(2,1)S(1)} %copy-done.18), kind=kOutput, calls=%fused_computation.14 | convolution fusion | flops 135331840 | bytes 1179648 | tf_op jit(solution)/shard_map/dot_general | solution.py:397
  47.4 2.1 %fusion.7 = bf16[5,256,256]{2,1,0:T(8,128)(2,1)} fusion(bf16[5,256,256]{2,1,0:T(8,128)(2,1)} %fusion.5, bf16[256,1024]{1,0:T(8,128)(2,1)} %collective-permute-done.2.refs_3_, bf16[1024,128]{1,0:T(8,128)(2,1)S(1)} %get-tuple-element.24, bf16[1024,128]{1,0:T(8,128)(2,1)} %get-tuple-element.25), kind=kOutput, calls=%fused_computation.16 | convolution fusion | flops 135331840 | bytes 1179648 | tf_op jit(solution)/shard_map/dot_general | solution.py:397
  49.5 2.0 %fusion.9.refs_0_ = bf16[5,256,256]{2,1,0:T(8,128)(2,1)} fusion(bf16[5,256,256]{2,1,0:T(8,128)(2,1)} %fusion.7, bf16[256,1024]{1,0:T(8,128)(2,1)} %collective-permute-done.3.refs_4_, bf16[1024,128]{1,0:T(8,128)(2,1)S(1)} %get-tuple-element.24, bf16[1024,128]{1,0:T(8,128)(2,1)} %get-tuple-element.25), kind=kOutput, calls=%fused_computation.18 | convolution fusion | flops 135331840 | bytes 1179648 | tf_op jit(solution)/shard_map/dot_general | solution.py:397
  52.0 4.6 %collective-permute-done.5.refs_6_ = bf16[256,1024]{1,0:T(8,128)(2,1)S(1)} collective-permute-done((bf16[256,1024]{1,0:T(8,128)(2,1)}, bf16[256,1024]{1,0:T(8,128)(2,1)S(1)}, u32[]{:S(2)}, u32[]{:S(2)}) %collective-permute-start.5) | collective-permute-done | bytes 524320 | tf_op jit(solution)/shard_map/ppermute | solution.py:361
  56.9 1.9 %collective-permute-start.6 = (bf16[128,1024]{1,0:T(8,128)(2,1)S(1)}, bf16[128,1024]{1,0:T(8,128)(2,1)S(1)}, u32[]{:S(2)}, u32[]{:S(2)}) collective-permute-start(bf16[128,1024]{1,0:T(8,128)(2,1)S(1)} %slice.8), channel_id=1, source_target_pairs={{0,4},{1,5},{4,8},{5,9},{8,12},{9,13},{12,14},{13,15},{14,10},{15,... | collective-permute-start | bytes 786440 | tf_op jit(solution)/shard_map/ppermute | solution.py:361
  59.4 4.6 %collective-permute-done.6 = bf16[128,1024]{1,0:T(8,128)(2,1)S(1)} collective-permute-done((bf16[128,1024]{1,0:T(8,128)(2,1)S(1)}, bf16[128,1024]{1,0:T(8,128)(2,1)S(1)}, u32[]{:S(2)}, u32[]{:S(2)}) %collective-permute-start.6) | collective-permute-done | bytes 262176 | tf_op jit(solution)/shard_map/ppermute | solution.py:361
  65.8 1.1 collective-permute-done.9.refs_3_
  66.9 0.8 copy-done.17
  67.7 34.1 %attention.1 = (bf16[8,256,256]{2,1,0:T(8,128)(2,1)}, bf16[8,256,256]{2,1,0:T(8,128)(2,1)}) custom-call(s32[2,8]{1,0:T(2,128)} %dynamic-slice_bitcast_fusion.ids, s32[4096]{0:T(1024)} %bitcast.40, bf16[5,256,256]{2,1,0:T(8,128)(2,1)} %fusion.9.refs_0_, bf16[3,256,256]{2,1,0:T(8,128)(2,1)} %copy-done.14, bf16[5,256,256]{2,1,0:T(8,128)(2,1)} %copy-done.15, ...), custom_call_target="tpu_custom_call" | custom-call | tf_op jit(solution)/shard_map/attention/pallas_call | solution.py:187
  102.3 2.5 %collective-permute-done.11 = bf16[8,256,256]{2,1,0:T(8,128)(2,1)S(1)} collective-permute-done((bf16[8,256,256]{2,1,0:T(8,128)(2,1)}, bf16[8,256,256]{2,1,0:T(8,128)(2,1)S(1)}, u32[]{:S(2)}, u32[]{:S(2)}) %collective-permute-start.11) | collective-permute-done | bytes 1048608 | tf_op jit(solution)/shard_map/ppermute | solution.py:367
  104.8 2.4 %add_convert_fusion.grads = bf16[8,256,256]{2,1,0:T(8,128)(2,1)} fusion(bf16[8,256,256]{2,1,0:T(8,128)(2,1)S(1)} %collective-permute-done.11, bf16[8,256,256]{2,1,0:T(8,128)(2,1)} %get-tuple-element.16), kind=kLoop, calls=%fused_computation | loop fusion | flops 2097152 | bytes 3145728 | tf_op jit(solution)/shard_map/convert_element_type | solution.py:408
  107.2 3.2 %weight_grad.1 = (bf16[8,64,256]{2,1,0:T(8,128)(2,1)S(1)}, bf16[8,64,256]{2,1,0:T(8,128)(2,1)S(1)}) custom-call(s32[2,8]{1,0:T(2,128)S(1)} %copy-done.13, bf16[8,256,256]{2,1,0:T(8,128)(2,1)} %add_convert_fusion.grads, bf16[256,1024]{1,0:T(8,128)(2,1)S(1)} %copy-done.7, bf16[256,1024]{1,0:T(8,128)(2,1)} %collective-permute-done.refs_1_, ...), custom_call_target="tpu_custom_call" | custom-call | tf_op jit(solution)/shard_map/weight_grad/pallas_call | solution.py:267
  110.9 1.2 collective-permute-done.12
  112.1 13.9 %all_to_all.15.d_rows = bf16[8,64,256]{2,1,0:T(8,128)(2,1)S(1)} all-to-all(bf16[8,64,256]{2,1,0:T(8,128)(2,1)S(1)} %add_convert_fusion.1), channel_id=1, replica_groups={{0,2,4,6,8,10,12,14},{1,3,5,7,9,11,13,15},{16,18,20,22,24,26,28,30},{17..., dimensions={0} | all-to-all | bytes 524288 | tf_op jit(solution)/shard_map/all_to_all | solution.py:370
  126.1 3.6 %all-to-all-start.1 = ((bf16[8,256,256]{2,1,0:T(8,128)(2,1)}), bf16[8,256,256]{2,1,0:T(8,128)(2,1)S(1)}, u32[]{:S(2)}, u32[]{:S(2)}) async-start(bf16[8,256,256]{2,1,0:T(8,128)(2,1)} %add_convert_fusion.grads), calls=%async_computation.1 | async-start | bytes 2097152 | tf_op jit(solution)/shard_map/all_to_all | solution.py:370
  129.7 25.9 %all-to-all-done.1.grads = bf16[8,256,256]{2,1,0:T(8,128)(2,1)S(1)} async-done(((bf16[8,256,256]{2,1,0:T(8,128)(2,1)}), bf16[8,256,256]{2,1,0:T(8,128)(2,1)S(1)}, u32[]{:S(2)}, u32[]{:S(2)}) %all-to-all-start.1) | async-done | bytes 1048608 | tf_op jit(solution)/shard_map/all_to_all | solution.py:370
  155.5 1.6 copy-done.2
  157.1 1.0 copy-done.4
  158.1 2.9 %home.1 = (bf16[256,1024]{1,0:T(8,128)(2,1)}, f32[64,1024]{1,0:T(8,128)}, f32[64,1024]{1,0:T(8,128)}, f32[64,1]{1,0:T(8,128)S(1)}) custom-call(s32[2,8]{1,0:T(2,128)S(1)} %copy-done.13, bf16[8,256,256]{2,1,0:T(8,128)(2,1)S(1)} %all-to-all-done.1.grads, bf16[8,64,256]{2,1,0:T(8,128)(2,1)S(1)} %all_to_all.15.d_rows, bf16[1024,1024]{1,0:T(8,128)(2,1)S(1)} %copy-done.2, ...), custom_call_target="tpu_custom_call" | custom-call | tf_op jit(solution)/shard_map/home/pallas_call | solution.py:308
  (63 shorter events, 7.2 us)
Async XLA Ops:
  0.6 64.6 %copy-start = (s32[2,4096]{1,0:T(2,128)S(1)}, s32[2,4096]{1,0:T(2,128)}, u32[]{:S(2)}) copy-start(s32[2,4096]{1,0:T(2,128)} %param.15) | copy-start | bytes 98308
  0.6 14.1 %copy-start.1 = (bf16[1024,1024]{1,0:T(8,128)(2,1)S(1)}, bf16[1024,1024]{1,0:T(8,128)(2,1)}, u32[]{:S(2)}) copy-start(bf16[1024,1024]{1,0:T(8,128)(2,1)} %w_v.1) | copy-start | bytes 6291460
  0.7 1.2 copy-start.3
  1.9 1.0 copy-start.5
  5.4 24.8 %copy-start.6 = (bf16[256,1024]{1,0:T(8,128)(2,1)}, bf16[256,1024]{1,0:T(8,128)(2,1)S(1)}, u32[]{:S(2)}) copy-start(bf16[256,1024]{1,0:T(8,128)(2,1)S(1)} %get-tuple-element.14.refs_0_) | copy-start | bytes 1572868
  5.4 16.5 %collective-permute-start.1 = (bf16[256,1024]{1,0:T(8,128)(2,1)S(1)}, bf16[256,1024]{1,0:T(8,128)(2,1)S(1)}, u32[]{:S(2)}, u32[]{:S(2)}) collective-permute-start(bf16[256,1024]{1,0:T(8,128)(2,1)S(1)} %get-tuple-element.14.refs_0_), channel_id=1, source_target_pairs={{0,2},{1,3},{4,0},{5,1},{8,4},{9,5},{12,8},{13,9},{14,12},{15,13},... | collective-permute-start | bytes 1572872 | tf_op jit(solution)/shard_map/ppermute | solution.py:361
  8.4 16.4 %collective-permute-start = (bf16[256,1024]{1,0:T(8,128)(2,1)S(1)}, bf16[256,1024]{1,0:T(8,128)(2,1)}, u32[]{:S(2)}, u32[]{:S(2)}) collective-permute-start(bf16[256,1024]{1,0:T(8,128)(2,1)S(1)} %get-tuple-element.14.refs_0_), channel_id=1, source_target_pairs={{0,4},{1,5},{4,8},{5,9},{8,12},{9,13},{12,14},{13,15},{14,10},{15,... | collective-permute-start | bytes 1572872 | tf_op jit(solution)/shard_map/ppermute | solution.py:361
  8.4 39.0 %all-to-all-start = ((bf16[8,272,128]{2,1,0:T(8,128)(2,1)}), bf16[8,272,128]{2,1,0:T(8,128)(2,1)}, u32[]{:S(2)}, u32[]{:S(2)}) async-start(bf16[8,272,128]{2,1,0:T(8,128)(2,1)} %get-tuple-element.15), calls=%async_computation | async-start | bytes 1114112 | tf_op jit(solution)/shard_map/all_to_all | solution.py:370
  21.9 19.4 %copy-start.8 = (bf16[256,1024]{1,0:T(8,128)(2,1)}, bf16[256,1024]{1,0:T(8,128)(2,1)S(1)}, u32[]{:S(2)}) copy-start(bf16[256,1024]{1,0:T(8,128)(2,1)S(1)} %collective-permute-done.1.refs_2_) | copy-start | bytes 1572868
  21.9 18.7 %collective-permute-start.3 = (bf16[256,1024]{1,0:T(8,128)(2,1)S(1)}, bf16[256,1024]{1,0:T(8,128)(2,1)}, u32[]{:S(2)}, u32[]{:S(2)}) collective-permute-start(bf16[256,1024]{1,0:T(8,128)(2,1)S(1)} %collective-permute-done.1.refs_2_), channel_id=1, source_target_pairs={{0,2},{1,3},{4,0},{5,1},{8,4},{9,5},{12,8},{13,9},{14,12},{15,13},... | collective-permute-start | bytes 1572872 | tf_op jit(solution)/shard_map/ppermute | solution.py:361
  24.8 16.6 %collective-permute-start.2 = (bf16[256,1024]{1,0:T(8,128)(2,1)}, bf16[256,1024]{1,0:T(8,128)(2,1)}, u32[]{:S(2)}, u32[]{:S(2)}) collective-permute-start(bf16[256,1024]{1,0:T(8,128)(2,1)} %collective-permute-done.refs_1_), channel_id=1, source_target_pairs={{0,4},{1,5},{4,8},{5,9},{8,12},{9,13},{12,14},{13,15},{14,10},{15,... | collective-permute-start | bytes 1572872 | tf_op jit(solution)/shard_map/ppermute | solution.py:361
  26.1 19.3 %copy-start.18 = (bf16[1024,128]{1,0:T(8,128)(2,1)S(1)}, bf16[1024,128]{1,0:T(8,128)(2,1)}, u32[]{:S(2)}) copy-start(bf16[1024,128]{1,0:T(8,128)(2,1)} %get-tuple-element.25) | copy-start | bytes 786436
  40.6 16.0 %collective-permute-start.5 = (bf16[256,1024]{1,0:T(8,128)(2,1)}, bf16[256,1024]{1,0:T(8,128)(2,1)S(1)}, u32[]{:S(2)}, u32[]{:S(2)}) collective-permute-start(bf16[256,1024]{1,0:T(8,128)(2,1)} %collective-permute-done.3.refs_4_), channel_id=1, source_target_pairs={{0,2},{1,3},{4,0},{5,1},{8,4},{9,5},{12,8},{13,9},{14,12},{15,13},... | collective-permute-start | bytes 1572872 | tf_op jit(solution)/shard_map/ppermute | solution.py:361
  41.3 15.5 %collective-permute-start.4 = (bf16[256,1024]{1,0:T(8,128)(2,1)}, bf16[256,1024]{1,0:T(8,128)(2,1)S(1)}, u32[]{:S(2)}, u32[]{:S(2)}) collective-permute-start(bf16[256,1024]{1,0:T(8,128)(2,1)} %collective-permute-done.2.refs_3_), channel_id=1, source_target_pairs={{0,4},{1,5},{4,8},{5,9},{8,12},{9,13},{12,14},{13,15},{14,10},{15,... | collective-permute-start | bytes 1572872 | tf_op jit(solution)/shard_map/ppermute | solution.py:361
  47.4 11.4 %copy-start.19 = (bf16[1024,128]{1,0:T(8,128)(2,1)S(1)}, bf16[1024,128]{1,0:T(8,128)(2,1)}, u32[]{:S(2)}) copy-start(bf16[1024,128]{1,0:T(8,128)(2,1)} %get-tuple-element.25) | copy-start | bytes 786436
  47.4 18.4 %collective-permute-start.10 = (bf16[8,272,128]{2,1,0:T(8,128)(2,1)}, bf16[8,272,128]{2,1,0:T(8,128)(2,1)S(1)}, u32[]{:S(2)}, u32[]{:S(2)}) collective-permute-start(bf16[8,272,128]{2,1,0:T(8,128)(2,1)} %all-to-all-done.refs_4_), channel_id=1, source_target_pairs={{0,1},{1,0},{2,3},{3,2},{4,5},{5,4},{6,7},{7,6},{8,9},{9,8},{10,11... | collective-permute-start | bytes 1671176 | tf_op jit(solution)/shard_map/ppermute | solution.py:367
  51.6 14.3 %collective-permute-start.8 = (bf16[5,256,256]{2,1,0:T(8,128)(2,1)}, bf16[5,256,256]{2,1,0:T(8,128)(2,1)S(1)}, u32[]{:S(2)}, u32[]{:S(2)}) collective-permute-start(bf16[5,256,256]{2,1,0:T(8,128)(2,1)} %fusion.9.refs_0_), channel_id=1, source_target_pairs={{0,1},{1,0},{2,3},{3,2},{4,5},{5,4},{6,7},{7,6},{8,9},{9,8},{10,11... | collective-permute-start | bytes 1966088 | tf_op jit(solution)/shard_map/ppermute | solution.py:367
  56.6 7.4 %collective-permute-start.7 = (bf16[128,1024]{1,0:T(8,128)(2,1)S(1)}, bf16[128,1024]{1,0:T(8,128)(2,1)S(1)}, u32[]{:S(2)}, u32[]{:S(2)}) collective-permute-start(bf16[128,1024]{1,0:T(8,128)(2,1)S(1)} %slice.9), channel_id=1, source_target_pairs={{0,2},{1,3},{4,0},{5,1},{8,4},{9,5},{12,8},{13,9},{14,12},{15,13},... | collective-permute-start | bytes 786440 | tf_op jit(solution)/shard_map/ppermute | solution.py:361
  56.9 7.2 %collective-permute-start.6 = (bf16[128,1024]{1,0:T(8,128)(2,1)S(1)}, bf16[128,1024]{1,0:T(8,128)(2,1)S(1)}, u32[]{:S(2)}, u32[]{:S(2)}) collective-permute-start(bf16[128,1024]{1,0:T(8,128)(2,1)S(1)} %slice.8), channel_id=1, source_target_pairs={{0,4},{1,5},{4,8},{5,9},{8,12},{9,13},{12,14},{13,15},{14,10},{15,... | collective-permute-start | bytes 786440 | tf_op jit(solution)/shard_map/ppermute | solution.py:361
  65.2 1.7 %collective-permute-start.9 = (bf16[3,256,256]{2,1,0:T(8,128)(2,1)S(1)}, bf16[3,256,256]{2,1,0:T(8,128)(2,1)S(1)}, u32[]{:S(2)}, u32[]{:S(2)}) collective-permute-start(bf16[3,256,256]{2,1,0:T(8,128)(2,1)S(1)} %pad_maximum_fusion.1.refs_1_), channel_id=1, source_target_pairs={{0,1},{1,0},{2,3},{3,2},{4,5},{5,4},{6,7},{7,6},{8,9},{9,8},{10,11... | collective-permute-start | bytes 1179656 | tf_op jit(solution)/shard_map/ppermute | solution.py:367
  65.8 1.1 copy-start.16
  65.8 1.1 copy-start.15
  66.9 0.8 copy-start.17
  101.8 5.5 %copy-start.7 = (bf16[256,1024]{1,0:T(8,128)(2,1)S(1)}, bf16[256,1024]{1,0:T(8,128)(2,1)}, u32[]{:S(2)}) copy-start(bf16[256,1024]{1,0:T(8,128)(2,1)} %copy-done.6) | copy-start | bytes 1572868
  101.8 5.5 %copy-start.9 = (bf16[256,1024]{1,0:T(8,128)(2,1)S(1)}, bf16[256,1024]{1,0:T(8,128)(2,1)}, u32[]{:S(2)}) copy-start(bf16[256,1024]{1,0:T(8,128)(2,1)} %copy-done.8) | copy-start | bytes 1572868
  101.8 5.5 %copy-start.13 = (s32[2,8]{1,0:T(2,128)S(1)}, s32[2,8]{1,0:T(2,128)}, u32[]{:S(2)}) copy-start(s32[2,8]{1,0:T(2,128)} %dynamic-slice_bitcast_fusion.ids) | copy-start | bytes 196
  101.8 3.0 %collective-permute-start.11 = (bf16[8,256,256]{2,1,0:T(8,128)(2,1)}, bf16[8,256,256]{2,1,0:T(8,128)(2,1)S(1)}, u32[]{:S(2)}, u32[]{:S(2)}) collective-permute-start(bf16[8,256,256]{2,1,0:T(8,128)(2,1)} %get-tuple-element.17), channel_id=1, source_target_pairs={{0,1},{1,0},{2,3},{3,2},{4,5},{5,4},{6,7},{7,6},{8,9},{9,8},{10,11... | collective-permute-start | bytes 3145736 | tf_op jit(solution)/shard_map/ppermute | solution.py:367
  110.5 45.0 %copy-start.11 = (f32[1024]{0:T(1024)S(1)}, f32[1024]{0:T(1024)}, u32[]{:S(2)}) copy-start(f32[1024]{0:T(1024)} %param.10) | copy-start | bytes 12292
  110.5 1.6 collective-permute-start.12
  126.1 29.4 %all-to-all-start.1 = ((bf16[8,256,256]{2,1,0:T(8,128)(2,1)}), bf16[8,256,256]{2,1,0:T(8,128)(2,1)S(1)}, u32[]{:S(2)}, u32[]{:S(2)}) async-start(bf16[8,256,256]{2,1,0:T(8,128)(2,1)} %add_convert_fusion.grads), calls=%async_computation.1 | async-start | bytes 2097152 | tf_op jit(solution)/shard_map/all_to_all | solution.py:370
  155.5 1.6 copy-start.2
  157.1 1.0 copy-start.4
  (3 other events, 2.2 us)

commit v2 on v1

--- a/solution.py
+++ b/solution.py
@@ -255,9 +255,10 @@
         n += 1
     total[...] = grad_t.T
     for m in range(per):
-        for c in range(chips):
-            start = pl.multiple_of((c * per + ids[LANES, m]) * rows, rows)
-            outs[m][c] = total[pl.ds(start, rows), :].astype(BF16)
+        for k in range(chips):
+            chip = lax.rem(ids[SHARDS, 0] + k, chips)
+            start = pl.multiple_of((chip * per + ids[LANES, m]) * rows, rows)
+            outs[m][k] = total[pl.ds(start, rows), :].astype(BF16)
 
 
 def weight_grad(per, rows, ids, grads, shards):
@@ -275,8 +276,11 @@
     )(ids, grads, *shards)
 
 
-def home_kernel(scale_out, ids, grads, d_rows, w_qk, w_v, tokens, gain, out, d_wqk, d_wv, d_gain):
-    heads, rows, both = d_rows.shape
+def home_kernel(scale_out, ids, grads, w_qk, w_v, tokens, gain, *refs):
+    heads = grads.shape[0]
+    d_rows = refs[:heads]
+    out, d_wqk, d_wv, d_gain = refs[heads:]
+    rows, both = d_rows[0].shape
     head_dim = both // 2
     total = jnp.zeros(tokens.shape, F32)
     start = pl.multiple_of(ids[LANES, ids.shape[1] - 1] * rows, rows)
@@ -285,8 +289,11 @@
         columns = slice(head * head_dim, (head + 1) * head_dim)
         weights = jnp.concatenate([w_qk[:, columns], w_v[:, columns]], axis=1)
         total = total + dot(grads[head], weights, NT)
-        qk_rows = d_rows[head, :, :head_dim].astype(F32) * scale_out
-        v_rows = d_rows[head, :, head_dim:].astype(F32) * scale_out
+        k = head
+        source = lax.rem(ids[SHARDS, 0] + heads - k, heads)
+        columns = pl.ds(pl.multiple_of(source * head_dim, head_dim), head_dim)
+        qk_rows = d_rows[k][:, :head_dim].astype(F32) * scale_out
+        v_rows = d_rows[k][:, head_dim:].astype(F32) * scale_out
         d_wqk[:, columns] = qk_rows
         d_wv[:, columns] = v_rows
         own = qk_rows * w_qk[pl.ds(start, rows), columns].astype(F32)
@@ -301,7 +308,7 @@
 
 
 def home(scale_out, ids, grads, d_rows, w_qk, w_v, tokens, gain):
-    rows = d_rows.shape[1]
+    rows = d_rows[0].shape[0]
     width = tokens.shape[1]
     smem = pl.BlockSpec(memory_space=pltpu.SMEM)
     vmem = pl.BlockSpec(memory_space=pltpu.VMEM)
@@ -313,11 +320,11 @@
             jax.ShapeDtypeStruct((rows, width), F32),
             jax.ShapeDtypeStruct((rows, 1), F32),
         ],
-        in_specs=[smem] + [vmem] * 6,
+        in_specs=[smem] + [vmem] * (5 + len(d_rows)),
         out_specs=[vmem] * 4,
         compiler_params=pltpu.CompilerParams(vmem_limit_bytes=SMALL_VMEM_BYTES),
         name="home",
-    )(ids, grads, d_rows, w_qk, w_v, tokens, gain)
+    )(ids, grads, w_qk, w_v, tokens, gain, *d_rows)
 
 
 def tables(devices, per, rounds, ring, block_total):
@@ -366,6 +373,12 @@
         ]
         return lax.ppermute(x, "tok", route)
 
+    def send(x, distance):
+        route = [
+            (c * per + j, (c + distance) % chips * per + j) for c in range(chips) for j in range(per)
+        ]
+        return lax.ppermute(x, "tok", route)
+
     def exchange(x):
         return lax.all_to_all(x, "tok", 0, 0, tiled=True, axis_index_groups=groups)
 
@@ -413,7 +426,8 @@
     mine = partials[0].astype(F32)
     for shift in range(1, per):
         mine = mine + swap(partials[shift], per - shift).astype(F32)
-    d_rows = exchange(mine.astype(BF16))
+    mine = mine.astype(BF16)
+    d_rows = [mine[0]] + [send(mine[k], k) for k in range(1, chips)]
     d_tokens, d_wqk, d_wv, gains = home(
         1.0 / math.sqrt(total), ids, inbound, d_rows, w_qk, w_v, tokens, gain_row
     )

time: 163 us -> 153 us (0.939)
  waiting for transfers between devices: 55.9 us -> 32.6 us
  starting transfers between devices: 24.1 us -> 46.1 us
  blocking collectives: 13.9 us -> 0 us
  local copies, waits for them, and re-layouts: 11.5 us -> 17.1 us
    all_to_all x2, waiting for transfers between devices: 25.9 us -> 0.01 us  [exchange(): return lax.all_to_all(x, 'tok', 0, 0, tiled=True, axis_index_groups=groups)]
    ppermute x0 -> x7, starting transfers between devices: none -> 21.2 us  [send(): return lax.ppermute(x, 'tok', route)]
    all_to_all x1 -> x0, blocking collectives: 13.9 us -> none  [exchange(): return lax.all_to_all(x, 'tok', 0, 0, tiled=True, axis_index_groups=groups)]
    unnamed x41 -> x53, local copies, waits for them, and re-layouts: 7.83 us -> 12.8 us
    ppermute x0 -> x7, waiting for transfers between devices: none -> 2.31 us  [send(): return lax.ppermute(x, 'tok', route)]
  transfers between devices with their start and end apart: 15 -> 22, of which waited for: 9 -> 11; matrix products, arithmetic and copies ran while one was open for 9% -> 10% of each run, Pallas kernels for 0% -> 2%
where the time goes in v2:
time: 153 us; the launch traced here: 152 us
  starting transfers between devices  46.1 us (30%)
  Pallas kernels  41.3 us (27%)
  waiting for transfers between devices  32.6 us (21%)
  local copies, waits for them, and re-layouts  17.1 us (11%)
  matrix products  11.1 us (7%)
  other arithmetic  3.33 us (2%)
    pallas_call x1, Pallas kernels, attention(): pl.pallas_call(partial(attention_kernel, per, parts, blocks, rounds, len(...  34 us
    ppermute x8, waiting for transfers between devices, hop(): return lax.ppermute(x, 'tok', route)  25.2 us
    ppermute x7, starting transfers between devices, send(): return lax.ppermute(x, 'tok', route)  21.2 us
    unnamed x53, local copies, waits for them, and re-layouts  12.8 us
    ppermute x8, starting transfers between devices, hop(): return lax.ppermute(x, 'tok', route)  12.8 us
    dot_general x8, matrix products, project(): jnp.dot(n, my_weights, preferred_element_type=F32).astype(BF16)  11.1 us
    all_to_all x2, starting transfers between devices, exchange(): return lax.all_to_all(x, 'tok', 0, 0, tiled=True, axis_index_groups=groups)  11 us
    ppermute x5, waiting for transfers between devices, swap(): return lax.ppermute(x, 'tok', route)  5 us
  transfers between devices with their start and end apart: 22, of which 11 were waited for; matrix products, arithmetic and copies ran while one was open for 10% of the time, Pallas kernels for 2%

profile of v2, /device:TPU:0, one launch (start us, length us, event | category | flops | bytes accessed | tf_op | source)
XLA Modules:
  0.0 152.3 jit_solution(5556228007844864672)
XLA Ops:
  0.7 1.2 copy-done.3
  4.3 1.1 prepare.1
  5.4 3.0 %collective-permute-start.1 = (bf16[256,1024]{1,0:T(8,128)(2,1)S(1)}, bf16[256,1024]{1,0:T(8,128)(2,1)S(1)}, u32[]{:S(2)}, u32[]{:S(2)}) collective-permute-start(bf16[256,1024]{1,0:T(8,128)(2,1)S(1)} %get-tuple-element.14.refs_0_), channel_id=1, source_target_pairs={{0,2},{1,3},{4,0},{5,1},{8,4},{9,5},{12,8},{13,9},{14,12},{15,13},... | collective-permute-start | bytes 1572872 | tf_op jit(solution)/shard_map/ppermute | solution.py:368
  8.4 6.3 %all-to-all-start = ((bf16[8,272,128]{2,1,0:T(8,128)(2,1)}), bf16[8,272,128]{2,1,0:T(8,128)(2,1)}, u32[]{:S(2)}, u32[]{:S(2)}) async-start(bf16[8,272,128]{2,1,0:T(8,128)(2,1)} %get-tuple-element.15), calls=%async_computation | async-start | bytes 1114112 | tf_op jit(solution)/shard_map/all_to_all | solution.py:383
  14.7 1.7 %constant_dynamic-slice_fusion = (bf16[1024,128]{1,0:T(8,128)(2,1)S(1)}, bf16[1024,128]{1,0:T(8,128)(2,1)}) fusion(bf16[1024,1024]{1,0:T(8,128)(2,1)S(1)} %copy-done.1, s32[]{:T(128)S(6)} %select_n.35, bf16[1024,1024]{1,0:T(8,128)(2,1)} %w_qk.1), kind=kLoop, calls=%fused_computation.36 | loop fusion | bytes 1048580 | tf_op jit(solution)/shard_map/dynamic_slice | solution.py:404
  16.4 5.5 %collective-permute-done.1.refs_2_ = bf16[256,1024]{1,0:T(8,128)(2,1)S(1)} collective-permute-done((bf16[256,1024]{1,0:T(8,128)(2,1)S(1)}, bf16[256,1024]{1,0:T(8,128)(2,1)S(1)}, u32[]{:S(2)}, u32[]{:S(2)}) %collective-permute-start.1) | collective-permute-done | bytes 524320 | tf_op jit(solution)/shard_map/ppermute | solution.py:368
  21.9 2.8 %collective-permute-start.3 = (bf16[256,1024]{1,0:T(8,128)(2,1)S(1)}, bf16[256,1024]{1,0:T(8,128)(2,1)}, u32[]{:S(2)}, u32[]{:S(2)}) collective-permute-start(bf16[256,1024]{1,0:T(8,128)(2,1)S(1)} %collective-permute-done.1.refs_2_), channel_id=1, source_target_pairs={{0,2},{1,3},{4,0},{5,1},{8,4},{9,5},{12,8},{13,9},{14,12},{15,13},... | collective-permute-start | bytes 1572872 | tf_op jit(solution)/shard_map/ppermute | solution.py:368
  24.9 1.2 dynamic-slice_bitcast_fusion.ids
  26.1 2.0 %fusion.1 = bf16[5,256,256]{2,1,0:T(8,128)(2,1)} fusion(bf16[256,1024]{1,0:T(8,128)(2,1)S(1)} %get-tuple-element.14.refs_0_, bf16[1024,128]{1,0:T(8,128)(2,1)S(1)} %get-tuple-element.32, bf16[1024,128]{1,0:T(8,128)(2,1)} %get-tuple-element.33), kind=kOutput, calls=%fused_computation.10 | convolution fusion | flops 135331840 | bytes 1179648 | tf_op jit(solution)/shard_map/dot_general | solution.py:410
  28.1 2.1 %fusion.3 = bf16[5,256,256]{2,1,0:T(8,128)(2,1)} fusion(bf16[5,256,256]{2,1,0:T(8,128)(2,1)} %fusion.1, bf16[256,1024]{1,0:T(8,128)(2,1)} %collective-permute-done.refs_1_, bf16[1024,128]{1,0:T(8,128)(2,1)S(1)} %get-tuple-element.32, bf16[1024,128]{1,0:T(8,128)(2,1)} %get-tuple-element.33), kind=kOutput, calls=%fused_computation.12 | convolution fusion | flops 135331840 | bytes 1179648 | tf_op jit(solution)/shard_map/dot_general | solution.py:410
  30.2 10.5 %collective-permute-done.3.refs_4_ = bf16[256,1024]{1,0:T(8,128)(2,1)} collective-permute-done((bf16[256,1024]{1,0:T(8,128)(2,1)S(1)}, bf16[256,1024]{1,0:T(8,128)(2,1)}, u32[]{:S(2)}, u32[]{:S(2)}) %collective-permute-start.3) | collective-permute-done | bytes 524320 | tf_op jit(solution)/shard_map/ppermute | solution.py:368
  41.3 4.1 %collective-permute-start.4 = (bf16[256,1024]{1,0:T(8,128)(2,1)}, bf16[256,1024]{1,0:T(8,128)(2,1)S(1)}, u32[]{:S(2)}, u32[]{:S(2)}) collective-permute-start(bf16[256,1024]{1,0:T(8,128)(2,1)} %collective-permute-done.2.refs_3_), channel_id=1, source_target_pairs={{0,4},{1,5},{4,8},{5,9},{8,12},{9,13},{12,14},{13,15},{14,10},{15,... | collective-permute-start | bytes 1572872 | tf_op jit(solution)/shard_map/ppermute | solution.py:368
  45.4 2.0 %fusion.5 = bf16[5,256,256]{2,1,0:T(8,128)(2,1)} fusion(bf16[5,256,256]{2,1,0:T(8,128)(2,1)} %fusion.3, bf16[256,1024]{1,0:T(8,128)(2,1)} %copy-done.14, bf16[1024,128]{1,0:T(8,128)(2,1)S(1)} %get-tuple-element.32, bf16[1024,128]{1,0:T(8,128)(2,1)S(1)} %copy-done.24), kind=kOutput, calls=%fused_computation.14 | convolution fusion | flops 135331840 | bytes 1179648 | tf_op jit(solution)/shard_map/dot_general | solution.py:410
  47.4 2.1 %fusion.7 = bf16[5,256,256]{2,1,0:T(8,128)(2,1)} fusion(bf16[5,256,256]{2,1,0:T(8,128)(2,1)} %fusion.5, bf16[256,1024]{1,0:T(8,128)(2,1)} %collective-permute-done.2.refs_3_, bf16[1024,128]{1,0:T(8,128)(2,1)S(1)} %get-tuple-element.32, bf16[1024,128]{1,0:T(8,128)(2,1)} %get-tuple-element.33), kind=kOutput, calls=%fused_computation.16 | convolution fusion | flops 135331840 | bytes 1179648 | tf_op jit(solution)/shard_map/dot_general | solution.py:410
  49.5 2.1 %fusion.9.refs_0_ = bf16[5,256,256]{2,1,0:T(8,128)(2,1)} fusion(bf16[5,256,256]{2,1,0:T(8,128)(2,1)} %fusion.7, bf16[256,1024]{1,0:T(8,128)(2,1)} %collective-permute-done.3.refs_4_, bf16[1024,128]{1,0:T(8,128)(2,1)S(1)} %get-tuple-element.32, bf16[1024,128]{1,0:T(8,128)(2,1)} %get-tuple-element.33), kind=kOutput, calls=%fused_computation.18 | convolution fusion | flops 135331840 | bytes 1179648 | tf_op jit(solution)/shard_map/dot_general | solution.py:410
  52.1 4.5 %collective-permute-done.5.refs_6_ = bf16[256,1024]{1,0:T(8,128)(2,1)S(1)} collective-permute-done((bf16[256,1024]{1,0:T(8,128)(2,1)}, bf16[256,1024]{1,0:T(8,128)(2,1)S(1)}, u32[]{:S(2)}, u32[]{:S(2)}) %collective-permute-start.5) | collective-permute-done | bytes 524320 | tf_op jit(solution)/shard_map/ppermute | solution.py:368
  56.9 1.9 %collective-permute-start.6 = (bf16[128,1024]{1,0:T(8,128)(2,1)S(1)}, bf16[128,1024]{1,0:T(8,128)(2,1)S(1)}, u32[]{:S(2)}, u32[]{:S(2)}) collective-permute-start(bf16[128,1024]{1,0:T(8,128)(2,1)S(1)} %slice.40), channel_id=1, source_target_pairs={{0,4},{1,5},{4,8},{5,9},{8,12},{9,13},{12,14},{13,15},{14,10},{15,... | collective-permute-start | bytes 786440 | tf_op jit(solution)/shard_map/ppermute | solution.py:368
  59.4 4.6 %collective-permute-done.6 = bf16[128,1024]{1,0:T(8,128)(2,1)S(1)} collective-permute-done((bf16[128,1024]{1,0:T(8,128)(2,1)S(1)}, bf16[128,1024]{1,0:T(8,128)(2,1)S(1)}, u32[]{:S(2)}, u32[]{:S(2)}) %collective-permute-start.6) | collective-permute-done | bytes 262176 | tf_op jit(solution)/shard_map/ppermute | solution.py:368
  65.8 1.0 collective-permute-done.9.refs_3_
  67.6 34.0 %attention.1 = (bf16[8,256,256]{2,1,0:T(8,128)(2,1)}, bf16[8,256,256]{2,1,0:T(8,128)(2,1)}) custom-call(s32[2,8]{1,0:T(2,128)} %dynamic-slice_bitcast_fusion.ids, s32[4096]{0:T(1024)} %bitcast.56, bf16[5,256,256]{2,1,0:T(8,128)(2,1)} %fusion.9.refs_0_, bf16[3,256,256]{2,1,0:T(8,128)(2,1)} %copy-done.20, bf16[5,256,256]{2,1,0:T(8,128)(2,1)} %copy-done.21, ...), custom_call_target="tpu_custom_call" | custom-call | tf_op jit(solution)/shard_map/attention/pallas_call | solution.py:187
  102.1 2.5 %collective-permute-done.11 = bf16[8,256,256]{2,1,0:T(8,128)(2,1)S(1)} collective-permute-done((bf16[8,256,256]{2,1,0:T(8,128)(2,1)}, bf16[8,256,256]{2,1,0:T(8,128)(2,1)S(1)}, u32[]{:S(2)}, u32[]{:S(2)}) %collective-permute-start.11) | collective-permute-done | bytes 1048608 | tf_op jit(solution)/shard_map/ppermute | solution.py:374
  104.6 2.5 %add_convert_fusion.grads = bf16[8,256,256]{2,1,0:T(8,128)(2,1)} fusion(bf16[8,256,256]{2,1,0:T(8,128)(2,1)S(1)} %collective-permute-done.11, bf16[8,256,256]{2,1,0:T(8,128)(2,1)} %get-tuple-element.16), kind=kLoop, calls=%fused_computation | loop fusion | flops 2097152 | bytes 3145728 | tf_op jit(solution)/shard_map/convert_element_type | solution.py:421
  107.1 4.7 %all-to-all-start.1 = ((bf16[8,256,256]{2,1,0:T(8,128)(2,1)}), bf16[8,256,256]{2,1,0:T(8,128)(2,1)S(1)}, u32[]{:S(2)}, u32[]{:S(2)}) async-start(bf16[8,256,256]{2,1,0:T(8,128)(2,1)} %add_convert_fusion.grads), calls=%async_computation.1 | async-start | bytes 2097152 | tf_op jit(solution)/shard_map/all_to_all | solution.py:383
  117.0 3.2 %weight_grad.1 = (bf16[8,64,256]{2,1,0:T(8,128)(2,1)S(1)}, bf16[8,64,256]{2,1,0:T(8,128)(2,1)S(1)}) custom-call(s32[2,8]{1,0:T(2,128)S(1)} %copy-done.19, bf16[8,256,256]{2,1,0:T(8,128)(2,1)} %add_convert_fusion.grads, bf16[256,1024]{1,0:T(8,128)(2,1)S(1)} %copy-done.13, bf16[256,1024]{1,0:T(8,128)(2,1)} %collective-permute-done.refs_1_, ...), custom_call_target="tpu_custom_call" | custom-call | tf_op jit(solution)/shard_map/weight_grad/pallas_call | solution.py:268
  120.3 1.5 collective-permute-done.12
  122.5 4.7 %collective-permute-start.19 = (bf16[64,256]{1,0:T(8,128)(2,1)S(1)}, bf16[64,256]{1,0:T(8,128)(2,1)S(1)}, u32[]{:S(2)}, u32[]{:S(2)}) collective-permute-start(bf16[64,256]{1,0:T(8,128)(2,1)S(1)} %get-tuple-element.24), channel_id=1, source_target_pairs={{0,14},{1,15},{2,0},{3,1},{4,2},{5,3},{6,4},{7,5},{8,6},{9,7},{10,... | collective-permute-start | bytes 98312 | tf_op jit(solution)/shard_map/ppermute | solution.py:380
  127.8 2.9 %collective-permute-start.16 = (bf16[64,256]{1,0:T(8,128)(2,1)}, bf16[64,256]{1,0:T(8,128)(2,1)S(1)}, u32[]{:S(2)}, u32[]{:S(2)}) collective-permute-start(bf16[64,256]{1,0:T(8,128)(2,1)} %get-tuple-element.27), channel_id=1, source_target_pairs={{0,8},{1,9},{2,10},{3,11},{4,12},{5,13},{6,14},{7,15},{8,0},{9,1},... | collective-permute-start | bytes 98312 | tf_op jit(solution)/shard_map/ppermute | solution.py:380
  131.4 1.3 collective-permute-start.14
  132.7 11.7 %collective-permute-start.13 = (bf16[64,256]{1,0:T(8,128)(2,1)S(1)}, bf16[64,256]{1,0:T(8,128)(2,1)S(1)}, u32[]{:S(2)}, u32[]{:S(2)}) collective-permute-start(bf16[64,256]{1,0:T(8,128)(2,1)S(1)} %get-tuple-element.30), channel_id=1, source_target_pairs={{0,2},{1,3},{2,4},{3,5},{4,6},{5,7},{6,8},{7,9},{8,10},{9,11},{10,... | collective-permute-start | bytes 98312 | tf_op jit(solution)/shard_map/ppermute | solution.py:380
  144.5 1.5 %collective-permute-done.13.refs_1_ = bf16[64,256]{1,0:T(8,128)(2,1)S(1)} collective-permute-done((bf16[64,256]{1,0:T(8,128)(2,1)S(1)}, bf16[64,256]{1,0:T(8,128)(2,1)S(1)}, u32[]{:S(2)}, u32[]{:S(2)}) %collective-permute-start.13) | collective-permute-done | bytes 32800 | tf_op jit(solution)/shard_map/ppermute | solution.py:380
  146.1 1.6 %copy-done.2 = bf16[1024,1024]{1,0:T(8,128)(2,1)S(1)} copy-done((bf16[1024,1024]{1,0:T(8,128)(2,1)S(1)}, bf16[1024,1024]{1,0:T(8,128)(2,1)}, u32[]{:S(2)}) %copy-start.2) | copy-done | bytes 2097176
  148.7 2.9 %home.1 = (bf16[256,1024]{1,0:T(8,128)(2,1)}, f32[64,1024]{1,0:T(8,128)}, f32[64,1024]{1,0:T(8,128)}, f32[64,1]{1,0:T(8,128)S(1)}) custom-call(s32[2,8]{1,0:T(2,128)S(1)} %copy-done.19, bf16[8,256,256]{2,1,0:T(8,128)(2,1)S(1)} %all-to-all-done.1.grads, bf16[1024,1024]{1,0:T(8,128)(2,1)S(1)} %copy-done.2, bf16[1024,1024]{1,0:T(8,128)(2,1)S(1)} %copy-done.1, ...), custom_call_target="tpu_custom_call" | custom-call | tf_op jit(solution)/shard_map/home/pallas_call | solution.py:315
  (89 shorter events, 16.7 us)
Async XLA Ops:
  0.6 64.5 %copy-start = (s32[2,4096]{1,0:T(2,128)S(1)}, s32[2,4096]{1,0:T(2,128)}, u32[]{:S(2)}) copy-start(s32[2,4096]{1,0:T(2,128)} %param.15) | copy-start | bytes 98308
  0.6 14.1 %copy-start.1 = (bf16[1024,1024]{1,0:T(8,128)(2,1)S(1)}, bf16[1024,1024]{1,0:T(8,128)(2,1)}, u32[]{:S(2)}) copy-start(bf16[1024,1024]{1,0:T(8,128)(2,1)} %w_v.1) | copy-start | bytes 6291460
  5.4 24.8 %copy-start.12 = (bf16[256,1024]{1,0:T(8,128)(2,1)}, bf16[256,1024]{1,0:T(8,128)(2,1)S(1)}, u32[]{:S(2)}) copy-start(bf16[256,1024]{1,0:T(8,128)(2,1)S(1)} %get-tuple-element.14.refs_0_) | copy-start | bytes 1572868
  5.4 16.5 %collective-permute-start.1 = (bf16[256,1024]{1,0:T(8,128)(2,1)S(1)}, bf16[256,1024]{1,0:T(8,128)(2,1)S(1)}, u32[]{:S(2)}, u32[]{:S(2)}) collective-permute-start(bf16[256,1024]{1,0:T(8,128)(2,1)S(1)} %get-tuple-element.14.refs_0_), channel_id=1, source_target_pairs={{0,2},{1,3},{4,0},{5,1},{8,4},{9,5},{12,8},{13,9},{14,12},{15,13},... | collective-permute-start | bytes 1572872 | tf_op jit(solution)/shard_map/ppermute | solution.py:368
  8.4 16.4 %collective-permute-start = (bf16[256,1024]{1,0:T(8,128)(2,1)S(1)}, bf16[256,1024]{1,0:T(8,128)(2,1)}, u32[]{:S(2)}, u32[]{:S(2)}) collective-permute-start(bf16[256,1024]{1,0:T(8,128)(2,1)S(1)} %get-tuple-element.14.refs_0_), channel_id=1, source_target_pairs={{0,4},{1,5},{4,8},{5,9},{8,12},{9,13},{12,14},{13,15},{14,10},{15,... | collective-permute-start | bytes 1572872 | tf_op jit(solution)/shard_map/ppermute | solution.py:368
  8.4 39.0 %all-to-all-start = ((bf16[8,272,128]{2,1,0:T(8,128)(2,1)}), bf16[8,272,128]{2,1,0:T(8,128)(2,1)}, u32[]{:S(2)}, u32[]{:S(2)}) async-start(bf16[8,272,128]{2,1,0:T(8,128)(2,1)} %get-tuple-element.15), calls=%async_computation | async-start | bytes 1114112 | tf_op jit(solution)/shard_map/all_to_all | solution.py:383
  21.9 19.4 %copy-start.14 = (bf16[256,1024]{1,0:T(8,128)(2,1)}, bf16[256,1024]{1,0:T(8,128)(2,1)S(1)}, u32[]{:S(2)}) copy-start(bf16[256,1024]{1,0:T(8,128)(2,1)S(1)} %collective-permute-done.1.refs_2_) | copy-start | bytes 1572868
  21.9 18.7 %collective-permute-start.3 = (bf16[256,1024]{1,0:T(8,128)(2,1)S(1)}, bf16[256,1024]{1,0:T(8,128)(2,1)}, u32[]{:S(2)}, u32[]{:S(2)}) collective-permute-start(bf16[256,1024]{1,0:T(8,128)(2,1)S(1)} %collective-permute-done.1.refs_2_), channel_id=1, source_target_pairs={{0,2},{1,3},{4,0},{5,1},{8,4},{9,5},{12,8},{13,9},{14,12},{15,13},... | collective-permute-start | bytes 1572872 | tf_op jit(solution)/shard_map/ppermute | solution.py:368
  24.8 16.6 %collective-permute-start.2 = (bf16[256,1024]{1,0:T(8,128)(2,1)}, bf16[256,1024]{1,0:T(8,128)(2,1)}, u32[]{:S(2)}, u32[]{:S(2)}) collective-permute-start(bf16[256,1024]{1,0:T(8,128)(2,1)} %collective-permute-done.refs_1_), channel_id=1, source_target_pairs={{0,4},{1,5},{4,8},{5,9},{8,12},{9,13},{12,14},{13,15},{14,10},{15,... | collective-permute-start | bytes 1572872 | tf_op jit(solution)/shard_map/ppermute | solution.py:368
  26.1 19.3 %copy-start.24 = (bf16[1024,128]{1,0:T(8,128)(2,1)S(1)}, bf16[1024,128]{1,0:T(8,128)(2,1)}, u32[]{:S(2)}) copy-start(bf16[1024,128]{1,0:T(8,128)(2,1)} %get-tuple-element.33) | copy-start | bytes 786436
  40.6 16.0 %collective-permute-start.5 = (bf16[256,1024]{1,0:T(8,128)(2,1)}, bf16[256,1024]{1,0:T(8,128)(2,1)S(1)}, u32[]{:S(2)}, u32[]{:S(2)}) collective-permute-start(bf16[256,1024]{1,0:T(8,128)(2,1)} %collective-permute-done.3.refs_4_), channel_id=1, source_target_pairs={{0,2},{1,3},{4,0},{5,1},{8,4},{9,5},{12,8},{13,9},{14,12},{15,13},... | collective-permute-start | bytes 1572872 | tf_op jit(solution)/shard_map/ppermute | solution.py:368
  41.3 15.5 %collective-permute-start.4 = (bf16[256,1024]{1,0:T(8,128)(2,1)}, bf16[256,1024]{1,0:T(8,128)(2,1)S(1)}, u32[]{:S(2)}, u32[]{:S(2)}) collective-permute-start(bf16[256,1024]{1,0:T(8,128)(2,1)} %collective-permute-done.2.refs_3_), channel_id=1, source_target_pairs={{0,4},{1,5},{4,8},{5,9},{8,12},{9,13},{12,14},{13,15},{14,10},{15,... | collective-permute-start | bytes 1572872 | tf_op jit(solution)/shard_map/ppermute | solution.py:368
  47.4 11.4 %copy-start.25 = (bf16[1024,128]{1,0:T(8,128)(2,1)S(1)}, bf16[1024,128]{1,0:T(8,128)(2,1)}, u32[]{:S(2)}) copy-start(bf16[1024,128]{1,0:T(8,128)(2,1)} %get-tuple-element.33) | copy-start | bytes 786436
  47.4 18.3 %collective-permute-start.10 = (bf16[8,272,128]{2,1,0:T(8,128)(2,1)}, bf16[8,272,128]{2,1,0:T(8,128)(2,1)S(1)}, u32[]{:S(2)}, u32[]{:S(2)}) collective-permute-start(bf16[8,272,128]{2,1,0:T(8,128)(2,1)} %all-to-all-done.refs_4_), channel_id=1, source_target_pairs={{0,1},{1,0},{2,3},{3,2},{4,5},{5,4},{6,7},{7,6},{8,9},{9,8},{10,11... | collective-permute-start | bytes 1671176 | tf_op jit(solution)/shard_map/ppermute | solution.py:374
  51.6 14.1 %collective-permute-start.8 = (bf16[5,256,256]{2,1,0:T(8,128)(2,1)}, bf16[5,256,256]{2,1,0:T(8,128)(2,1)S(1)}, u32[]{:S(2)}, u32[]{:S(2)}) collective-permute-start(bf16[5,256,256]{2,1,0:T(8,128)(2,1)} %fusion.9.refs_0_), channel_id=1, source_target_pairs={{0,1},{1,0},{2,3},{3,2},{4,5},{5,4},{6,7},{7,6},{8,9},{9,8},{10,11... | collective-permute-start | bytes 1966088 | tf_op jit(solution)/shard_map/ppermute | solution.py:374
  56.6 7.4 %copy-start.5 = (bf16[256,1024]{1,0:T(8,128)(2,1)}, bf16[256,1024]{1,0:T(8,128)(2,1)S(1)}, u32[]{:S(2)}) copy-start(bf16[256,1024]{1,0:T(8,128)(2,1)S(1)} %collective-permute-done.5.refs_6_) | copy-start | bytes 1572868
  56.6 7.4 %collective-permute-start.7 = (bf16[128,1024]{1,0:T(8,128)(2,1)S(1)}, bf16[128,1024]{1,0:T(8,128)(2,1)S(1)}, u32[]{:S(2)}, u32[]{:S(2)}) collective-permute-start(bf16[128,1024]{1,0:T(8,128)(2,1)S(1)} %slice.41), channel_id=1, source_target_pairs={{0,2},{1,3},{4,0},{5,1},{8,4},{9,5},{12,8},{13,9},{14,12},{15,13},... | collective-permute-start | bytes 786440 | tf_op jit(solution)/shard_map/ppermute | solution.py:368
  56.9 7.2 %copy-start.7 = (bf16[256,1024]{1,0:T(8,128)(2,1)}, bf16[256,1024]{1,0:T(8,128)(2,1)S(1)}, u32[]{:S(2)}) copy-start(bf16[256,1024]{1,0:T(8,128)(2,1)S(1)} %collective-permute-done.4.refs_5_) | copy-start | bytes 1572868
  56.9 7.2 %collective-permute-start.6 = (bf16[128,1024]{1,0:T(8,128)(2,1)S(1)}, bf16[128,1024]{1,0:T(8,128)(2,1)S(1)}, u32[]{:S(2)}, u32[]{:S(2)}) collective-permute-start(bf16[128,1024]{1,0:T(8,128)(2,1)S(1)} %slice.40), channel_id=1, source_target_pairs={{0,4},{1,5},{4,8},{5,9},{8,12},{9,13},{12,14},{13,15},{14,10},{15,... | collective-permute-start | bytes 786440 | tf_op jit(solution)/shard_map/ppermute | solution.py:368
  65.0 1.8 %collective-permute-start.9 = (bf16[3,256,256]{2,1,0:T(8,128)(2,1)S(1)}, bf16[3,256,256]{2,1,0:T(8,128)(2,1)S(1)}, u32[]{:S(2)}, u32[]{:S(2)}) collective-permute-start(bf16[3,256,256]{2,1,0:T(8,128)(2,1)S(1)} %pad_maximum_fusion.1.refs_1_), channel_id=1, source_target_pairs={{0,1},{1,0},{2,3},{3,2},{4,5},{5,4},{6,7},{7,6},{8,9},{9,8},{10,11... | collective-permute-start | bytes 1179656 | tf_op jit(solution)/shard_map/ppermute | solution.py:374
  101.6 3.0 %collective-permute-start.11 = (bf16[8,256,256]{2,1,0:T(8,128)(2,1)}, bf16[8,256,256]{2,1,0:T(8,128)(2,1)S(1)}, u32[]{:S(2)}, u32[]{:S(2)}) collective-permute-start(bf16[8,256,256]{2,1,0:T(8,128)(2,1)} %get-tuple-element.17), channel_id=1, source_target_pairs={{0,1},{1,0},{2,3},{3,2},{4,5},{5,4},{6,7},{7,6},{8,9},{9,8},{10,11... | collective-permute-start | bytes 3145736 | tf_op jit(solution)/shard_map/ppermute | solution.py:374
  104.5 7.2 %copy-start.19 = (s32[2,8]{1,0:T(2,128)S(1)}, s32[2,8]{1,0:T(2,128)}, u32[]{:S(2)}) copy-start(s32[2,8]{1,0:T(2,128)} %dynamic-slice_bitcast_fusion.ids) | copy-start | bytes 196
  107.1 39.0 %all-to-all-start.1 = ((bf16[8,256,256]{2,1,0:T(8,128)(2,1)}), bf16[8,256,256]{2,1,0:T(8,128)(2,1)S(1)}, u32[]{:S(2)}, u32[]{:S(2)}) async-start(bf16[8,256,256]{2,1,0:T(8,128)(2,1)} %add_convert_fusion.grads), calls=%async_computation.1 | async-start | bytes 2097152 | tf_op jit(solution)/shard_map/all_to_all | solution.py:383
  117.0 29.1 %copy-start.17 = (f32[1024]{0:T(1024)S(1)}, f32[1024]{0:T(1024)}, u32[]{:S(2)}) copy-start(f32[1024]{0:T(1024)} %param.10) | copy-start | bytes 12292
  120.2 1.6 %collective-permute-start.12 = (bf16[8,64,256]{2,1,0:T(8,128)(2,1)S(1)}, bf16[8,64,256]{2,1,0:T(8,128)(2,1)S(1)}, u32[]{:S(2)}, u32[]{:S(2)}) collective-permute-start(bf16[8,64,256]{2,1,0:T(8,128)(2,1)S(1)} %get-tuple-element.19), channel_id=1, source_target_pairs={{0,1},{1,0},{2,3},{3,2},{4,5},{5,4},{6,7},{7,6},{8,9},{9,8},{10,11... | collective-permute-start | bytes 786440 | tf_op jit(solution)/shard_map/ppermute | solution.py:374
  122.5 8.9 %collective-permute-start.19 = (bf16[64,256]{1,0:T(8,128)(2,1)S(1)}, bf16[64,256]{1,0:T(8,128)(2,1)S(1)}, u32[]{:S(2)}, u32[]{:S(2)}) collective-permute-start(bf16[64,256]{1,0:T(8,128)(2,1)S(1)} %get-tuple-element.24), channel_id=1, source_target_pairs={{0,14},{1,15},{2,0},{3,1},{4,2},{5,3},{6,4},{7,5},{8,6},{9,7},{10,... | collective-permute-start | bytes 98312 | tf_op jit(solution)/shard_map/ppermute | solution.py:380
  127.2 5.5 %collective-permute-start.18 = (bf16[64,256]{1,0:T(8,128)(2,1)S(1)}, bf16[64,256]{1,0:T(8,128)(2,1)S(1)}, u32[]{:S(2)}, u32[]{:S(2)}) collective-permute-start(bf16[64,256]{1,0:T(8,128)(2,1)S(1)} %get-tuple-element.25), channel_id=1, source_target_pairs={{0,12},{1,13},{2,14},{3,15},{4,0},{5,1},{6,2},{7,3},{8,4},{9,5},{1... | collective-permute-start | bytes 98312 | tf_op jit(solution)/shard_map/ppermute | solution.py:380
  127.8 16.7 %collective-permute-start.17 = (bf16[64,256]{1,0:T(8,128)(2,1)}, bf16[64,256]{1,0:T(8,128)(2,1)S(1)}, u32[]{:S(2)}, u32[]{:S(2)}) collective-permute-start(bf16[64,256]{1,0:T(8,128)(2,1)} %get-tuple-element.26), channel_id=1, source_target_pairs={{0,10},{1,11},{2,12},{3,13},{4,14},{5,15},{6,0},{7,1},{8,2},{9,3},... | collective-permute-start | bytes 98312 | tf_op jit(solution)/shard_map/ppermute | solution.py:380
  127.8 16.7 %collective-permute-start.16 = (bf16[64,256]{1,0:T(8,128)(2,1)}, bf16[64,256]{1,0:T(8,128)(2,1)S(1)}, u32[]{:S(2)}, u32[]{:S(2)}) collective-permute-start(bf16[64,256]{1,0:T(8,128)(2,1)} %get-tuple-element.27), channel_id=1, source_target_pairs={{0,8},{1,9},{2,10},{3,11},{4,12},{5,13},{6,14},{7,15},{8,0},{9,1},... | collective-permute-start | bytes 98312 | tf_op jit(solution)/shard_map/ppermute | solution.py:380
  130.7 13.8 %collective-permute-start.15 = (bf16[64,256]{1,0:T(8,128)(2,1)S(1)}, bf16[64,256]{1,0:T(8,128)(2,1)S(1)}, u32[]{:S(2)}, u32[]{:S(2)}) collective-permute-start(bf16[64,256]{1,0:T(8,128)(2,1)S(1)} %get-tuple-element.28), channel_id=1, source_target_pairs={{0,6},{1,7},{2,8},{3,9},{4,10},{5,11},{6,12},{7,13},{8,14},{9,15},... | collective-permute-start | bytes 98312 | tf_op jit(solution)/shard_map/ppermute | solution.py:380
  131.4 13.1 %collective-permute-start.14 = (bf16[64,256]{1,0:T(8,128)(2,1)S(1)}, bf16[64,256]{1,0:T(8,128)(2,1)S(1)}, u32[]{:S(2)}, u32[]{:S(2)}) collective-permute-start(bf16[64,256]{1,0:T(8,128)(2,1)S(1)} %get-tuple-element.29), channel_id=1, source_target_pairs={{0,4},{1,5},{2,6},{3,7},{4,8},{5,9},{6,10},{7,11},{8,12},{9,13},{1... | collective-permute-start | bytes 98312 | tf_op jit(solution)/shard_map/ppermute | solution.py:380
  132.7 13.3 %collective-permute-start.13 = (bf16[64,256]{1,0:T(8,128)(2,1)S(1)}, bf16[64,256]{1,0:T(8,128)(2,1)S(1)}, u32[]{:S(2)}, u32[]{:S(2)}) collective-permute-start(bf16[64,256]{1,0:T(8,128)(2,1)S(1)} %get-tuple-element.30), channel_id=1, source_target_pairs={{0,2},{1,3},{2,4},{3,5},{4,6},{5,7},{6,8},{7,9},{8,10},{9,11},{10,... | collective-permute-start | bytes 98312 | tf_op jit(solution)/shard_map/ppermute | solution.py:380
  (16 other events, 17.0 us)

commit v3 on v2

--- a/solution.py
+++ b/solution.py
@@ -35,7 +35,7 @@
     refs = refs[per * pieces :]
     cot_refs = refs[:per]
     out_refs = refs[per : 2 * per]
-    table, picked, packed, log_sums, keys, values, queries, dq, dk, dv = refs[2 * per :]
+    table, picked, packed, log_sums, keys, values, queries, dq, dk, dv, halo = refs[2 * per :]
     chips, size, width = out_refs[0].shape
     head_dim = width // 2
     total = table.shape[0] // TILE
@@ -72,68 +72,48 @@
 
         lax.fori_loop(0, chips, fill, 0)
 
-    def gather(block):
-        start = block * BLOCK
-
-        def body(step, carry):
-            for u in range(32):
-                p = step * 32 + u
-                row = pl.multiple_of(order[start + p] * TILE, TILE)
-                picked[pl.ds(pl.multiple_of(p * TILE, TILE), TILE), :] = table[pl.ds(row, TILE), :]
-            return carry
-
-        lax.fori_loop(0, BLOCK // 32, body, 0)
-
-    def scatter(block):
-        start = block * BLOCK
-
-        def body(step, carry):
-            for u in range(32):
-                p = step * 32 + u
-                row = pl.multiple_of(order[start + p] * TILE, TILE)
-                table[pl.ds(row, TILE), :] = packed[pl.ds(pl.multiple_of(p * TILE, TILE), TILE), :]
-            return carry
-
-        lax.fori_loop(0, BLOCK // 32, body, 0)
+    def rows_of(block):
+        start = lax.rem(block, block_total) * BLOCK
+        for p in range(BLOCK):
+            yield p * TILE, pl.multiple_of(order[start + p] * TILE, TILE)
+
+    def gather(block, slot):
+        for place, row in rows_of(block):
+            picked[slot, place : place + TILE, :] = table[pl.ds(row, TILE), :]
+
+    def scatter(block, slot):
+        for place, row in rows_of(block):
+            table[pl.ds(row, TILE), :] = packed[slot, place : place + TILE, :]
 
     def load(slot):
-        q = picked[every(0, BLOCK), :]
+        q = picked[slot, every(0, BLOCK), :]
         scale = lax.rsqrt(jnp.mean(q * q, axis=-1, keepdims=True) + EPS) * (1.0 / math.sqrt(head_dim))
         queries[slot] = q
         keys[slot] = (q * scale).astype(BF16)
-        values[slot] = picked[every(1, BLOCK), :].astype(BF16)
-
-    def finish(slot, block):
-        q = queries[slot]
-        d_key = dk[slot]
+        values[slot] = picked[slot, every(1, BLOCK), :].astype(BF16)
+
+    def finish(slot, q, d_query, d_key, d_value):
         scale = lax.rsqrt(jnp.mean(q * q, axis=-1, keepdims=True) + EPS)
         inner = jnp.mean(q * d_key, axis=-1, keepdims=True)
         pulled = (scale * (1.0 / math.sqrt(head_dim))) * (d_key - q * (scale * scale * inner))
-        packed[every(3, BLOCK), :] = dq[slot] + pulled
-        packed[every(4, BLOCK), :] = dv[slot]
-        scatter(block)
-
-    halo_block = lax.rem(first_block + block_total - 1, block_total)
-    gather(halo_block)
-    load(2)
-    dk[2] = jnp.zeros_like(dk[2])
-    dv[2] = jnp.zeros_like(dv[2])
-    dq[2] = jnp.zeros_like(dq[2])
-
-    row_id = lax.broadcasted_iota(jnp.int32, (BLOCK, BLOCK), 0)
-    col_id = lax.broadcasted_iota(jnp.int32, (BLOCK, BLOCK), 1)
-    diagonal = row_id == col_id
-
-    def step(b, carry):
+        packed[slot, every(3, BLOCK), :] = pulled if d_query is None else d_query + pulled
+        packed[slot, every(4, BLOCK), :] = d_value
+
+    diagonal = lax.broadcasted_iota(jnp.int32, (BLOCK, BLOCK), 0) == lax.broadcasted_iota(
+        jnp.int32, (BLOCK, BLOCK), 1
+    )
+
+    def step(b, cur, first=False, write=True):
         block = first_block + b
-        cur = lax.rem(b, 2)
-        prev = jnp.where(b == 0, 2, 1 - cur)
-        gather(block)
+        prev = 1 - cur
+        gather(block + 1, prev)
+        if write:
+            scatter(block - 2, cur)
         load(cur)
         log_sum = jnp.concatenate(
             [log_sums[block, k : k + 1, :] for k in range(BLOCK // head_dim)], axis=1
         )
-        cot = picked[every(2, BLOCK), :].astype(BF16)
+        cot = picked[cur, every(2, BLOCK), :].astype(BF16)
         query = queries[cur].astype(BF16)
         key_a, key_b = keys[prev], keys[cur]
         w_a = jnp.exp(dot(key_a, query, NT) - log_sum)
@@ -143,26 +123,43 @@
         delta = jnp.sum(w_a * dw_a + w_b * dw_b, axis=0, keepdims=True)
         ds_a = (w_a * (dw_a - delta)).astype(BF16)
         ds_b = (w_b * (dw_b - delta)).astype(BF16)
-        dv[prev] = dv[prev] + dot(w_a.astype(BF16), cot, NN)
+        dv_a = dot(w_a.astype(BF16), cot, NN)
+        dk_a = dot(ds_a, query, NN)
+        if first:
+            halo[0] = dk_a
+            halo[1] = dv_a
+        else:
+            finish(prev, queries[prev], dq[prev], dk[prev] + dk_a, dv[prev] + dv_a)
         dv[cur] = dot(w_b.astype(BF16), cot, NN)
-        dk[prev] = dk[prev] + dot(ds_a, query, NN)
         dk[cur] = dot(ds_b, query, NN)
         dq[cur] = (dot(key_a, ds_a, TN) + dot(key_b, ds_b, TN)).T
 
-        @pl.when(b > 0)
-        def _():
-            finish(prev, block - 1)
-
+    halo_block = first_block + block_total - 1
+    gather(halo_block, 1)
+    load(1)
+    if parts > 1:
+        halo[2] = queries[1]
+    gather(first_block, 0)
+    step(0, 0, first=True, write=False)
+    step(1, 1, write=False)
+
+    def pair(i, carry):
+        step(2 * i, 0)
+        step(2 * i + 1, 1)
         return carry
 
-    lax.fori_loop(0, blocks, step, 0)
+    lax.fori_loop(1, blocks // 2, pair, 0)
+    if blocks % 2:
+        step(blocks - 1, 0)
     last = (blocks - 1) % 2
+    scatter(first_block + blocks - 2, 1 - last)
     if parts == 1:
-        dk[last] = dk[last] + dk[2]
-        dv[last] = dv[last] + dv[2]
+        finish(last, queries[last], dq[last], dk[last] + halo[0], dv[last] + halo[1])
     else:
-        finish(2, halo_block)
-    finish(last, first_block + blocks - 1)
+        finish(1 - last, halo[2], None, halo[0], halo[1])
+        scatter(halo_block, 1 - last)
+        finish(last, queries[last], dq[last], dk[last], dv[last])
+    scatter(first_block + blocks - 1, last)
 
     for m in range(per):
 
@@ -191,14 +188,15 @@
         out_specs=[vmem] * per,
         scratch_shapes=[
             pltpu.VMEM((total * TILE, head_dim), F32),
-            pltpu.VMEM((BLOCK * TILE, head_dim), F32),
-            pltpu.VMEM((BLOCK * TILE, head_dim), F32),
+            pltpu.VMEM((2, BLOCK * TILE, head_dim), F32),
+            pltpu.VMEM((2, BLOCK * TILE, head_dim), F32),
             pltpu.VMEM((total // BLOCK, TILE, head_dim), F32),
-            pltpu.VMEM((3, BLOCK, head_dim), BF16),
-            pltpu.VMEM((3, BLOCK, head_dim), BF16),
-            pltpu.VMEM((3, BLOCK, head_dim), F32),
-            pltpu.VMEM((3, BLOCK, head_dim), F32),
-            pltpu.VMEM((3, BLOCK, head_dim), F32),
+            pltpu.VMEM((2, BLOCK, head_dim), BF16),
+            pltpu.VMEM((2, BLOCK, head_dim), BF16),
+            pltpu.VMEM((2, BLOCK, head_dim), F32),
+            pltpu.VMEM((2, BLOCK, head_dim), F32),
+            pltpu.VMEM((2, BLOCK, head_dim), F32),
+            pltpu.VMEM((2, BLOCK, head_dim), F32),
             pltpu.VMEM((3, BLOCK, head_dim), F32),
         ],
         compiler_params=pltpu.CompilerParams(vmem_limit_bytes=VMEM_BYTES),

time: 153 us -> 140 us (0.915)
  Pallas kernels: 41.3 us -> 28.3 us
    pallas_call x1, Pallas kernels: 34 us -> 21 us  [attention(): pl.pallas_call(partial(attention_kernel, per, parts, blocks, rounds, len(...]
  transfers between devices with their start and end apart: 22 -> 22, of which waited for: 11 -> 11; matrix products, arithmetic and copies ran while one was open for 10% -> 11% of each run, Pallas kernels for 2% -> 2%
where the time goes in v3:
time: 140 us; the launch traced here: 139 us
  starting transfers between devices  46.1 us (33%)
  waiting for transfers between devices  32.6 us (23%)
  Pallas kernels  28.3 us (20%)
  local copies, waits for them, and re-layouts  17.1 us (12%)
  matrix products  11.1 us (8%)
  other arithmetic  3.33 us (2%)
    ppermute x8, waiting for transfers between devices, hop(): return lax.ppermute(x, 'tok', route)  25.2 us
    ppermute x7, starting transfers between devices, send(): return lax.ppermute(x, 'tok', route)  21.2 us
    pallas_call x1, Pallas kernels, attention(): pl.pallas_call(partial(attention_kernel, per, parts, blocks, rounds, len(...  21 us
    unnamed x53, local copies, waits for them, and re-layouts  12.8 us
    ppermute x8, starting transfers between devices, hop(): return lax.ppermute(x, 'tok', route)  12.8 us
    dot_general x8, matrix products, project(): jnp.dot(n, my_weights, preferred_element_type=F32).astype(BF16)  11.1 us
    all_to_all x2, starting transfers between devices, exchange(): return lax.all_to_all(x, 'tok', 0, 0, tiled=True, axis_index_groups=groups)  11 us
    ppermute x5, waiting for transfers between devices, swap(): return lax.ppermute(x, 'tok', route)  5 us
  transfers between devices with their start and end apart: 22, of which 11 were waited for; matrix products, arithmetic and copies ran while one was open for 11% of the time, Pallas kernels for 2%

profile of v3, /device:TPU:0, one launch (start us, length us, event | category | flops | bytes accessed | tf_op | source)
XLA Modules:
  0.0 139.3 jit_solution(13378751717595577070)
XLA Ops:
  0.7 1.2 copy-done.3
  4.3 1.1 prepare.1
  5.4 3.0 %collective-permute-start.1 = (bf16[256,1024]{1,0:T(8,128)(2,1)S(1)}, bf16[256,1024]{1,0:T(8,128)(2,1)S(1)}, u32[]{:S(2)}, u32[]{:S(2)}) collective-permute-start(bf16[256,1024]{1,0:T(8,128)(2,1)S(1)} %get-tuple-element.14.refs_0_), channel_id=1, source_target_pairs={{0,2},{1,3},{4,0},{5,1},{8,4},{9,5},{12,8},{13,9},{14,12},{15,13},... | collective-permute-start | bytes 1572872 | tf_op jit(solution)/shard_map/ppermute | solution.py:366
  8.4 6.3 %all-to-all-start = ((bf16[8,272,128]{2,1,0:T(8,128)(2,1)}), bf16[8,272,128]{2,1,0:T(8,128)(2,1)}, u32[]{:S(2)}, u32[]{:S(2)}) async-start(bf16[8,272,128]{2,1,0:T(8,128)(2,1)} %get-tuple-element.15), calls=%async_computation | async-start | bytes 1114112 | tf_op jit(solution)/shard_map/all_to_all | solution.py:381
  14.7 1.7 %constant_dynamic-slice_fusion = (bf16[1024,128]{1,0:T(8,128)(2,1)S(1)}, bf16[1024,128]{1,0:T(8,128)(2,1)}) fusion(bf16[1024,1024]{1,0:T(8,128)(2,1)S(1)} %copy-done.1, s32[]{:T(128)S(6)} %select_n.35, bf16[1024,1024]{1,0:T(8,128)(2,1)} %w_qk.1), kind=kLoop, calls=%fused_computation.36 | loop fusion | bytes 1048580 | tf_op jit(solution)/shard_map/dynamic_slice | solution.py:402
  16.4 5.5 %collective-permute-done.1.refs_2_ = bf16[256,1024]{1,0:T(8,128)(2,1)S(1)} collective-permute-done((bf16[256,1024]{1,0:T(8,128)(2,1)S(1)}, bf16[256,1024]{1,0:T(8,128)(2,1)S(1)}, u32[]{:S(2)}, u32[]{:S(2)}) %collective-permute-start.1) | collective-permute-done | bytes 524320 | tf_op jit(solution)/shard_map/ppermute | solution.py:366
  21.9 2.8 %collective-permute-start.3 = (bf16[256,1024]{1,0:T(8,128)(2,1)S(1)}, bf16[256,1024]{1,0:T(8,128)(2,1)}, u32[]{:S(2)}, u32[]{:S(2)}) collective-permute-start(bf16[256,1024]{1,0:T(8,128)(2,1)S(1)} %collective-permute-done.1.refs_2_), channel_id=1, source_target_pairs={{0,2},{1,3},{4,0},{5,1},{8,4},{9,5},{12,8},{13,9},{14,12},{15,13},... | collective-permute-start | bytes 1572872 | tf_op jit(solution)/shard_map/ppermute | solution.py:366
  24.9 1.2 dynamic-slice_bitcast_fusion.ids
  26.1 2.0 %fusion.1 = bf16[5,256,256]{2,1,0:T(8,128)(2,1)} fusion(bf16[256,1024]{1,0:T(8,128)(2,1)S(1)} %get-tuple-element.14.refs_0_, bf16[1024,128]{1,0:T(8,128)(2,1)S(1)} %get-tuple-element.32, bf16[1024,128]{1,0:T(8,128)(2,1)} %get-tuple-element.33), kind=kOutput, calls=%fused_computation.10 | convolution fusion | flops 135331840 | bytes 1179648 | tf_op jit(solution)/shard_map/dot_general | solution.py:408
  28.1 2.1 %fusion.3 = bf16[5,256,256]{2,1,0:T(8,128)(2,1)} fusion(bf16[5,256,256]{2,1,0:T(8,128)(2,1)} %fusion.1, bf16[256,1024]{1,0:T(8,128)(2,1)} %collective-permute-done.refs_1_, bf16[1024,128]{1,0:T(8,128)(2,1)S(1)} %get-tuple-element.32, bf16[1024,128]{1,0:T(8,128)(2,1)} %get-tuple-element.33), kind=kOutput, calls=%fused_computation.12 | convolution fusion | flops 135331840 | bytes 1179648 | tf_op jit(solution)/shard_map/dot_general | solution.py:408
  30.2 10.5 %collective-permute-done.3.refs_4_ = bf16[256,1024]{1,0:T(8,128)(2,1)} collective-permute-done((bf16[256,1024]{1,0:T(8,128)(2,1)S(1)}, bf16[256,1024]{1,0:T(8,128)(2,1)}, u32[]{:S(2)}, u32[]{:S(2)}) %collective-permute-start.3) | collective-permute-done | bytes 524320 | tf_op jit(solution)/shard_map/ppermute | solution.py:366
  41.3 4.1 %collective-permute-start.4 = (bf16[256,1024]{1,0:T(8,128)(2,1)}, bf16[256,1024]{1,0:T(8,128)(2,1)S(1)}, u32[]{:S(2)}, u32[]{:S(2)}) collective-permute-start(bf16[256,1024]{1,0:T(8,128)(2,1)} %collective-permute-done.2.refs_3_), channel_id=1, source_target_pairs={{0,4},{1,5},{4,8},{5,9},{8,12},{9,13},{12,14},{13,15},{14,10},{15,... | collective-permute-start | bytes 1572872 | tf_op jit(solution)/shard_map/ppermute | solution.py:366
  45.4 2.0 %fusion.5 = bf16[5,256,256]{2,1,0:T(8,128)(2,1)} fusion(bf16[5,256,256]{2,1,0:T(8,128)(2,1)} %fusion.3, bf16[256,1024]{1,0:T(8,128)(2,1)} %copy-done.14, bf16[1024,128]{1,0:T(8,128)(2,1)S(1)} %get-tuple-element.32, bf16[1024,128]{1,0:T(8,128)(2,1)S(1)} %copy-done.24), kind=kOutput, calls=%fused_computation.14 | convolution fusion | flops 135331840 | bytes 1179648 | tf_op jit(solution)/shard_map/dot_general | solution.py:408
  47.4 2.1 %fusion.7 = bf16[5,256,256]{2,1,0:T(8,128)(2,1)} fusion(bf16[5,256,256]{2,1,0:T(8,128)(2,1)} %fusion.5, bf16[256,1024]{1,0:T(8,128)(2,1)} %collective-permute-done.2.refs_3_, bf16[1024,128]{1,0:T(8,128)(2,1)S(1)} %get-tuple-element.32, bf16[1024,128]{1,0:T(8,128)(2,1)} %get-tuple-element.33), kind=kOutput, calls=%fused_computation.16 | convolution fusion | flops 135331840 | bytes 1179648 | tf_op jit(solution)/shard_map/dot_general | solution.py:408
  49.5 2.1 %fusion.9.refs_0_ = bf16[5,256,256]{2,1,0:T(8,128)(2,1)} fusion(bf16[5,256,256]{2,1,0:T(8,128)(2,1)} %fusion.7, bf16[256,1024]{1,0:T(8,128)(2,1)} %collective-permute-done.3.refs_4_, bf16[1024,128]{1,0:T(8,128)(2,1)S(1)} %get-tuple-element.32, bf16[1024,128]{1,0:T(8,128)(2,1)} %get-tuple-element.33), kind=kOutput, calls=%fused_computation.18 | convolution fusion | flops 135331840 | bytes 1179648 | tf_op jit(solution)/shard_map/dot_general | solution.py:408
  52.1 4.5 %collective-permute-done.5.refs_6_ = bf16[256,1024]{1,0:T(8,128)(2,1)S(1)} collective-permute-done((bf16[256,1024]{1,0:T(8,128)(2,1)}, bf16[256,1024]{1,0:T(8,128)(2,1)S(1)}, u32[]{:S(2)}, u32[]{:S(2)}) %collective-permute-start.5) | collective-permute-done | bytes 524320 | tf_op jit(solution)/shard_map/ppermute | solution.py:366
  56.9 1.9 %collective-permute-start.6 = (bf16[128,1024]{1,0:T(8,128)(2,1)S(1)}, bf16[128,1024]{1,0:T(8,128)(2,1)S(1)}, u32[]{:S(2)}, u32[]{:S(2)}) collective-permute-start(bf16[128,1024]{1,0:T(8,128)(2,1)S(1)} %slice.40), channel_id=1, source_target_pairs={{0,4},{1,5},{4,8},{5,9},{8,12},{9,13},{12,14},{13,15},{14,10},{15,... | collective-permute-start | bytes 786440 | tf_op jit(solution)/shard_map/ppermute | solution.py:366
  59.4 4.6 %collective-permute-done.6 = bf16[128,1024]{1,0:T(8,128)(2,1)S(1)} collective-permute-done((bf16[128,1024]{1,0:T(8,128)(2,1)S(1)}, bf16[128,1024]{1,0:T(8,128)(2,1)S(1)}, u32[]{:S(2)}, u32[]{:S(2)}) %collective-permute-start.6) | collective-permute-done | bytes 262176 | tf_op jit(solution)/shard_map/ppermute | solution.py:366
  65.8 1.0 collective-permute-done.9.refs_3_
  67.6 21.0 %attention.1 = (bf16[8,256,256]{2,1,0:T(8,128)(2,1)}, bf16[8,256,256]{2,1,0:T(8,128)(2,1)}) custom-call(s32[2,8]{1,0:T(2,128)} %dynamic-slice_bitcast_fusion.ids, s32[4096]{0:T(1024)} %bitcast.56, bf16[5,256,256]{2,1,0:T(8,128)(2,1)} %fusion.9.refs_0_, bf16[3,256,256]{2,1,0:T(8,128)(2,1)} %copy-done.20, bf16[5,256,256]{2,1,0:T(8,128)(2,1)} %copy-done.21, ...), custom_call_target="tpu_custom_call" | custom-call | tf_op jit(solution)/shard_map/attention/pallas_call | solution.py:184
  89.0 2.5 %collective-permute-done.11 = bf16[8,256,256]{2,1,0:T(8,128)(2,1)S(1)} collective-permute-done((bf16[8,256,256]{2,1,0:T(8,128)(2,1)}, bf16[8,256,256]{2,1,0:T(8,128)(2,1)S(1)}, u32[]{:S(2)}, u32[]{:S(2)}) %collective-permute-start.11) | collective-permute-done | bytes 1048608 | tf_op jit(solution)/shard_map/ppermute | solution.py:372
  91.5 2.5 %add_convert_fusion.grads = bf16[8,256,256]{2,1,0:T(8,128)(2,1)} fusion(bf16[8,256,256]{2,1,0:T(8,128)(2,1)S(1)} %collective-permute-done.11, bf16[8,256,256]{2,1,0:T(8,128)(2,1)} %get-tuple-element.16), kind=kLoop, calls=%fused_computation | loop fusion | flops 2097152 | bytes 3145728 | tf_op jit(solution)/shard_map/convert_element_type | solution.py:419
  94.0 4.7 %all-to-all-start.1 = ((bf16[8,256,256]{2,1,0:T(8,128)(2,1)}), bf16[8,256,256]{2,1,0:T(8,128)(2,1)S(1)}, u32[]{:S(2)}, u32[]{:S(2)}) async-start(bf16[8,256,256]{2,1,0:T(8,128)(2,1)} %add_convert_fusion.grads), calls=%async_computation.1 | async-start | bytes 2097152 | tf_op jit(solution)/shard_map/all_to_all | solution.py:381
  103.9 3.2 %weight_grad.1 = (bf16[8,64,256]{2,1,0:T(8,128)(2,1)S(1)}, bf16[8,64,256]{2,1,0:T(8,128)(2,1)S(1)}) custom-call(s32[2,8]{1,0:T(2,128)S(1)} %copy-done.19, bf16[8,256,256]{2,1,0:T(8,128)(2,1)} %add_convert_fusion.grads, bf16[256,1024]{1,0:T(8,128)(2,1)S(1)} %copy-done.13, bf16[256,1024]{1,0:T(8,128)(2,1)} %collective-permute-done.refs_1_, ...), custom_call_target="tpu_custom_call" | custom-call | tf_op jit(solution)/shard_map/weight_grad/pallas_call | solution.py:266
  107.3 1.5 %collective-permute-done.12 = bf16[8,64,256]{2,1,0:T(8,128)(2,1)S(1)} collective-permute-done((bf16[8,64,256]{2,1,0:T(8,128)(2,1)S(1)}, bf16[8,64,256]{2,1,0:T(8,128)(2,1)S(1)}, u32[]{:S(2)}, u32[]{:S(2)}) %collective-permute-start.12) | collective-permute-done | bytes 262176 | tf_op jit(solution)/shard_map/ppermute | solution.py:372
  109.5 4.7 %collective-permute-start.19 = (bf16[64,256]{1,0:T(8,128)(2,1)S(1)}, bf16[64,256]{1,0:T(8,128)(2,1)S(1)}, u32[]{:S(2)}, u32[]{:S(2)}) collective-permute-start(bf16[64,256]{1,0:T(8,128)(2,1)S(1)} %get-tuple-element.24), channel_id=1, source_target_pairs={{0,14},{1,15},{2,0},{3,1},{4,2},{5,3},{6,4},{7,5},{8,6},{9,7},{10,... | collective-permute-start | bytes 98312 | tf_op jit(solution)/shard_map/ppermute | solution.py:378
  114.7 2.9 %collective-permute-start.16 = (bf16[64,256]{1,0:T(8,128)(2,1)}, bf16[64,256]{1,0:T(8,128)(2,1)S(1)}, u32[]{:S(2)}, u32[]{:S(2)}) collective-permute-start(bf16[64,256]{1,0:T(8,128)(2,1)} %get-tuple-element.27), channel_id=1, source_target_pairs={{0,8},{1,9},{2,10},{3,11},{4,12},{5,13},{6,14},{7,15},{8,0},{9,1},... | collective-permute-start | bytes 98312 | tf_op jit(solution)/shard_map/ppermute | solution.py:378
  118.4 1.3 collective-permute-start.14
  119.7 11.7 %collective-permute-start.13 = (bf16[64,256]{1,0:T(8,128)(2,1)S(1)}, bf16[64,256]{1,0:T(8,128)(2,1)S(1)}, u32[]{:S(2)}, u32[]{:S(2)}) collective-permute-start(bf16[64,256]{1,0:T(8,128)(2,1)S(1)} %get-tuple-element.30), channel_id=1, source_target_pairs={{0,2},{1,3},{2,4},{3,5},{4,6},{5,7},{6,8},{7,9},{8,10},{9,11},{10,... | collective-permute-start | bytes 98312 | tf_op jit(solution)/shard_map/ppermute | solution.py:378
  131.5 1.5 %collective-permute-done.13.refs_1_ = bf16[64,256]{1,0:T(8,128)(2,1)S(1)} collective-permute-done((bf16[64,256]{1,0:T(8,128)(2,1)S(1)}, bf16[64,256]{1,0:T(8,128)(2,1)S(1)}, u32[]{:S(2)}, u32[]{:S(2)}) %collective-permute-start.13) | collective-permute-done | bytes 32800 | tf_op jit(solution)/shard_map/ppermute | solution.py:378
  133.0 1.6 %copy-done.2 = bf16[1024,1024]{1,0:T(8,128)(2,1)S(1)} copy-done((bf16[1024,1024]{1,0:T(8,128)(2,1)S(1)}, bf16[1024,1024]{1,0:T(8,128)(2,1)}, u32[]{:S(2)}) %copy-start.2) | copy-done | bytes 2097176
  135.6 2.9 %home.1 = (bf16[256,1024]{1,0:T(8,128)(2,1)}, f32[64,1024]{1,0:T(8,128)}, f32[64,1024]{1,0:T(8,128)}, f32[64,1]{1,0:T(8,128)S(1)}) custom-call(s32[2,8]{1,0:T(2,128)S(1)} %copy-done.19, bf16[8,256,256]{2,1,0:T(8,128)(2,1)S(1)} %all-to-all-done.1.grads, bf16[1024,1024]{1,0:T(8,128)(2,1)S(1)} %copy-done.2, bf16[1024,1024]{1,0:T(8,128)(2,1)S(1)} %copy-done.1, ...), custom_call_target="tpu_custom_call" | custom-call | tf_op jit(solution)/shard_map/home/pallas_call | solution.py:313
  (89 shorter events, 16.7 us)
Async XLA Ops:
  0.6 64.5 %copy-start = (s32[2,4096]{1,0:T(2,128)S(1)}, s32[2,4096]{1,0:T(2,128)}, u32[]{:S(2)}) copy-start(s32[2,4096]{1,0:T(2,128)} %param.15) | copy-start | bytes 98308
  0.6 14.1 %copy-start.1 = (bf16[1024,1024]{1,0:T(8,128)(2,1)S(1)}, bf16[1024,1024]{1,0:T(8,128)(2,1)}, u32[]{:S(2)}) copy-start(bf16[1024,1024]{1,0:T(8,128)(2,1)} %w_v.1) | copy-start | bytes 6291460
  5.4 24.8 %copy-start.12 = (bf16[256,1024]{1,0:T(8,128)(2,1)}, bf16[256,1024]{1,0:T(8,128)(2,1)S(1)}, u32[]{:S(2)}) copy-start(bf16[256,1024]{1,0:T(8,128)(2,1)S(1)} %get-tuple-element.14.refs_0_) | copy-start | bytes 1572868
  5.4 16.5 %collective-permute-start.1 = (bf16[256,1024]{1,0:T(8,128)(2,1)S(1)}, bf16[256,1024]{1,0:T(8,128)(2,1)S(1)}, u32[]{:S(2)}, u32[]{:S(2)}) collective-permute-start(bf16[256,1024]{1,0:T(8,128)(2,1)S(1)} %get-tuple-element.14.refs_0_), channel_id=1, source_target_pairs={{0,2},{1,3},{4,0},{5,1},{8,4},{9,5},{12,8},{13,9},{14,12},{15,13},... | collective-permute-start | bytes 1572872 | tf_op jit(solution)/shard_map/ppermute | solution.py:366
  8.4 16.4 %collective-permute-start = (bf16[256,1024]{1,0:T(8,128)(2,1)S(1)}, bf16[256,1024]{1,0:T(8,128)(2,1)}, u32[]{:S(2)}, u32[]{:S(2)}) collective-permute-start(bf16[256,1024]{1,0:T(8,128)(2,1)S(1)} %get-tuple-element.14.refs_0_), channel_id=1, source_target_pairs={{0,4},{1,5},{4,8},{5,9},{8,12},{9,13},{12,14},{13,15},{14,10},{15,... | collective-permute-start | bytes 1572872 | tf_op jit(solution)/shard_map/ppermute | solution.py:366
  8.4 39.0 %all-to-all-start = ((bf16[8,272,128]{2,1,0:T(8,128)(2,1)}), bf16[8,272,128]{2,1,0:T(8,128)(2,1)}, u32[]{:S(2)}, u32[]{:S(2)}) async-start(bf16[8,272,128]{2,1,0:T(8,128)(2,1)} %get-tuple-element.15), calls=%async_computation | async-start | bytes 1114112 | tf_op jit(solution)/shard_map/all_to_all | solution.py:381
  21.9 19.4 %copy-start.14 = (bf16[256,1024]{1,0:T(8,128)(2,1)}, bf16[256,1024]{1,0:T(8,128)(2,1)S(1)}, u32[]{:S(2)}) copy-start(bf16[256,1024]{1,0:T(8,128)(2,1)S(1)} %collective-permute-done.1.refs_2_) | copy-start | bytes 1572868
  21.9 18.7 %collective-permute-start.3 = (bf16[256,1024]{1,0:T(8,128)(2,1)S(1)}, bf16[256,1024]{1,0:T(8,128)(2,1)}, u32[]{:S(2)}, u32[]{:S(2)}) collective-permute-start(bf16[256,1024]{1,0:T(8,128)(2,1)S(1)} %collective-permute-done.1.refs_2_), channel_id=1, source_target_pairs={{0,2},{1,3},{4,0},{5,1},{8,4},{9,5},{12,8},{13,9},{14,12},{15,13},... | collective-permute-start | bytes 1572872 | tf_op jit(solution)/shard_map/ppermute | solution.py:366
  24.8 16.6 %collective-permute-start.2 = (bf16[256,1024]{1,0:T(8,128)(2,1)}, bf16[256,1024]{1,0:T(8,128)(2,1)}, u32[]{:S(2)}, u32[]{:S(2)}) collective-permute-start(bf16[256,1024]{1,0:T(8,128)(2,1)} %collective-permute-done.refs_1_), channel_id=1, source_target_pairs={{0,4},{1,5},{4,8},{5,9},{8,12},{9,13},{12,14},{13,15},{14,10},{15,... | collective-permute-start | bytes 1572872 | tf_op jit(solution)/shard_map/ppermute | solution.py:366
  26.1 19.3 %copy-start.24 = (bf16[1024,128]{1,0:T(8,128)(2,1)S(1)}, bf16[1024,128]{1,0:T(8,128)(2,1)}, u32[]{:S(2)}) copy-start(bf16[1024,128]{1,0:T(8,128)(2,1)} %get-tuple-element.33) | copy-start | bytes 786436
  40.6 16.0 %collective-permute-start.5 = (bf16[256,1024]{1,0:T(8,128)(2,1)}, bf16[256,1024]{1,0:T(8,128)(2,1)S(1)}, u32[]{:S(2)}, u32[]{:S(2)}) collective-permute-start(bf16[256,1024]{1,0:T(8,128)(2,1)} %collective-permute-done.3.refs_4_), channel_id=1, source_target_pairs={{0,2},{1,3},{4,0},{5,1},{8,4},{9,5},{12,8},{13,9},{14,12},{15,13},... | collective-permute-start | bytes 1572872 | tf_op jit(solution)/shard_map/ppermute | solution.py:366
  41.3 15.5 %collective-permute-start.4 = (bf16[256,1024]{1,0:T(8,128)(2,1)}, bf16[256,1024]{1,0:T(8,128)(2,1)S(1)}, u32[]{:S(2)}, u32[]{:S(2)}) collective-permute-start(bf16[256,1024]{1,0:T(8,128)(2,1)} %collective-permute-done.2.refs_3_), channel_id=1, source_target_pairs={{0,4},{1,5},{4,8},{5,9},{8,12},{9,13},{12,14},{13,15},{14,10},{15,... | collective-permute-start | bytes 1572872 | tf_op jit(solution)/shard_map/ppermute | solution.py:366
  47.4 11.4 %copy-start.25 = (bf16[1024,128]{1,0:T(8,128)(2,1)S(1)}, bf16[1024,128]{1,0:T(8,128)(2,1)}, u32[]{:S(2)}) copy-start(bf16[1024,128]{1,0:T(8,128)(2,1)} %get-tuple-element.33) | copy-start | bytes 786436
  47.4 18.3 %collective-permute-start.10 = (bf16[8,272,128]{2,1,0:T(8,128)(2,1)}, bf16[8,272,128]{2,1,0:T(8,128)(2,1)S(1)}, u32[]{:S(2)}, u32[]{:S(2)}) collective-permute-start(bf16[8,272,128]{2,1,0:T(8,128)(2,1)} %all-to-all-done.refs_4_), channel_id=1, source_target_pairs={{0,1},{1,0},{2,3},{3,2},{4,5},{5,4},{6,7},{7,6},{8,9},{9,8},{10,11... | collective-permute-start | bytes 1671176 | tf_op jit(solution)/shard_map/ppermute | solution.py:372
  51.6 14.1 %collective-permute-start.8 = (bf16[5,256,256]{2,1,0:T(8,128)(2,1)}, bf16[5,256,256]{2,1,0:T(8,128)(2,1)S(1)}, u32[]{:S(2)}, u32[]{:S(2)}) collective-permute-start(bf16[5,256,256]{2,1,0:T(8,128)(2,1)} %fusion.9.refs_0_), channel_id=1, source_target_pairs={{0,1},{1,0},{2,3},{3,2},{4,5},{5,4},{6,7},{7,6},{8,9},{9,8},{10,11... | collective-permute-start | bytes 1966088 | tf_op jit(solution)/shard_map/ppermute | solution.py:372
  56.6 7.4 %copy-start.5 = (bf16[256,1024]{1,0:T(8,128)(2,1)}, bf16[256,1024]{1,0:T(8,128)(2,1)S(1)}, u32[]{:S(2)}) copy-start(bf16[256,1024]{1,0:T(8,128)(2,1)S(1)} %collective-permute-done.5.refs_6_) | copy-start | bytes 1572868
  56.6 7.4 %collective-permute-start.7 = (bf16[128,1024]{1,0:T(8,128)(2,1)S(1)}, bf16[128,1024]{1,0:T(8,128)(2,1)S(1)}, u32[]{:S(2)}, u32[]{:S(2)}) collective-permute-start(bf16[128,1024]{1,0:T(8,128)(2,1)S(1)} %slice.41), channel_id=1, source_target_pairs={{0,2},{1,3},{4,0},{5,1},{8,4},{9,5},{12,8},{13,9},{14,12},{15,13},... | collective-permute-start | bytes 786440 | tf_op jit(solution)/shard_map/ppermute | solution.py:366
  56.9 7.2 %copy-start.7 = (bf16[256,1024]{1,0:T(8,128)(2,1)}, bf16[256,1024]{1,0:T(8,128)(2,1)S(1)}, u32[]{:S(2)}) copy-start(bf16[256,1024]{1,0:T(8,128)(2,1)S(1)} %collective-permute-done.4.refs_5_) | copy-start | bytes 1572868
  56.9 7.2 %collective-permute-start.6 = (bf16[128,1024]{1,0:T(8,128)(2,1)S(1)}, bf16[128,1024]{1,0:T(8,128)(2,1)S(1)}, u32[]{:S(2)}, u32[]{:S(2)}) collective-permute-start(bf16[128,1024]{1,0:T(8,128)(2,1)S(1)} %slice.40), channel_id=1, source_target_pairs={{0,4},{1,5},{4,8},{5,9},{8,12},{9,13},{12,14},{13,15},{14,10},{15,... | collective-permute-start | bytes 786440 | tf_op jit(solution)/shard_map/ppermute | solution.py:366
  65.0 1.8 %collective-permute-start.9 = (bf16[3,256,256]{2,1,0:T(8,128)(2,1)S(1)}, bf16[3,256,256]{2,1,0:T(8,128)(2,1)S(1)}, u32[]{:S(2)}, u32[]{:S(2)}) collective-permute-start(bf16[3,256,256]{2,1,0:T(8,128)(2,1)S(1)} %pad_maximum_fusion.1.refs_1_), channel_id=1, source_target_pairs={{0,1},{1,0},{2,3},{3,2},{4,5},{5,4},{6,7},{7,6},{8,9},{9,8},{10,11... | collective-permute-start | bytes 1179656 | tf_op jit(solution)/shard_map/ppermute | solution.py:372
  88.6 2.9 %collective-permute-start.11 = (bf16[8,256,256]{2,1,0:T(8,128)(2,1)}, bf16[8,256,256]{2,1,0:T(8,128)(2,1)S(1)}, u32[]{:S(2)}, u32[]{:S(2)}) collective-permute-start(bf16[8,256,256]{2,1,0:T(8,128)(2,1)} %get-tuple-element.17), channel_id=1, source_target_pairs={{0,1},{1,0},{2,3},{3,2},{4,5},{5,4},{6,7},{7,6},{8,9},{9,8},{10,11... | collective-permute-start | bytes 3145736 | tf_op jit(solution)/shard_map/ppermute | solution.py:372
  91.5 7.2 %copy-start.19 = (s32[2,8]{1,0:T(2,128)S(1)}, s32[2,8]{1,0:T(2,128)}, u32[]{:S(2)}) copy-start(s32[2,8]{1,0:T(2,128)} %dynamic-slice_bitcast_fusion.ids) | copy-start | bytes 196
  94.0 39.0 %all-to-all-start.1 = ((bf16[8,256,256]{2,1,0:T(8,128)(2,1)}), bf16[8,256,256]{2,1,0:T(8,128)(2,1)S(1)}, u32[]{:S(2)}, u32[]{:S(2)}) async-start(bf16[8,256,256]{2,1,0:T(8,128)(2,1)} %add_convert_fusion.grads), calls=%async_computation.1 | async-start | bytes 2097152 | tf_op jit(solution)/shard_map/all_to_all | solution.py:381
  103.9 29.1 %copy-start.17 = (f32[1024]{0:T(1024)S(1)}, f32[1024]{0:T(1024)}, u32[]{:S(2)}) copy-start(f32[1024]{0:T(1024)} %param.10) | copy-start | bytes 12292
  107.1 1.6 %collective-permute-start.12 = (bf16[8,64,256]{2,1,0:T(8,128)(2,1)S(1)}, bf16[8,64,256]{2,1,0:T(8,128)(2,1)S(1)}, u32[]{:S(2)}, u32[]{:S(2)}) collective-permute-start(bf16[8,64,256]{2,1,0:T(8,128)(2,1)S(1)} %get-tuple-element.19), channel_id=1, source_target_pairs={{0,1},{1,0},{2,3},{3,2},{4,5},{5,4},{6,7},{7,6},{8,9},{9,8},{10,11... | collective-permute-start | bytes 786440 | tf_op jit(solution)/shard_map/ppermute | solution.py:372
  109.5 8.9 %collective-permute-start.19 = (bf16[64,256]{1,0:T(8,128)(2,1)S(1)}, bf16[64,256]{1,0:T(8,128)(2,1)S(1)}, u32[]{:S(2)}, u32[]{:S(2)}) collective-permute-start(bf16[64,256]{1,0:T(8,128)(2,1)S(1)} %get-tuple-element.24), channel_id=1, source_target_pairs={{0,14},{1,15},{2,0},{3,1},{4,2},{5,3},{6,4},{7,5},{8,6},{9,7},{10,... | collective-permute-start | bytes 98312 | tf_op jit(solution)/shard_map/ppermute | solution.py:378
  114.2 5.5 %collective-permute-start.18 = (bf16[64,256]{1,0:T(8,128)(2,1)S(1)}, bf16[64,256]{1,0:T(8,128)(2,1)S(1)}, u32[]{:S(2)}, u32[]{:S(2)}) collective-permute-start(bf16[64,256]{1,0:T(8,128)(2,1)S(1)} %get-tuple-element.25), channel_id=1, source_target_pairs={{0,12},{1,13},{2,14},{3,15},{4,0},{5,1},{6,2},{7,3},{8,4},{9,5},{1... | collective-permute-start | bytes 98312 | tf_op jit(solution)/shard_map/ppermute | solution.py:378
  114.7 16.7 %collective-permute-start.17 = (bf16[64,256]{1,0:T(8,128)(2,1)}, bf16[64,256]{1,0:T(8,128)(2,1)S(1)}, u32[]{:S(2)}, u32[]{:S(2)}) collective-permute-start(bf16[64,256]{1,0:T(8,128)(2,1)} %get-tuple-element.26), channel_id=1, source_target_pairs={{0,10},{1,11},{2,12},{3,13},{4,14},{5,15},{6,0},{7,1},{8,2},{9,3},... | collective-permute-start | bytes 98312 | tf_op jit(solution)/shard_map/ppermute | solution.py:378
  114.7 16.7 %collective-permute-start.16 = (bf16[64,256]{1,0:T(8,128)(2,1)}, bf16[64,256]{1,0:T(8,128)(2,1)S(1)}, u32[]{:S(2)}, u32[]{:S(2)}) collective-permute-start(bf16[64,256]{1,0:T(8,128)(2,1)} %get-tuple-element.27), channel_id=1, source_target_pairs={{0,8},{1,9},{2,10},{3,11},{4,12},{5,13},{6,14},{7,15},{8,0},{9,1},... | collective-permute-start | bytes 98312 | tf_op jit(solution)/shard_map/ppermute | solution.py:378
  117.7 13.8 %collective-permute-start.15 = (bf16[64,256]{1,0:T(8,128)(2,1)S(1)}, bf16[64,256]{1,0:T(8,128)(2,1)S(1)}, u32[]{:S(2)}, u32[]{:S(2)}) collective-permute-start(bf16[64,256]{1,0:T(8,128)(2,1)S(1)} %get-tuple-element.28), channel_id=1, source_target_pairs={{0,6},{1,7},{2,8},{3,9},{4,10},{5,11},{6,12},{7,13},{8,14},{9,15},... | collective-permute-start | bytes 98312 | tf_op jit(solution)/shard_map/ppermute | solution.py:378
  118.4 13.1 %collective-permute-start.14 = (bf16[64,256]{1,0:T(8,128)(2,1)S(1)}, bf16[64,256]{1,0:T(8,128)(2,1)S(1)}, u32[]{:S(2)}, u32[]{:S(2)}) collective-permute-start(bf16[64,256]{1,0:T(8,128)(2,1)S(1)} %get-tuple-element.29), channel_id=1, source_target_pairs={{0,4},{1,5},{2,6},{3,7},{4,8},{5,9},{6,10},{7,11},{8,12},{9,13},{1... | collective-permute-start | bytes 98312 | tf_op jit(solution)/shard_map/ppermute | solution.py:378
  119.7 13.3 %collective-permute-start.13 = (bf16[64,256]{1,0:T(8,128)(2,1)S(1)}, bf16[64,256]{1,0:T(8,128)(2,1)S(1)}, u32[]{:S(2)}, u32[]{:S(2)}) collective-permute-start(bf16[64,256]{1,0:T(8,128)(2,1)S(1)} %get-tuple-element.30), channel_id=1, source_target_pairs={{0,2},{1,3},{2,4},{3,5},{4,6},{5,7},{6,8},{7,9},{8,10},{9,11},{10,... | collective-permute-start | bytes 98312 | tf_op jit(solution)/shard_map/ppermute | solution.py:378
  (16 other events, 17.0 us)

commit v4 on v3

--- a/solution.py
+++ b/solution.py
@@ -14,10 +14,12 @@
 F32 = jnp.float32
 BF16 = jnp.bfloat16
 TILE = 8
+PITCH = 9
 NN = (((1,), (0,)), ((), ()))
 NT = (((1,), (1,)), ((), ()))
 TN = (((0,), (0,)), ((), ()))
-VMEM_BYTES = 60 * 1024 * 1024
+LANE_BYTES = 3 * 1024 * 1024
+LARGE_VMEM_BYTES = 60 * 1024 * 1024
 SMALL_VMEM_BYTES = 24 * 1024 * 1024
 SHARDS, LANES = 0, 1
 
@@ -27,7 +29,7 @@
 
 
 def every(lead, size):
-    return pl.ds(lead, size, stride=TILE)
+    return pl.ds(lead, size, stride=PITCH)
 
 
 def attention_kernel(per, parts, blocks, rounds, pieces, ids, order, *refs):
@@ -38,7 +40,7 @@
     table, picked, packed, log_sums, keys, values, queries, dq, dk, dv, halo = refs[2 * per :]
     chips, size, width = out_refs[0].shape
     head_dim = width // 2
-    total = table.shape[0] // TILE
+    total = table.shape[0] // PITCH
     block_total = total // BLOCK
     sum_rows = size // head_dim
     lo_start = rounds * sum_rows
@@ -49,14 +51,14 @@
         n = 0
         for ref in qv_refs[m]:
             for row in range(ref.shape[0]):
-                base = (ids[SHARDS, n] * per + ids[LANES, m]) * (size * TILE)
+                base = (ids[SHARDS, n] * per + ids[LANES, m]) * (size * PITCH)
                 table[every(base, size), :] = ref[row, :, :head_dim].astype(F32)
                 table[every(base + 1, size), :] = ref[row, :, head_dim:].astype(F32)
                 n += 1
 
         def fill(n, carry):
             device = n * per + ids[LANES, m]
-            base = device * (size * TILE)
+            base = device * (size * PITCH)
             table[every(base + 2, size), :] = cot_refs[m][n, :size, :].astype(F32)
             if parts > 1:
                 zero = jnp.zeros((size, head_dim), F32)
@@ -75,7 +77,7 @@
     def rows_of(block):
         start = lax.rem(block, block_total) * BLOCK
         for p in range(BLOCK):
-            yield p * TILE, pl.multiple_of(order[start + p] * TILE, TILE)
+            yield p * PITCH, order[start + p]
 
     def gather(block, slot):
         for place, row in rows_of(block):
@@ -117,22 +119,23 @@
         query = queries[cur].astype(BF16)
         key_a, key_b = keys[prev], keys[cur]
         w_a = jnp.exp(dot(key_a, query, NT) - log_sum)
+        p_a = w_a * dot(values[prev], cot, NT)
         w_b = jnp.where(diagonal, 0.0, jnp.exp(dot(key_b, query, NT) - log_sum))
-        dw_a = dot(values[prev], cot, NT)
-        dw_b = dot(values[cur], cot, NT)
-        delta = jnp.sum(w_a * dw_a + w_b * dw_b, axis=0, keepdims=True)
-        ds_a = (w_a * (dw_a - delta)).astype(BF16)
-        ds_b = (w_b * (dw_b - delta)).astype(BF16)
-        dv_a = dot(w_a.astype(BF16), cot, NN)
+        p_b = w_b * dot(values[cur], cot, NT)
+        delta = jnp.sum(p_a + p_b, axis=0, keepdims=True)
+        w_a, w_b = w_a.astype(BF16), w_b.astype(BF16)
+        dv_a = dot(w_a, cot, NN)
+        dv[cur] = dot(w_b, cot, NN)
+        ds_a = (p_a - w_a.astype(F32) * delta).astype(BF16)
+        ds_b = (p_b - w_b.astype(F32) * delta).astype(BF16)
         dk_a = dot(ds_a, query, NN)
         if first:
             halo[0] = dk_a
             halo[1] = dv_a
         else:
             finish(prev, queries[prev], dq[prev], dk[prev] + dk_a, dv[prev] + dv_a)
-        dv[cur] = dot(w_b.astype(BF16), cot, NN)
         dk[cur] = dot(ds_b, query, NN)
-        dq[cur] = (dot(key_a, ds_a, TN) + dot(key_b, ds_b, TN)).T
+        dq[cur] = dot(ds_a, key_a, TN) + dot(ds_b, key_b, TN)
 
     halo_block = first_block + block_total - 1
     gather(halo_block, 1)
@@ -164,7 +167,7 @@
     for m in range(per):
 
         def drain(n, carry):
-            base = (n * per + ids[LANES, m]) * (size * TILE)
+            base = (n * per + ids[LANES, m]) * (size * PITCH)
             out_refs[m][n, :, :head_dim] = table[every(base + 3, size), :].astype(BF16)
             out_refs[m][n, :, head_dim:] = table[every(base + 4, size), :].astype(BF16)
             return carry
@@ -187,9 +190,9 @@
         in_specs=[smem, smem] + [vmem] * len(flat),
         out_specs=[vmem] * per,
         scratch_shapes=[
-            pltpu.VMEM((total * TILE, head_dim), F32),
-            pltpu.VMEM((2, BLOCK * TILE, head_dim), F32),
-            pltpu.VMEM((2, BLOCK * TILE, head_dim), F32),
+            pltpu.VMEM((total * PITCH, head_dim), F32),
+            pltpu.VMEM((2, BLOCK * PITCH, head_dim), F32),
+            pltpu.VMEM((2, BLOCK * PITCH, head_dim), F32),
             pltpu.VMEM((total // BLOCK, TILE, head_dim), F32),
             pltpu.VMEM((2, BLOCK, head_dim), BF16),
             pltpu.VMEM((2, BLOCK, head_dim), BF16),
@@ -199,7 +202,7 @@
             pltpu.VMEM((2, BLOCK, head_dim), F32),
             pltpu.VMEM((3, BLOCK, head_dim), F32),
         ],
-        compiler_params=pltpu.CompilerParams(vmem_limit_bytes=VMEM_BYTES),
+        compiler_params=pltpu.CompilerParams(vmem_limit_bytes=total * PITCH * head_dim * 4 + (per + 3) * LANE_BYTES),
         name="attention",
     )(ids, order, *flat)
 
@@ -236,7 +239,7 @@
             jax.ShapeDtypeStruct(tokens.shape, BF16),
             jax.ShapeDtypeStruct((heads, size + extra, head_dim), BF16),
         ],
-        compiler_params=pltpu.CompilerParams(vmem_limit_bytes=SMALL_VMEM_BYTES),
+        compiler_params=pltpu.CompilerParams(vmem_limit_bytes=LARGE_VMEM_BYTES),
         name="prepare",
     )(tokens, gain, cot, log_sums)
 
@@ -247,10 +250,8 @@
     total = refs[count + per]
     chips, rows, _ = outs[0].shape
     grad_t = jnp.zeros((grads.shape[-1], shards[0].shape[-1]), F32)
-    n = 0
-    for shard in shards:
+    for n, shard in enumerate(shards):
         grad_t = grad_t + dot(grads[ids[SHARDS, n]], shard[...], TN)
-        n += 1
     total[...] = grad_t.T
     for m in range(per):
         for k in range(chips):
@@ -266,63 +267,73 @@
     return pl.pallas_call(
         partial(weight_grad_kernel, per, len(shards)),
         out_shape=[jax.ShapeDtypeStruct((chips, rows, both), BF16)] * per,
-        in_specs=[smem, vmem] + [vmem] * len(shards),
+        in_specs=[smem] + [vmem] * (1 + len(shards)),
         out_specs=[vmem] * per,
         scratch_shapes=[pltpu.VMEM((shards[0].shape[1], both), F32)],
-        compiler_params=pltpu.CompilerParams(vmem_limit_bytes=SMALL_VMEM_BYTES),
+        compiler_params=pltpu.CompilerParams(vmem_limit_bytes=LARGE_VMEM_BYTES),
         name="weight_grad",
     )(ids, grads, *shards)
 
 
-def home_kernel(scale_out, ids, grads, w_qk, w_v, tokens, gain, *refs):
-    heads = grads.shape[0]
-    d_rows = refs[:heads]
-    out, d_wqk, d_wv, d_gain = refs[heads:]
+def home_kernel(grads, w_qk, w_v, tokens, gain, out):
+    heads, _, both = grads.shape
+    head_dim = both // 2
+    total = jnp.zeros(tokens.shape, F32)
+    for k in range(heads):
+        columns = slice(k * head_dim, (k + 1) * head_dim)
+        weights = jnp.concatenate([w_qk[:, columns], w_v[:, columns]], axis=1)
+        total = total + dot(grads[k], weights, NT)
+    x = tokens[...].astype(F32)
+    scale = lax.rsqrt(jnp.mean(x * x, axis=-1, keepdims=True) + EPS)
+    scaled = total * gain[...]
+    inner = jnp.mean(x * scaled, axis=-1, keepdims=True)
+    out[...] = (scale * (scaled - x * (scale * scale * inner))).astype(BF16)
+
+
+def home(grads, w_qk, w_v, tokens, gain):
+    return pl.pallas_call(
+        home_kernel,
+        out_shape=jax.ShapeDtypeStruct(tokens.shape, BF16),
+        compiler_params=pltpu.CompilerParams(vmem_limit_bytes=SMALL_VMEM_BYTES),
+        name="home",
+    )(grads, w_qk, w_v, tokens, gain)
+
+
+def rows_kernel(scale_out, ids, qk_own, v_own, own_gain, *refs):
+    d_rows = refs[:-3]
+    d_wqk, d_wv, d_gain = refs[-3:]
+    heads = len(d_rows)
     rows, both = d_rows[0].shape
     head_dim = both // 2
-    total = jnp.zeros(tokens.shape, F32)
-    start = pl.multiple_of(ids[LANES, ids.shape[1] - 1] * rows, rows)
-    gains = jnp.zeros((rows, 1), F32)
-    for head in range(heads):
-        columns = slice(head * head_dim, (head + 1) * head_dim)
-        weights = jnp.concatenate([w_qk[:, columns], w_v[:, columns]], axis=1)
-        total = total + dot(grads[head], weights, NT)
-        k = head
+    gains = jnp.zeros((rows, head_dim), F32)
+    for k in range(heads):
         source = lax.rem(ids[SHARDS, 0] + heads - k, heads)
         columns = pl.ds(pl.multiple_of(source * head_dim, head_dim), head_dim)
         qk_rows = d_rows[k][:, :head_dim].astype(F32) * scale_out
         v_rows = d_rows[k][:, head_dim:].astype(F32) * scale_out
         d_wqk[:, columns] = qk_rows
         d_wv[:, columns] = v_rows
-        own = qk_rows * w_qk[pl.ds(start, rows), columns].astype(F32)
-        own = own + v_rows * w_v[pl.ds(start, rows), columns].astype(F32)
-        gains = gains + jnp.sum(own, axis=1, keepdims=True)
-    d_gain[...] = gains
-    x = tokens[...].astype(F32)
-    scale = lax.rsqrt(jnp.mean(x * x, axis=-1, keepdims=True) + EPS)
-    scaled = total * gain[...]
-    inner = jnp.mean(x * scaled, axis=-1, keepdims=True)
-    out[...] = (scale * (scaled - x * (scale * scale * inner))).astype(BF16)
-
-
-def home(scale_out, ids, grads, d_rows, w_qk, w_v, tokens, gain):
-    rows = d_rows[0].shape[0]
-    width = tokens.shape[1]
+        gains = gains + qk_rows * qk_own[:, columns].astype(F32)
+        gains = gains + v_rows * v_own[:, columns].astype(F32)
+    d_gain[...] = jnp.sum(gains.T, axis=0, keepdims=True) / own_gain[...]
+
+
+def weight_rows(scale_out, ids, d_rows, qk_own, v_own, own_gain):
+    rows, width = qk_own.shape
     smem = pl.BlockSpec(memory_space=pltpu.SMEM)
     vmem = pl.BlockSpec(memory_space=pltpu.VMEM)
     return pl.pallas_call(
-        partial(home_kernel, scale_out),
+        partial(rows_kernel, scale_out),
         out_shape=[
-            jax.ShapeDtypeStruct(tokens.shape, BF16),
             jax.ShapeDtypeStruct((rows, width), F32),
             jax.ShapeDtypeStruct((rows, width), F32),
-            jax.ShapeDtypeStruct((rows, 1), F32),
+            jax.ShapeDtypeStruct((1, rows), F32),
         ],
-        in_specs=[smem] + [vmem] * (5 + len(d_rows)),
-        out_specs=[vmem] * 4,
+        in_specs=[smem] + [vmem] * (3 + len(d_rows)),
+        out_specs=[vmem] * 3,
         compiler_params=pltpu.CompilerParams(vmem_limit_bytes=SMALL_VMEM_BYTES),
-        name="home",
-    )(ids, grads, w_qk, w_v, tokens, gain, *d_rows)
+        name="weight_rows",
+    )(ids, qk_own, v_own, own_gain, *d_rows)
 
 
 def tables(devices, per, rounds, ring, block_total):
@@ -383,7 +394,7 @@
     ids = lax.dynamic_index_in_dim(
         jnp.asarray(tables(devices, per, rounds, ring, total // BLOCK)), me, 0, keepdims=False
     )
-    my_order = lax.dynamic_index_in_dim(bucket_order, lane % rounds, 0, keepdims=False)
+    my_order = PITCH * lax.dynamic_index_in_dim(bucket_order, lane % rounds, 0, keepdims=False)
     gain_row = norm_gain[None, :]
     normal, chunks = prepare(tokens, gain_row, cotangent, log_sums)
 
@@ -403,13 +414,21 @@
 
     my_weights = jnp.concatenate([my_columns(w_qk), my_columns(w_v)], axis=1)
 
+    rows = width // devices
+    qk_own, v_own, own_gain = [
+        lax.dynamic_slice_in_dim(v, me * rows, rows, 0) for v in (w_qk, w_v, norm_gain)
+    ]
+    shards[0], ids, my_order, qk_own, v_own, own_gain = lax.optimization_barrier(
+        (shards[0], ids, my_order, qk_own, v_own, own_gain)
+    )
+
     def project(some):
         return jnp.stack(
             [jnp.dot(n, my_weights, preferred_element_type=F32).astype(BF16) for n in some]
         )
 
     early = chips - 3
-    qv = [project(shards[:early]), project(shards[early:])]
+    qv = [project(shards[:early]), project(shards[early:-1]), project(shards[-1:])]
     qv_all = [qv] + [[swap(x, shift) for x in qv] for shift in range(1, per)]
     cot_all = [cot] + [swap(cot, shift) for shift in range(1, per)]
     sent = attention(per, parts, rounds, ids, my_order, qv_all, cot_all)
@@ -417,20 +436,18 @@
     for shift in range(1, per):
         grads = grads + swap(sent[shift], per - shift).astype(F32)
     grads = grads.astype(BF16)
-
     inbound = exchange(grads)
-    rows = width // devices
     partials = weight_grad(per, rows, ids, grads, shards)
     mine = partials[0].astype(F32)
     for shift in range(1, per):
         mine = mine + swap(partials[shift], per - shift).astype(F32)
     mine = mine.astype(BF16)
     d_rows = [mine[0]] + [send(mine[k], k) for k in range(1, chips)]
-    d_tokens, d_wqk, d_wv, gains = home(
-        1.0 / math.sqrt(total), ids, inbound, d_rows, w_qk, w_v, tokens, gain_row
-    )
-    d_gain = gains[:, 0] / lax.dynamic_slice_in_dim(norm_gain, me * rows, rows, 0)
-    return d_tokens, d_gain, d_wqk, d_wv
+    d_tokens = home(inbound, w_qk, w_v, tokens, gain_row)
+    d_wqk, d_wv, d_gain = weight_rows(
+        1.0 / math.sqrt(total), ids, d_rows, qk_own, v_own, own_gain[None, :]
+    )
+    return d_tokens, d_gain.reshape(rows), d_wqk, d_wv
 
 
 def solution(mesh):

time: 140 us -> 129 us (0.921)
  local copies, waits for them, and re-layouts: 17.1 us -> 8.04 us
  waiting for transfers between devices: 32.6 us -> 36.6 us
  Pallas kernels: 28.3 us -> 24.4 us
    unnamed x53 -> x27, local copies, waits for them, and re-layouts: 12.8 us -> 2.7 us
    pallas_call x1, Pallas kernels: 21 us -> 13.2 us  [attention(): pl.pallas_call(partial(attention_kernel, per, parts, blocks, rounds, len(...]
    ppermute x7, waiting for transfers between devices: 2.31 us -> 5.98 us  [send(): return lax.ppermute(x, 'tok', route)]
    pallas_call x1, Pallas kernels: 3.22 us -> 4.8 us  [weight_grad(): pl.pallas_call(partial(weight_grad_kernel, per, len(shards)), out_shape=[...]
    pallas_call x1, Pallas kernels: 1.09 us -> 2.64 us  [prepare(): pl.pallas_call(prepare_kernel, out_shape=[jax.ShapeDtypeStruct(tokens.sha...]
    pallas_call x1 -> x2, Pallas kernels: 2.93 us -> 3.74 us  [the longest x1 2.28 us: home(): pl.pallas_call(home_kernel, out_shape=jax.ShapeDtypeStruct(tokens.shape,...]
    ppermute x5 -> x6, waiting for transfers between devices: 5 us -> 5.52 us  [swap(): return lax.ppermute(x, 'tok', route)]
  transfers between devices with their start and end apart: 22 -> 23, of which waited for: 11 -> 10; matrix products, arithmetic and copies ran while one was open for 11% -> 13% of each run, Pallas kernels for 2% -> 5%
where the time goes in v4:
time: 129 us; the launch traced here: 128 us
  starting transfers between devices  46.2 us (36%)
  waiting for transfers between devices  36.6 us (28%)
  Pallas kernels  24.4 us (19%)
  matrix products  10 us (8%)
  local copies, waits for them, and re-layouts  8.04 us (6%)
  other arithmetic  2.35 us (2%)
    ppermute x8, waiting for transfers between devices, hop(): return lax.ppermute(x, 'tok', route)  25.1 us
    ppermute x7, starting transfers between devices, send(): return lax.ppermute(x, 'tok', route)  20.7 us
    pallas_call x1, Pallas kernels, attention(): pl.pallas_call(partial(attention_kernel, per, parts, blocks, rounds, len(...  13.2 us
    ppermute x8, starting transfers between devices, hop(): return lax.ppermute(x, 'tok', route)  13 us
    all_to_all x2, starting transfers between devices, exchange(): return lax.all_to_all(x, 'tok', 0, 0, tiled=True, axis_index_groups=groups)  11.5 us
    dot_general x8, matrix products, project(): jnp.dot(n, my_weights, preferred_element_type=F32).astype(BF16)  10 us
    ppermute x7, waiting for transfers between devices, send(): return lax.ppermute(x, 'tok', route)  5.98 us
    ppermute x6, waiting for transfers between devices, swap(): return lax.ppermute(x, 'tok', route)  5.52 us
  transfers between devices with their start and end apart: 23, of which 10 were waited for; matrix products, arithmetic and copies ran while one was open for 13% of the time, Pallas kernels for 5%

profile of v4, /device:TPU:0, one launch (start us, length us, event | category | flops | bytes accessed | tf_op | source)
XLA Modules:
  0.0 128.5 jit_solution(7516763213643366600)
XLA Ops:
  0.7 2.6 %prepare.1 = (bf16[256,1024]{1,0:T(8,128)(2,1)}, bf16[8,272,128]{2,1,0:T(8,128)(2,1)}) custom-call(bf16[256,1024]{1,0:T(8,128)(2,1)} %tokens.3, f32[1,1024]{1,0:T(1,128)} %bitcast.57, bf16[256,1024]{1,0:T(8,128)(2,1)} %cot.1, f32[2,8,256]{2,1,0:T(8,128)} %log_sums.1), custom_call_target="tpu_custom_call" | custom-call | tf_op jit(solution)/shard_map/prepare/pallas_call | solution.py:236
  3.3 3.0 %collective-permute-start.1 = (bf16[256,1024]{1,0:T(8,128)(2,1)}, bf16[256,1024]{1,0:T(8,128)(2,1)}, u32[]{:S(2)}, u32[]{:S(2)}) collective-permute-start(bf16[256,1024]{1,0:T(8,128)(2,1)} %get-tuple-element.22.refs_0_), channel_id=1, source_target_pairs={{0,2},{1,3},{4,0},{5,1},{8,4},{9,5},{12,8},{13,9},{14,12},{15,13},... | collective-permute-start | bytes 1572872 | tf_op jit(solution)/shard_map/ppermute | solution.py:377
  6.3 6.3 %all-to-all-start = ((bf16[8,272,128]{2,1,0:T(8,128)(2,1)}), bf16[8,272,128]{2,1,0:T(8,128)(2,1)S(1)}, u32[]{:S(2)}, u32[]{:S(2)}) async-start(bf16[8,272,128]{2,1,0:T(8,128)(2,1)} %get-tuple-element.23), calls=%async_computation | async-start | bytes 1114112 | tf_op jit(solution)/shard_map/all_to_all | solution.py:392
  12.7 1.6 %constant_dynamic-slice_fusion.2 = (bf16[64,1024]{1,0:T(8,128)(2,1)S(1)}, bf16[64,1024]{1,0:T(8,128)(2,1)}) fusion(bf16[1024,1024]{1,0:T(8,128)(2,1)S(1)} %copy-done, s32[]{:T(128)S(6)} %select_n.36, bf16[1024,1024]{1,0:T(8,128)(2,1)} %w_qk.1), kind=kLoop, calls=%fused_computation.38 | loop fusion | bytes 524292 | tf_op jit(solution)/shard_map/dynamic_slice | solution.py:419
  15.3 4.7 %collective-permute-done.1.refs_2_ = bf16[256,1024]{1,0:T(8,128)(2,1)} collective-permute-done((bf16[256,1024]{1,0:T(8,128)(2,1)}, bf16[256,1024]{1,0:T(8,128)(2,1)}, u32[]{:S(2)}, u32[]{:S(2)}) %collective-permute-start.1) | collective-permute-done | bytes 524320 | tf_op jit(solution)/shard_map/ppermute | solution.py:377
  20.0 2.8 %collective-permute-start.3 = (bf16[256,1024]{1,0:T(8,128)(2,1)}, bf16[256,1024]{1,0:T(8,128)(2,1)}, u32[]{:S(2)}, u32[]{:S(2)}) collective-permute-start(bf16[256,1024]{1,0:T(8,128)(2,1)} %collective-permute-done.1.refs_2_), channel_id=1, source_target_pairs={{0,2},{1,3},{4,0},{5,1},{8,4},{9,5},{12,8},{13,9},{14,12},{15,13},... | collective-permute-start | bytes 1572872 | tf_op jit(solution)/shard_map/ppermute | solution.py:377
  23.9 1.3 %fusion.1 = bf16[5,256,256]{2,1,0:T(8,128)(2,1)S(1)} fusion(bf16[256,1024]{1,0:T(8,128)(2,1)} %get-tuple-element.22.refs_0_, bf16[1024,128]{1,0:T(8,128)(2,1)S(1)} %get-tuple-element.44, bf16[1024,128]{1,0:T(8,128)(2,1)S(1)} %get-tuple-element.45), kind=kOutput, calls=%fused_computation.10 | convolution fusion | flops 135331840 | bytes 1179648 | tf_op jit(solution)/shard_map/dot_general | solution.py:427
  25.2 1.3 %fusion.3 = bf16[5,256,256]{2,1,0:T(8,128)(2,1)S(1)} fusion(bf16[5,256,256]{2,1,0:T(8,128)(2,1)S(1)} %fusion.1, bf16[256,1024]{1,0:T(8,128)(2,1)} %collective-permute-done.refs_1_, bf16[1024,128]{1,0:T(8,128)(2,1)S(1)} %get-tuple-element.44, bf16[1024,128]{1,0:T(8,128)(2,1)S(1)} %get-tuple-element.45), kind=kOutput, calls=%fused_computation.12 | convolution fusion | flops 135331840 | bytes 1179648 | tf_op jit(solution)/shard_map/dot_general | solution.py:427
  26.6 12.2 %collective-permute-done.3.refs_4_ = bf16[256,1024]{1,0:T(8,128)(2,1)} collective-permute-done((bf16[256,1024]{1,0:T(8,128)(2,1)}, bf16[256,1024]{1,0:T(8,128)(2,1)}, u32[]{:S(2)}, u32[]{:S(2)}) %collective-permute-start.3) | collective-permute-done | bytes 524320 | tf_op jit(solution)/shard_map/ppermute | solution.py:377
  39.5 4.0 %collective-permute-start.4 = (bf16[256,1024]{1,0:T(8,128)(2,1)}, bf16[256,1024]{1,0:T(8,128)(2,1)}, u32[]{:S(2)}, u32[]{:S(2)}) collective-permute-start(bf16[256,1024]{1,0:T(8,128)(2,1)} %collective-permute-done.2.refs_3_), channel_id=1, source_target_pairs={{0,4},{1,5},{4,8},{5,9},{8,12},{9,13},{12,14},{13,15},{14,10},{15,... | collective-permute-start | bytes 1572872 | tf_op jit(solution)/shard_map/ppermute | solution.py:377
  43.5 1.3 %fusion.5 = bf16[5,256,256]{2,1,0:T(8,128)(2,1)S(1)} fusion(bf16[5,256,256]{2,1,0:T(8,128)(2,1)S(1)} %fusion.3, bf16[256,1024]{1,0:T(8,128)(2,1)} %collective-permute-done.1.refs_2_, bf16[1024,128]{1,0:T(8,128)(2,1)S(1)} %get-tuple-element.44, bf16[1024,128]{1,0:T(8,128)(2,1)S(1)} %get-tuple-element.45), kind=kOutput, calls=%fused_computation.14 | convolution fusion | flops 135331840 | bytes 1179648 | tf_op jit(solution)/shard_map/dot_general | solution.py:427
  45.0 1.5 %fusion.7 = bf16[5,256,256]{2,1,0:T(8,128)(2,1)S(1)} fusion(bf16[5,256,256]{2,1,0:T(8,128)(2,1)S(1)} %fusion.5, bf16[256,1024]{1,0:T(8,128)(2,1)} %collective-permute-done.2.refs_3_, bf16[1024,128]{1,0:T(8,128)(2,1)} %copy-done.8, bf16[1024,128]{1,0:T(8,128)(2,1)} %copy-done.10), kind=kOutput, calls=%fused_computation.16 | convolution fusion | flops 135331840 | bytes 1179648 | tf_op jit(solution)/shard_map/dot_general | solution.py:427
  46.5 1.5 %fusion.9.refs_0_ = bf16[5,256,256]{2,1,0:T(8,128)(2,1)S(1)} fusion(bf16[5,256,256]{2,1,0:T(8,128)(2,1)S(1)} %fusion.7, bf16[256,1024]{1,0:T(8,128)(2,1)} %collective-permute-done.3.refs_4_, bf16[1024,128]{1,0:T(8,128)(2,1)} %copy-done.8, bf16[1024,128]{1,0:T(8,128)(2,1)} %copy-done.10), kind=kOutput, calls=%fused_computation.18 | convolution fusion | flops 135331840 | bytes 1179648 | tf_op jit(solution)/shard_map/dot_general | solution.py:427
  48.5 6.3 %collective-permute-done.5.refs_6_ = bf16[256,1024]{1,0:T(8,128)(2,1)} collective-permute-done((bf16[256,1024]{1,0:T(8,128)(2,1)}, bf16[256,1024]{1,0:T(8,128)(2,1)}, u32[]{:S(2)}, u32[]{:S(2)}) %collective-permute-start.5) | collective-permute-done | bytes 524320 | tf_op jit(solution)/shard_map/ppermute | solution.py:377
  56.9 2.1 %collective-permute-start.6 = (bf16[128,1024]{1,0:T(8,128)(2,1)S(1)}, bf16[128,1024]{1,0:T(8,128)(2,1)S(1)}, u32[]{:S(2)}, u32[]{:S(2)}) collective-permute-start(bf16[128,1024]{1,0:T(8,128)(2,1)S(1)} %slice.40), channel_id=1, source_target_pairs={{0,4},{1,5},{4,8},{5,9},{8,12},{9,13},{12,14},{13,15},{14,10},{15,... | collective-permute-start | bytes 786440 | tf_op jit(solution)/shard_map/ppermute | solution.py:377
  58.9 1.3 %fusion.11 = bf16[1,256,256]{2,1,0:T(8,128)(2,1)S(1)} fusion(bf16[256,1024]{1,0:T(8,128)(2,1)} %collective-permute-done.5.refs_6_, bf16[1024,128]{1,0:T(8,128)(2,1)S(1)} %copy-done.9, bf16[1024,128]{1,0:T(8,128)(2,1)S(1)} %copy-done.11), kind=kOutput, calls=%fused_computation.20 | convolution fusion | flops 135331840 | bytes 1179648 | tf_op jit(solution)/shard_map/dot_general | solution.py:427
  60.3 1.3 %fusion.10 = bf16[1,256,256]{2,1,0:T(8,128)(2,1)S(1)} fusion(bf16[256,1024]{1,0:T(8,128)(2,1)} %collective-permute-done.4.refs_5_, bf16[1024,128]{1,0:T(8,128)(2,1)S(1)} %copy-done.9, bf16[1024,128]{1,0:T(8,128)(2,1)S(1)} %copy-done.11), kind=kOutput, calls=%fused_computation.19 | convolution fusion | flops 135331840 | bytes 1179648 | tf_op jit(solution)/shard_map/dot_general | solution.py:427
  61.7 1.9 %collective-permute-done.6 = bf16[128,1024]{1,0:T(8,128)(2,1)S(1)} collective-permute-done((bf16[128,1024]{1,0:T(8,128)(2,1)S(1)}, bf16[128,1024]{1,0:T(8,128)(2,1)S(1)}, u32[]{:S(2)}, u32[]{:S(2)}) %collective-permute-start.6) | collective-permute-done | bytes 262176 | tf_op jit(solution)/shard_map/ppermute | solution.py:377
  64.1 1.3 %collective-permute-done.10.refs_5_ = bf16[1,256,256]{2,1,0:T(8,128)(2,1)S(1)} collective-permute-done((bf16[1,256,256]{2,1,0:T(8,128)(2,1)S(1)}, bf16[1,256,256]{2,1,0:T(8,128)(2,1)S(1)}, u32[]{:S(2)}, u32[]{:S(2)}) %collective-permute-start.10) | collective-permute-done | bytes 131104 | tf_op jit(solution)/shard_map/ppermute | solution.py:383
  65.4 13.2 %attention.1 = (bf16[8,256,256]{2,1,0:T(8,128)(2,1)S(1)}, bf16[8,256,256]{2,1,0:T(8,128)(2,1)S(1)}) custom-call(s32[2,8]{1,0:T(2,128)S(1)} %fusion.13.ids, s32[4096]{0:T(1024)S(1)} %bitcast.56, bf16[5,256,256]{2,1,0:T(8,128)(2,1)S(1)} %fusion.9.refs_0_, bf16[2,256,256]{2,1,0:T(8,128)(2,1)S(1)} %pad_maximum_fusion.1.refs_1_, ...), custom_call_target="tpu_custom_call" | custom-call | tf_op jit(solution)/shard_map/attention/pallas_call | solution.py:187
  78.8 2.5 %collective-permute-done.12 = bf16[8,256,256]{2,1,0:T(8,128)(2,1)S(1)} collective-permute-done((bf16[8,256,256]{2,1,0:T(8,128)(2,1)S(1)}, bf16[8,256,256]{2,1,0:T(8,128)(2,1)S(1)}, u32[]{:S(2)}, u32[]{:S(2)}) %collective-permute-start.12) | collective-permute-done | bytes 1048608 | tf_op jit(solution)/shard_map/ppermute | solution.py:383
  82.6 5.2 %all-to-all-start.1 = ((bf16[8,256,256]{2,1,0:T(8,128)(2,1)}), bf16[8,256,256]{2,1,0:T(8,128)(2,1)S(1)}, u32[]{:S(2)}, u32[]{:S(2)}) async-start(bf16[8,256,256]{2,1,0:T(8,128)(2,1)} %add_convert_fusion.grads), calls=%async_computation.1 | async-start | bytes 2097152 | tf_op jit(solution)/shard_map/all_to_all | solution.py:392
  87.8 4.8 %weight_grad.1 = (bf16[8,64,256]{2,1,0:T(8,128)(2,1)}, bf16[8,64,256]{2,1,0:T(8,128)(2,1)}) custom-call(s32[2,8]{1,0:T(2,128)} %copy-done.5, bf16[8,256,256]{2,1,0:T(8,128)(2,1)} %add_convert_fusion.grads, bf16[256,1024]{1,0:T(8,128)(2,1)} %get-tuple-element.22.refs_0_, bf16[256,1024]{1,0:T(8,128)(2,1)} %collective-permute-done.refs_1_, ...), custom_call_target="tpu_custom_call" | custom-call | tf_op jit(solution)/shard_map/weight_grad/pallas_call | solution.py:267
  92.6 1.7 %collective-permute-done.13 = bf16[8,64,256]{2,1,0:T(8,128)(2,1)S(1)} collective-permute-done((bf16[8,64,256]{2,1,0:T(8,128)(2,1)}, bf16[8,64,256]{2,1,0:T(8,128)(2,1)S(1)}, u32[]{:S(2)}, u32[]{:S(2)}) %collective-permute-start.13) | collective-permute-done | bytes 262176 | tf_op jit(solution)/shard_map/ppermute | solution.py:383
  95.4 4.8 %collective-permute-start.20 = (bf16[64,256]{1,0:T(8,128)(2,1)S(1)}, bf16[64,256]{1,0:T(8,128)(2,1)S(1)}, u32[]{:S(2)}, u32[]{:S(2)}) collective-permute-start(bf16[64,256]{1,0:T(8,128)(2,1)S(1)} %get-tuple-element.34), channel_id=1, source_target_pairs={{0,14},{1,15},{2,0},{3,1},{4,2},{5,3},{6,4},{7,5},{8,6},{9,7},{10,... | collective-permute-start | bytes 98312 | tf_op jit(solution)/shard_map/ppermute | solution.py:389
  100.7 2.9 %collective-permute-start.17 = (bf16[64,256]{1,0:T(8,128)(2,1)S(1)}, bf16[64,256]{1,0:T(8,128)(2,1)S(1)}, u32[]{:S(2)}, u32[]{:S(2)}) collective-permute-start(bf16[64,256]{1,0:T(8,128)(2,1)S(1)} %get-tuple-element.37), channel_id=1, source_target_pairs={{0,8},{1,9},{2,10},{3,11},{4,12},{5,13},{6,14},{7,15},{8,0},{9,1},... | collective-permute-start | bytes 98312 | tf_op jit(solution)/shard_map/ppermute | solution.py:389
  103.7 3.7 %collective-permute-done.20.refs_7_ = bf16[64,256]{1,0:T(8,128)(2,1)S(1)} collective-permute-done((bf16[64,256]{1,0:T(8,128)(2,1)S(1)}, bf16[64,256]{1,0:T(8,128)(2,1)S(1)}, u32[]{:S(2)}, u32[]{:S(2)}) %collective-permute-start.20) | collective-permute-done | bytes 32800 | tf_op jit(solution)/shard_map/ppermute | solution.py:389
  108.1 12.4 %collective-permute-start.14 = (bf16[64,256]{1,0:T(8,128)(2,1)S(1)}, bf16[64,256]{1,0:T(8,128)(2,1)S(1)}, u32[]{:S(2)}, u32[]{:S(2)}) collective-permute-start(bf16[64,256]{1,0:T(8,128)(2,1)S(1)} %get-tuple-element.40), channel_id=1, source_target_pairs={{0,2},{1,3},{2,4},{3,5},{4,6},{5,7},{6,8},{7,9},{8,10},{9,11},{10,... | collective-permute-start | bytes 98312 | tf_op jit(solution)/shard_map/ppermute | solution.py:389
  120.5 1.6 %collective-permute-done.14.refs_1_ = bf16[64,256]{1,0:T(8,128)(2,1)S(1)} collective-permute-done((bf16[64,256]{1,0:T(8,128)(2,1)S(1)}, bf16[64,256]{1,0:T(8,128)(2,1)S(1)}, u32[]{:S(2)}, u32[]{:S(2)}) %collective-permute-start.14) | collective-permute-done | bytes 32800 | tf_op jit(solution)/shard_map/ppermute | solution.py:389
  122.1 1.5 %weight_rows.1 = (f32[64,1024]{1,0:T(8,128)}, f32[64,1024]{1,0:T(8,128)}, f32[1,64]{1,0:T(1,128)}) custom-call(s32[2,8]{1,0:T(2,128)S(1)} %copy-done.6, bf16[64,1024]{1,0:T(8,128)(2,1)S(1)} %copy-done.3, bf16[64,1024]{1,0:T(8,128)(2,1)S(1)} %get-tuple-element.27.v_own, f32[1,64]{1,0:T(1,128)S(1)} %bitcast.59, bf16[64,256]{1,0:T(8,128)(2,1)S(1)} %get-tuple-element.41.refs_0_, ...), custom_call_target="tpu_custom_call" | custom-call | tf_op jit(solution)/shard_map/weight_rows/pallas_call | solution.py:325
  123.6 1.6 %copy-done.1 = bf16[1024,1024]{1,0:T(8,128)(2,1)S(1)} copy-done((bf16[1024,1024]{1,0:T(8,128)(2,1)S(1)}, bf16[1024,1024]{1,0:T(8,128)(2,1)}, u32[]{:S(2)}) %copy-start.1) | copy-done | bytes 2097176
  126.2 2.3 %home.1 = bf16[256,1024]{1,0:T(8,128)(2,1)} custom-call(bf16[8,256,256]{2,1,0:T(8,128)(2,1)S(1)} %all-to-all-done.1.grads, bf16[1024,1024]{1,0:T(8,128)(2,1)S(1)} %copy-done.1, bf16[1024,1024]{1,0:T(8,128)(2,1)S(1)} %copy-done, bf16[256,1024]{1,0:T(8,128)(2,1)S(1)} %copy-done.2, f32[1,1024]{1,0:T(1,128)S(1)} %bitcast.58), custom_call_target="tpu_custom_call" | custom-call | tf_op jit(solution)/shard_map/home/pallas_call | solution.py:294
  (66 shorter events, 11.1 us)
Async XLA Ops:
  0.6 23.2 %copy-start.4 = (f32[1024]{0:T(1024)S(1)}, f32[1024]{0:T(1024)}, u32[]{:S(2)}) copy-start(f32[1024]{0:T(1024)} %param.10) | copy-start | bytes 12292
  3.3 16.7 %collective-permute-start.1 = (bf16[256,1024]{1,0:T(8,128)(2,1)}, bf16[256,1024]{1,0:T(8,128)(2,1)}, u32[]{:S(2)}, u32[]{:S(2)}) collective-permute-start(bf16[256,1024]{1,0:T(8,128)(2,1)} %get-tuple-element.22.refs_0_), channel_id=1, source_target_pairs={{0,2},{1,3},{4,0},{5,1},{8,4},{9,5},{12,8},{13,9},{14,12},{15,13},... | collective-permute-start | bytes 1572872 | tf_op jit(solution)/shard_map/ppermute | solution.py:377
  6.3 16.5 %collective-permute-start = (bf16[256,1024]{1,0:T(8,128)(2,1)}, bf16[256,1024]{1,0:T(8,128)(2,1)}, u32[]{:S(2)}, u32[]{:S(2)}) collective-permute-start(bf16[256,1024]{1,0:T(8,128)(2,1)} %get-tuple-element.22.refs_0_), channel_id=1, source_target_pairs={{0,4},{1,5},{4,8},{5,9},{8,12},{9,13},{12,14},{13,15},{14,10},{15,... | collective-permute-start | bytes 1572872 | tf_op jit(solution)/shard_map/ppermute | solution.py:377
  6.3 38.5 %all-to-all-start = ((bf16[8,272,128]{2,1,0:T(8,128)(2,1)}), bf16[8,272,128]{2,1,0:T(8,128)(2,1)S(1)}, u32[]{:S(2)}, u32[]{:S(2)}) async-start(bf16[8,272,128]{2,1,0:T(8,128)(2,1)} %get-tuple-element.23), calls=%async_computation | async-start | bytes 1114112 | tf_op jit(solution)/shard_map/all_to_all | solution.py:392
  15.3 28.2 %copy-start.8 = (bf16[1024,128]{1,0:T(8,128)(2,1)}, bf16[1024,128]{1,0:T(8,128)(2,1)S(1)}, u32[]{:S(2)}) copy-start(bf16[1024,128]{1,0:T(8,128)(2,1)S(1)} %get-tuple-element.44) | copy-start | bytes 786436
  15.3 28.2 %copy-start.10 = (bf16[1024,128]{1,0:T(8,128)(2,1)}, bf16[1024,128]{1,0:T(8,128)(2,1)S(1)}, u32[]{:S(2)}) copy-start(bf16[1024,128]{1,0:T(8,128)(2,1)S(1)} %get-tuple-element.45) | copy-start | bytes 786436
  20.0 18.8 %collective-permute-start.3 = (bf16[256,1024]{1,0:T(8,128)(2,1)}, bf16[256,1024]{1,0:T(8,128)(2,1)}, u32[]{:S(2)}, u32[]{:S(2)}) collective-permute-start(bf16[256,1024]{1,0:T(8,128)(2,1)} %collective-permute-done.1.refs_2_), channel_id=1, source_target_pairs={{0,2},{1,3},{4,0},{5,1},{8,4},{9,5},{12,8},{13,9},{14,12},{15,13},... | collective-permute-start | bytes 1572872 | tf_op jit(solution)/shard_map/ppermute | solution.py:377
  22.8 16.8 %collective-permute-start.2 = (bf16[256,1024]{1,0:T(8,128)(2,1)}, bf16[256,1024]{1,0:T(8,128)(2,1)}, u32[]{:S(2)}, u32[]{:S(2)}) collective-permute-start(bf16[256,1024]{1,0:T(8,128)(2,1)} %collective-permute-done.refs_1_), channel_id=1, source_target_pairs={{0,4},{1,5},{4,8},{5,9},{8,12},{9,13},{12,14},{13,15},{14,10},{15,... | collective-permute-start | bytes 1572872 | tf_op jit(solution)/shard_map/ppermute | solution.py:377
  23.8 41.6 %copy-start.5 = (s32[2,8]{1,0:T(2,128)}, s32[2,8]{1,0:T(2,128)S(1)}, u32[]{:S(2)}) copy-start(s32[2,8]{1,0:T(2,128)S(1)} %fusion.13.ids) | copy-start | bytes 196
  38.7 16.1 %collective-permute-start.5 = (bf16[256,1024]{1,0:T(8,128)(2,1)}, bf16[256,1024]{1,0:T(8,128)(2,1)}, u32[]{:S(2)}, u32[]{:S(2)}) collective-permute-start(bf16[256,1024]{1,0:T(8,128)(2,1)} %collective-permute-done.3.refs_4_), channel_id=1, source_target_pairs={{0,2},{1,3},{4,0},{5,1},{8,4},{9,5},{12,8},{13,9},{14,12},{15,13},... | collective-permute-start | bytes 1572872 | tf_op jit(solution)/shard_map/ppermute | solution.py:377
  39.5 16.3 %collective-permute-start.4 = (bf16[256,1024]{1,0:T(8,128)(2,1)}, bf16[256,1024]{1,0:T(8,128)(2,1)}, u32[]{:S(2)}, u32[]{:S(2)}) collective-permute-start(bf16[256,1024]{1,0:T(8,128)(2,1)} %collective-permute-done.2.refs_3_), channel_id=1, source_target_pairs={{0,4},{1,5},{4,8},{5,9},{8,12},{9,13},{12,14},{13,15},{14,10},{15,... | collective-permute-start | bytes 1572872 | tf_op jit(solution)/shard_map/ppermute | solution.py:377
  44.9 14.1 %copy-start.9 = (bf16[1024,128]{1,0:T(8,128)(2,1)S(1)}, bf16[1024,128]{1,0:T(8,128)(2,1)}, u32[]{:S(2)}) copy-start(bf16[1024,128]{1,0:T(8,128)(2,1)} %copy-done.8) | copy-start | bytes 786436
  44.9 14.1 %copy-start.11 = (bf16[1024,128]{1,0:T(8,128)(2,1)S(1)}, bf16[1024,128]{1,0:T(8,128)(2,1)}, u32[]{:S(2)}) copy-start(bf16[1024,128]{1,0:T(8,128)(2,1)} %copy-done.10) | copy-start | bytes 786436
  44.9 19.2 %collective-permute-start.11 = (bf16[8,272,128]{2,1,0:T(8,128)(2,1)S(1)}, bf16[8,272,128]{2,1,0:T(8,128)(2,1)S(1)}, u32[]{:S(2)}, u32[]{:S(2)}) collective-permute-start(bf16[8,272,128]{2,1,0:T(8,128)(2,1)S(1)} %all-to-all-done.refs_6_), channel_id=1, source_target_pairs={{0,1},{1,0},{2,3},{3,2},{4,5},{5,4},{6,7},{7,6},{8,9},{9,8},{10,11... | collective-permute-start | bytes 1671176 | tf_op jit(solution)/shard_map/ppermute | solution.py:383
  48.0 16.1 %collective-permute-start.8 = (bf16[5,256,256]{2,1,0:T(8,128)(2,1)S(1)}, bf16[5,256,256]{2,1,0:T(8,128)(2,1)S(1)}, u32[]{:S(2)}, u32[]{:S(2)}) collective-permute-start(bf16[5,256,256]{2,1,0:T(8,128)(2,1)S(1)} %fusion.9.refs_0_), channel_id=1, source_target_pairs={{0,1},{1,0},{2,3},{3,2},{4,5},{5,4},{6,7},{7,6},{8,9},{9,8},{10,11... | collective-permute-start | bytes 1966088 | tf_op jit(solution)/shard_map/ppermute | solution.py:383
  55.8 7.8 %collective-permute-start.7 = (bf16[128,1024]{1,0:T(8,128)(2,1)S(1)}, bf16[128,1024]{1,0:T(8,128)(2,1)S(1)}, u32[]{:S(2)}, u32[]{:S(2)}) collective-permute-start(bf16[128,1024]{1,0:T(8,128)(2,1)S(1)} %slice.41), channel_id=1, source_target_pairs={{0,2},{1,3},{4,0},{5,1},{8,4},{9,5},{12,8},{13,9},{14,12},{15,13},... | collective-permute-start | bytes 786440 | tf_op jit(solution)/shard_map/ppermute | solution.py:377
  56.9 6.7 %collective-permute-start.6 = (bf16[128,1024]{1,0:T(8,128)(2,1)S(1)}, bf16[128,1024]{1,0:T(8,128)(2,1)S(1)}, u32[]{:S(2)}, u32[]{:S(2)}) collective-permute-start(bf16[128,1024]{1,0:T(8,128)(2,1)S(1)} %slice.40), channel_id=1, source_target_pairs={{0,4},{1,5},{4,8},{5,9},{8,12},{9,13},{12,14},{13,15},{14,10},{15,... | collective-permute-start | bytes 786440 | tf_op jit(solution)/shard_map/ppermute | solution.py:377
  61.7 2.4 %collective-permute-start.9 = (bf16[2,256,256]{2,1,0:T(8,128)(2,1)S(1)}, bf16[2,256,256]{2,1,0:T(8,128)(2,1)S(1)}, u32[]{:S(2)}, u32[]{:S(2)}) collective-permute-start(bf16[2,256,256]{2,1,0:T(8,128)(2,1)S(1)} %pad_maximum_fusion.1.refs_1_), channel_id=1, source_target_pairs={{0,1},{1,0},{2,3},{3,2},{4,5},{5,4},{6,7},{7,6},{8,9},{9,8},{10,11... | collective-permute-start | bytes 786440 | tf_op jit(solution)/shard_map/ppermute | solution.py:383
  63.7 14.9 %copy-start.7 = (bf16[256,1024]{1,0:T(8,128)(2,1)}, bf16[256,1024]{1,0:T(8,128)(2,1)S(1)}, u32[]{:S(2)}) copy-start(bf16[256,1024]{1,0:T(8,128)(2,1)S(1)} %constant_dynamic-update-slice_fusion.refs_7_) | copy-start | bytes 1572868
  64.0 1.4 %collective-permute-start.10 = (bf16[1,256,256]{2,1,0:T(8,128)(2,1)S(1)}, bf16[1,256,256]{2,1,0:T(8,128)(2,1)S(1)}, u32[]{:S(2)}, u32[]{:S(2)}) collective-permute-start(bf16[1,256,256]{2,1,0:T(8,128)(2,1)S(1)} %fusion.12.refs_2_), channel_id=1, source_target_pairs={{0,1},{1,0},{2,3},{3,2},{4,5},{5,4},{6,7},{7,6},{8,9},{9,8},{10,11... | collective-permute-start | bytes 393224 | tf_op jit(solution)/shard_map/ppermute | solution.py:383
  78.6 2.7 %collective-permute-start.12 = (bf16[8,256,256]{2,1,0:T(8,128)(2,1)S(1)}, bf16[8,256,256]{2,1,0:T(8,128)(2,1)S(1)}, u32[]{:S(2)}, u32[]{:S(2)}) collective-permute-start(bf16[8,256,256]{2,1,0:T(8,128)(2,1)S(1)} %get-tuple-element.25), channel_id=1, source_target_pairs={{0,1},{1,0},{2,3},{3,2},{4,5},{5,4},{6,7},{7,6},{8,9},{9,8},{10,11... | collective-permute-start | bytes 3145736 | tf_op jit(solution)/shard_map/ppermute | solution.py:383
  82.6 41.0 %all-to-all-start.1 = ((bf16[8,256,256]{2,1,0:T(8,128)(2,1)}), bf16[8,256,256]{2,1,0:T(8,128)(2,1)S(1)}, u32[]{:S(2)}, u32[]{:S(2)}) async-start(bf16[8,256,256]{2,1,0:T(8,128)(2,1)} %add_convert_fusion.grads), calls=%async_computation.1 | async-start | bytes 2097152 | tf_op jit(solution)/shard_map/all_to_all | solution.py:392
  87.8 34.3 %copy-start.3 = (bf16[64,1024]{1,0:T(8,128)(2,1)S(1)}, bf16[64,1024]{1,0:T(8,128)(2,1)}, u32[]{:S(2)}) copy-start(bf16[64,1024]{1,0:T(8,128)(2,1)} %get-tuple-element.26.qk_own) | copy-start | bytes 393220
  87.8 34.3 %copy-start.6 = (s32[2,8]{1,0:T(2,128)S(1)}, s32[2,8]{1,0:T(2,128)}, u32[]{:S(2)}) copy-start(s32[2,8]{1,0:T(2,128)} %copy-done.5) | copy-start | bytes 196
  92.6 1.7 %collective-permute-start.13 = (bf16[8,64,256]{2,1,0:T(8,128)(2,1)}, bf16[8,64,256]{2,1,0:T(8,128)(2,1)S(1)}, u32[]{:S(2)}, u32[]{:S(2)}) collective-permute-start(bf16[8,64,256]{2,1,0:T(8,128)(2,1)} %get-tuple-element.30), channel_id=1, source_target_pairs={{0,1},{1,0},{2,3},{3,2},{4,5},{5,4},{6,7},{7,6},{8,9},{9,8},{10,11... | collective-permute-start | bytes 786440 | tf_op jit(solution)/shard_map/ppermute | solution.py:383
  95.4 11.9 %collective-permute-start.20 = (bf16[64,256]{1,0:T(8,128)(2,1)S(1)}, bf16[64,256]{1,0:T(8,128)(2,1)S(1)}, u32[]{:S(2)}, u32[]{:S(2)}) collective-permute-start(bf16[64,256]{1,0:T(8,128)(2,1)S(1)} %get-tuple-element.34), channel_id=1, source_target_pairs={{0,14},{1,15},{2,0},{3,1},{4,2},{5,3},{6,4},{7,5},{8,6},{9,7},{10,... | collective-permute-start | bytes 98312 | tf_op jit(solution)/shard_map/ppermute | solution.py:389
  100.2 7.9 %collective-permute-start.19 = (bf16[64,256]{1,0:T(8,128)(2,1)S(1)}, bf16[64,256]{1,0:T(8,128)(2,1)S(1)}, u32[]{:S(2)}, u32[]{:S(2)}) collective-permute-start(bf16[64,256]{1,0:T(8,128)(2,1)S(1)} %get-tuple-element.35), channel_id=1, source_target_pairs={{0,12},{1,13},{2,14},{3,15},{4,0},{5,1},{6,2},{7,3},{8,4},{9,5},{1... | collective-permute-start | bytes 98312 | tf_op jit(solution)/shard_map/ppermute | solution.py:389
  100.7 19.8 %collective-permute-start.18 = (bf16[64,256]{1,0:T(8,128)(2,1)S(1)}, bf16[64,256]{1,0:T(8,128)(2,1)S(1)}, u32[]{:S(2)}, u32[]{:S(2)}) collective-permute-start(bf16[64,256]{1,0:T(8,128)(2,1)S(1)} %get-tuple-element.36), channel_id=1, source_target_pairs={{0,10},{1,11},{2,12},{3,13},{4,14},{5,15},{6,0},{7,1},{8,2},{9,3},... | collective-permute-start | bytes 98312 | tf_op jit(solution)/shard_map/ppermute | solution.py:389
  100.7 19.8 %collective-permute-start.17 = (bf16[64,256]{1,0:T(8,128)(2,1)S(1)}, bf16[64,256]{1,0:T(8,128)(2,1)S(1)}, u32[]{:S(2)}, u32[]{:S(2)}) collective-permute-start(bf16[64,256]{1,0:T(8,128)(2,1)S(1)} %get-tuple-element.37), channel_id=1, source_target_pairs={{0,8},{1,9},{2,10},{3,11},{4,12},{5,13},{6,14},{7,15},{8,0},{9,1},... | collective-permute-start | bytes 98312 | tf_op jit(solution)/shard_map/ppermute | solution.py:389
  103.7 16.8 %collective-permute-start.16 = (bf16[64,256]{1,0:T(8,128)(2,1)S(1)}, bf16[64,256]{1,0:T(8,128)(2,1)S(1)}, u32[]{:S(2)}, u32[]{:S(2)}) collective-permute-start(bf16[64,256]{1,0:T(8,128)(2,1)S(1)} %get-tuple-element.38), channel_id=1, source_target_pairs={{0,6},{1,7},{2,8},{3,9},{4,10},{5,11},{6,12},{7,13},{8,14},{9,15},... | collective-permute-start | bytes 98312 | tf_op jit(solution)/shard_map/ppermute | solution.py:389
  107.4 13.1 %collective-permute-start.15 = (bf16[64,256]{1,0:T(8,128)(2,1)S(1)}, bf16[64,256]{1,0:T(8,128)(2,1)S(1)}, u32[]{:S(2)}, u32[]{:S(2)}) collective-permute-start(bf16[64,256]{1,0:T(8,128)(2,1)S(1)} %get-tuple-element.39), channel_id=1, source_target_pairs={{0,4},{1,5},{2,6},{3,7},{4,8},{5,9},{6,10},{7,11},{8,12},{9,13},{1... | collective-permute-start | bytes 98312 | tf_op jit(solution)/shard_map/ppermute | solution.py:389
  108.1 14.0 %collective-permute-start.14 = (bf16[64,256]{1,0:T(8,128)(2,1)S(1)}, bf16[64,256]{1,0:T(8,128)(2,1)S(1)}, u32[]{:S(2)}, u32[]{:S(2)}) collective-permute-start(bf16[64,256]{1,0:T(8,128)(2,1)S(1)} %get-tuple-element.40), channel_id=1, source_target_pairs={{0,2},{1,3},{2,4},{3,5},{4,6},{5,7},{6,8},{7,9},{8,10},{9,11},{10,... | collective-permute-start | bytes 98312 | tf_op jit(solution)/shard_map/ppermute | solution.py:389
  (4 other events, 26.6 us)

commit v5 on v4

--- a/solution.py
+++ b/solution.py
@@ -444,6 +444,7 @@
     mine = mine.astype(BF16)
     d_rows = [mine[0]] + [send(mine[k], k) for k in range(1, chips)]
     d_tokens = home(inbound, w_qk, w_v, tokens, gain_row)
+    *d_rows, d_tokens = lax.optimization_barrier((*d_rows, d_tokens))
     d_wqk, d_wv, d_gain = weight_rows(
         1.0 / math.sqrt(total), ids, d_rows, qk_own, v_own, own_gain[None, :]
     )

time: 129 us -> 128 us (level)
  waiting for transfers between devices: 36.6 us -> 34.5 us
    ppermute x7, waiting for transfers between devices: 5.98 us -> 3.82 us  [send(): return lax.ppermute(x, 'tok', route)]
  transfers between devices with their start and end apart: 23 -> 23, of which waited for: 10 -> 9; matrix products, arithmetic and copies ran while one was open for 13% -> 13% of each run, Pallas kernels for 5% -> 6%
where the time goes in v5:
time: 128 us; the launch traced here: 127 us
  starting transfers between devices  46.1 us (36%)
  waiting for transfers between devices  34.5 us (27%)
  Pallas kernels  24.6 us (19%)
  matrix products  10 us (8%)
  local copies, waits for them, and re-layouts  8.68 us (7%)
  other arithmetic  2.35 us (2%)
    ppermute x8, waiting for transfers between devices, hop(): return lax.ppermute(x, 'tok', route)  25.1 us
    ppermute x7, starting transfers between devices, send(): return lax.ppermute(x, 'tok', route)  20.7 us
    pallas_call x1, Pallas kernels, attention(): pl.pallas_call(partial(attention_kernel, per, parts, blocks, rounds, len(...  13.2 us
    ppermute x8, starting transfers between devices, hop(): return lax.ppermute(x, 'tok', route)  13 us
    all_to_all x2, starting transfers between devices, exchange(): return lax.all_to_all(x, 'tok', 0, 0, tiled=True, axis_index_groups=groups)  11.5 us
    dot_general x8, matrix products, project(): jnp.dot(n, my_weights, preferred_element_type=F32).astype(BF16)  10 us
    ppermute x6, waiting for transfers between devices, swap(): return lax.ppermute(x, 'tok', route)  5.57 us
    pallas_call x1, Pallas kernels, weight_grad(): pl.pallas_call(partial(weight_grad_kernel, per, len(shards)), out_shape=[...  4.76 us
  transfers between devices with their start and end apart: 23, of which 9 were waited for; matrix products, arithmetic and copies ran while one was open for 13% of the time, Pallas kernels for 6%

profile of v5, /device:TPU:0, one launch (start us, length us, event | category | flops | bytes accessed | tf_op | source)
XLA Modules:
  0.0 127.2 jit_solution(712750285260496664)
XLA Ops:
  0.7 2.6 %prepare.1 = (bf16[256,1024]{1,0:T(8,128)(2,1)}, bf16[8,272,128]{2,1,0:T(8,128)(2,1)}) custom-call(bf16[256,1024]{1,0:T(8,128)(2,1)} %tokens.3, f32[1,1024]{1,0:T(1,128)} %bitcast.57, bf16[256,1024]{1,0:T(8,128)(2,1)} %cot.1, f32[2,8,256]{2,1,0:T(8,128)} %log_sums.1), custom_call_target="tpu_custom_call" | custom-call | tf_op jit(solution)/shard_map/prepare/pallas_call | solution.py:236
  3.3 3.0 %collective-permute-start.1 = (bf16[256,1024]{1,0:T(8,128)(2,1)}, bf16[256,1024]{1,0:T(8,128)(2,1)}, u32[]{:S(2)}, u32[]{:S(2)}) collective-permute-start(bf16[256,1024]{1,0:T(8,128)(2,1)} %get-tuple-element.31.refs_0_), channel_id=1, source_target_pairs={{0,2},{1,3},{4,0},{5,1},{8,4},{9,5},{12,8},{13,9},{14,12},{15,13},... | collective-permute-start | bytes 1572872 | tf_op jit(solution)/shard_map/ppermute | solution.py:377
  6.3 6.3 %all-to-all-start = ((bf16[8,272,128]{2,1,0:T(8,128)(2,1)}), bf16[8,272,128]{2,1,0:T(8,128)(2,1)S(1)}, u32[]{:S(2)}, u32[]{:S(2)}) async-start(bf16[8,272,128]{2,1,0:T(8,128)(2,1)} %get-tuple-element.32), calls=%async_computation | async-start | bytes 1114112 | tf_op jit(solution)/shard_map/all_to_all | solution.py:392
  12.7 1.6 %constant_dynamic-slice_fusion.2 = (bf16[64,1024]{1,0:T(8,128)(2,1)S(1)}, bf16[64,1024]{1,0:T(8,128)(2,1)}) fusion(bf16[1024,1024]{1,0:T(8,128)(2,1)S(1)} %copy-done, s32[]{:T(128)S(6)} %select_n.36, bf16[1024,1024]{1,0:T(8,128)(2,1)} %w_qk.1), kind=kLoop, calls=%fused_computation.38 | loop fusion | bytes 524292 | tf_op jit(solution)/shard_map/dynamic_slice | solution.py:419
  15.3 4.7 %collective-permute-done.1.refs_2_ = bf16[256,1024]{1,0:T(8,128)(2,1)} collective-permute-done((bf16[256,1024]{1,0:T(8,128)(2,1)}, bf16[256,1024]{1,0:T(8,128)(2,1)}, u32[]{:S(2)}, u32[]{:S(2)}) %collective-permute-start.1) | collective-permute-done | bytes 524320 | tf_op jit(solution)/shard_map/ppermute | solution.py:377
  20.0 2.8 %collective-permute-start.3 = (bf16[256,1024]{1,0:T(8,128)(2,1)}, bf16[256,1024]{1,0:T(8,128)(2,1)}, u32[]{:S(2)}, u32[]{:S(2)}) collective-permute-start(bf16[256,1024]{1,0:T(8,128)(2,1)} %collective-permute-done.1.refs_2_), channel_id=1, source_target_pairs={{0,2},{1,3},{4,0},{5,1},{8,4},{9,5},{12,8},{13,9},{14,12},{15,13},... | collective-permute-start | bytes 1572872 | tf_op jit(solution)/shard_map/ppermute | solution.py:377
  23.9 1.3 %fusion.1 = bf16[5,256,256]{2,1,0:T(8,128)(2,1)S(1)} fusion(bf16[256,1024]{1,0:T(8,128)(2,1)} %get-tuple-element.31.refs_0_, bf16[1024,128]{1,0:T(8,128)(2,1)S(1)} %get-tuple-element.62, bf16[1024,128]{1,0:T(8,128)(2,1)S(1)} %get-tuple-element.63), kind=kOutput, calls=%fused_computation.10 | convolution fusion | flops 135331840 | bytes 1179648 | tf_op jit(solution)/shard_map/dot_general | solution.py:427
  25.2 1.3 %fusion.3 = bf16[5,256,256]{2,1,0:T(8,128)(2,1)S(1)} fusion(bf16[5,256,256]{2,1,0:T(8,128)(2,1)S(1)} %fusion.1, bf16[256,1024]{1,0:T(8,128)(2,1)} %collective-permute-done.refs_1_, bf16[1024,128]{1,0:T(8,128)(2,1)S(1)} %get-tuple-element.62, bf16[1024,128]{1,0:T(8,128)(2,1)S(1)} %get-tuple-element.63), kind=kOutput, calls=%fused_computation.12 | convolution fusion | flops 135331840 | bytes 1179648 | tf_op jit(solution)/shard_map/dot_general | solution.py:427
  26.6 12.2 %collective-permute-done.3.refs_4_ = bf16[256,1024]{1,0:T(8,128)(2,1)} collective-permute-done((bf16[256,1024]{1,0:T(8,128)(2,1)}, bf16[256,1024]{1,0:T(8,128)(2,1)}, u32[]{:S(2)}, u32[]{:S(2)}) %collective-permute-start.3) | collective-permute-done | bytes 524320 | tf_op jit(solution)/shard_map/ppermute | solution.py:377
  39.5 4.0 %collective-permute-start.4 = (bf16[256,1024]{1,0:T(8,128)(2,1)}, bf16[256,1024]{1,0:T(8,128)(2,1)}, u32[]{:S(2)}, u32[]{:S(2)}) collective-permute-start(bf16[256,1024]{1,0:T(8,128)(2,1)} %collective-permute-done.2.refs_3_), channel_id=1, source_target_pairs={{0,4},{1,5},{4,8},{5,9},{8,12},{9,13},{12,14},{13,15},{14,10},{15,... | collective-permute-start | bytes 1572872 | tf_op jit(solution)/shard_map/ppermute | solution.py:377
  43.5 1.3 %fusion.5 = bf16[5,256,256]{2,1,0:T(8,128)(2,1)S(1)} fusion(bf16[5,256,256]{2,1,0:T(8,128)(2,1)S(1)} %fusion.3, bf16[256,1024]{1,0:T(8,128)(2,1)} %collective-permute-done.1.refs_2_, bf16[1024,128]{1,0:T(8,128)(2,1)S(1)} %get-tuple-element.62, bf16[1024,128]{1,0:T(8,128)(2,1)S(1)} %get-tuple-element.63), kind=kOutput, calls=%fused_computation.14 | convolution fusion | flops 135331840 | bytes 1179648 | tf_op jit(solution)/shard_map/dot_general | solution.py:427
  45.0 1.5 %fusion.7 = bf16[5,256,256]{2,1,0:T(8,128)(2,1)S(1)} fusion(bf16[5,256,256]{2,1,0:T(8,128)(2,1)S(1)} %fusion.5, bf16[256,1024]{1,0:T(8,128)(2,1)} %collective-permute-done.2.refs_3_, bf16[1024,128]{1,0:T(8,128)(2,1)} %copy-done.8, bf16[1024,128]{1,0:T(8,128)(2,1)} %copy-done.10), kind=kOutput, calls=%fused_computation.16 | convolution fusion | flops 135331840 | bytes 1179648 | tf_op jit(solution)/shard_map/dot_general | solution.py:427
  46.5 1.5 %fusion.9.refs_0_ = bf16[5,256,256]{2,1,0:T(8,128)(2,1)S(1)} fusion(bf16[5,256,256]{2,1,0:T(8,128)(2,1)S(1)} %fusion.7, bf16[256,1024]{1,0:T(8,128)(2,1)} %collective-permute-done.3.refs_4_, bf16[1024,128]{1,0:T(8,128)(2,1)} %copy-done.8, bf16[1024,128]{1,0:T(8,128)(2,1)} %copy-done.10), kind=kOutput, calls=%fused_computation.18 | convolution fusion | flops 135331840 | bytes 1179648 | tf_op jit(solution)/shard_map/dot_general | solution.py:427
  48.5 6.3 %collective-permute-done.5.refs_6_ = bf16[256,1024]{1,0:T(8,128)(2,1)} collective-permute-done((bf16[256,1024]{1,0:T(8,128)(2,1)}, bf16[256,1024]{1,0:T(8,128)(2,1)}, u32[]{:S(2)}, u32[]{:S(2)}) %collective-permute-start.5) | collective-permute-done | bytes 524320 | tf_op jit(solution)/shard_map/ppermute | solution.py:377
  56.9 2.1 %collective-permute-start.6 = (bf16[128,1024]{1,0:T(8,128)(2,1)S(1)}, bf16[128,1024]{1,0:T(8,128)(2,1)S(1)}, u32[]{:S(2)}, u32[]{:S(2)}) collective-permute-start(bf16[128,1024]{1,0:T(8,128)(2,1)S(1)} %slice.40), channel_id=1, source_target_pairs={{0,4},{1,5},{4,8},{5,9},{8,12},{9,13},{12,14},{13,15},{14,10},{15,... | collective-permute-start | bytes 786440 | tf_op jit(solution)/shard_map/ppermute | solution.py:377
  58.9 1.3 %fusion.11 = bf16[1,256,256]{2,1,0:T(8,128)(2,1)S(1)} fusion(bf16[256,1024]{1,0:T(8,128)(2,1)} %collective-permute-done.5.refs_6_, bf16[1024,128]{1,0:T(8,128)(2,1)S(1)} %copy-done.9, bf16[1024,128]{1,0:T(8,128)(2,1)S(1)} %copy-done.11), kind=kOutput, calls=%fused_computation.20 | convolution fusion | flops 135331840 | bytes 1179648 | tf_op jit(solution)/shard_map/dot_general | solution.py:427
  60.3 1.3 %fusion.10 = bf16[1,256,256]{2,1,0:T(8,128)(2,1)S(1)} fusion(bf16[256,1024]{1,0:T(8,128)(2,1)} %collective-permute-done.4.refs_5_, bf16[1024,128]{1,0:T(8,128)(2,1)S(1)} %copy-done.9, bf16[1024,128]{1,0:T(8,128)(2,1)S(1)} %copy-done.11), kind=kOutput, calls=%fused_computation.19 | convolution fusion | flops 135331840 | bytes 1179648 | tf_op jit(solution)/shard_map/dot_general | solution.py:427
  61.7 1.9 %collective-permute-done.6 = bf16[128,1024]{1,0:T(8,128)(2,1)S(1)} collective-permute-done((bf16[128,1024]{1,0:T(8,128)(2,1)S(1)}, bf16[128,1024]{1,0:T(8,128)(2,1)S(1)}, u32[]{:S(2)}, u32[]{:S(2)}) %collective-permute-start.6) | collective-permute-done | bytes 262176 | tf_op jit(solution)/shard_map/ppermute | solution.py:377
  64.1 1.3 %collective-permute-done.10.refs_5_ = bf16[1,256,256]{2,1,0:T(8,128)(2,1)S(1)} collective-permute-done((bf16[1,256,256]{2,1,0:T(8,128)(2,1)S(1)}, bf16[1,256,256]{2,1,0:T(8,128)(2,1)S(1)}, u32[]{:S(2)}, u32[]{:S(2)}) %collective-permute-start.10) | collective-permute-done | bytes 131104 | tf_op jit(solution)/shard_map/ppermute | solution.py:383
  65.4 13.2 %attention.1 = (bf16[8,256,256]{2,1,0:T(8,128)(2,1)S(1)}, bf16[8,256,256]{2,1,0:T(8,128)(2,1)S(1)}) custom-call(s32[2,8]{1,0:T(2,128)S(1)} %fusion.13.ids, s32[4096]{0:T(1024)S(1)} %bitcast.56, bf16[5,256,256]{2,1,0:T(8,128)(2,1)S(1)} %fusion.9.refs_0_, bf16[2,256,256]{2,1,0:T(8,128)(2,1)S(1)} %pad_maximum_fusion.1.refs_1_, ...), custom_call_target="tpu_custom_call" | custom-call | tf_op jit(solution)/shard_map/attention/pallas_call | solution.py:187
  78.8 2.5 %collective-permute-done.12 = bf16[8,256,256]{2,1,0:T(8,128)(2,1)S(1)} collective-permute-done((bf16[8,256,256]{2,1,0:T(8,128)(2,1)S(1)}, bf16[8,256,256]{2,1,0:T(8,128)(2,1)S(1)}, u32[]{:S(2)}, u32[]{:S(2)}) %collective-permute-start.12) | collective-permute-done | bytes 1048608 | tf_op jit(solution)/shard_map/ppermute | solution.py:383
  81.3 1.3 %add_convert_fusion.grads = bf16[8,256,256]{2,1,0:T(8,128)(2,1)} fusion(bf16[8,256,256]{2,1,0:T(8,128)(2,1)S(1)} %collective-permute-done.12, bf16[8,256,256]{2,1,0:T(8,128)(2,1)S(1)} %get-tuple-element.33), kind=kLoop, calls=%fused_computation | loop fusion | flops 2097152 | bytes 3145728 | tf_op jit(solution)/shard_map/convert_element_type | solution.py:438
  82.6 5.2 %all-to-all-start.1 = ((bf16[8,256,256]{2,1,0:T(8,128)(2,1)}), bf16[8,256,256]{2,1,0:T(8,128)(2,1)S(1)}, u32[]{:S(2)}, u32[]{:S(2)}) async-start(bf16[8,256,256]{2,1,0:T(8,128)(2,1)} %add_convert_fusion.grads), calls=%async_computation.1 | async-start | bytes 2097152 | tf_op jit(solution)/shard_map/all_to_all | solution.py:392
  87.8 4.8 %weight_grad.1 = (bf16[8,64,256]{2,1,0:T(8,128)(2,1)}, bf16[8,64,256]{2,1,0:T(8,128)(2,1)}) custom-call(s32[2,8]{1,0:T(2,128)} %copy-done.5, bf16[8,256,256]{2,1,0:T(8,128)(2,1)} %add_convert_fusion.grads, bf16[256,1024]{1,0:T(8,128)(2,1)} %get-tuple-element.31.refs_0_, bf16[256,1024]{1,0:T(8,128)(2,1)} %collective-permute-done.refs_1_, ...), custom_call_target="tpu_custom_call" | custom-call | tf_op jit(solution)/shard_map/weight_grad/pallas_call | solution.py:267
  92.6 1.7 %collective-permute-done.13 = bf16[8,64,256]{2,1,0:T(8,128)(2,1)S(1)} collective-permute-done((bf16[8,64,256]{2,1,0:T(8,128)(2,1)}, bf16[8,64,256]{2,1,0:T(8,128)(2,1)S(1)}, u32[]{:S(2)}, u32[]{:S(2)}) %collective-permute-start.13) | collective-permute-done | bytes 262176 | tf_op jit(solution)/shard_map/ppermute | solution.py:383
  96.0 4.7 %collective-permute-start.20 = (bf16[64,256]{1,0:T(8,128)(2,1)S(1)}, bf16[64,256]{1,0:T(8,128)(2,1)S(1)}, u32[]{:S(2)}, u32[]{:S(2)}) collective-permute-start(bf16[64,256]{1,0:T(8,128)(2,1)S(1)} %get-tuple-element.52), channel_id=1, source_target_pairs={{0,14},{1,15},{2,0},{3,1},{4,2},{5,3},{6,4},{7,5},{8,6},{9,7},{10,... | collective-permute-start | bytes 98312 | tf_op jit(solution)/shard_map/ppermute | solution.py:389
  101.3 2.9 %collective-permute-start.17 = (bf16[64,256]{1,0:T(8,128)(2,1)}, bf16[64,256]{1,0:T(8,128)(2,1)}, u32[]{:S(2)}, u32[]{:S(2)}) collective-permute-start(bf16[64,256]{1,0:T(8,128)(2,1)} %get-tuple-element.55), channel_id=1, source_target_pairs={{0,8},{1,9},{2,10},{3,11},{4,12},{5,13},{6,14},{7,15},{8,0},{9,1},... | collective-permute-start | bytes 98312 | tf_op jit(solution)/shard_map/ppermute | solution.py:389
  104.2 3.1 %collective-permute-done.20.refs_7_ = bf16[64,256]{1,0:T(8,128)(2,1)S(1)} collective-permute-done((bf16[64,256]{1,0:T(8,128)(2,1)S(1)}, bf16[64,256]{1,0:T(8,128)(2,1)S(1)}, u32[]{:S(2)}, u32[]{:S(2)}) %collective-permute-start.20) | collective-permute-done | bytes 32800 | tf_op jit(solution)/shard_map/ppermute | solution.py:389
  108.0 12.4 %collective-permute-start.14 = (bf16[64,256]{1,0:T(8,128)(2,1)}, bf16[64,256]{1,0:T(8,128)(2,1)}, u32[]{:S(2)}, u32[]{:S(2)}) collective-permute-start(bf16[64,256]{1,0:T(8,128)(2,1)} %get-tuple-element.58), channel_id=1, source_target_pairs={{0,2},{1,3},{2,4},{3,5},{4,6},{5,7},{6,8},{7,9},{8,10},{9,11},{10,... | collective-permute-start | bytes 98312 | tf_op jit(solution)/shard_map/ppermute | solution.py:389
  120.5 1.6 %copy-done.1 = bf16[1024,1024]{1,0:T(8,128)(2,1)S(1)} copy-done((bf16[1024,1024]{1,0:T(8,128)(2,1)S(1)}, bf16[1024,1024]{1,0:T(8,128)(2,1)}, u32[]{:S(2)}) %copy-start.1) | copy-done | bytes 2097176
  123.1 2.3 %home.1 = bf16[256,1024]{1,0:T(8,128)(2,1)} custom-call(bf16[8,256,256]{2,1,0:T(8,128)(2,1)S(1)} %all-to-all-done.1.grads, bf16[1024,1024]{1,0:T(8,128)(2,1)S(1)} %copy-done.1, bf16[1024,1024]{1,0:T(8,128)(2,1)S(1)} %copy-done, bf16[256,1024]{1,0:T(8,128)(2,1)S(1)} %copy-done.2, f32[1,1024]{1,0:T(1,128)S(1)} %bitcast.58), custom_call_target="tpu_custom_call" | custom-call | tf_op jit(solution)/shard_map/home/pallas_call | solution.py:294
  125.5 1.7 %weight_rows.1 = (f32[64,1024]{1,0:T(8,128)}, f32[64,1024]{1,0:T(8,128)}, f32[1,64]{1,0:T(1,128)}) custom-call(s32[2,8]{1,0:T(2,128)S(1)} %copy-done.6, bf16[64,1024]{1,0:T(8,128)(2,1)S(1)} %copy-done.3, bf16[64,1024]{1,0:T(8,128)(2,1)S(1)} %get-tuple-element.39.v_own, f32[1,64]{1,0:T(1,128)S(1)} %bitcast.59, bf16[64,256]{1,0:T(8,128)(2,1)S(1)} %get-tuple-element.41.refs_0_, ...), custom_call_target="tpu_custom_call" | custom-call | tf_op jit(solution)/shard_map/weight_rows/pallas_call | solution.py:325
  (66 shorter events, 10.4 us)
Async XLA Ops:
  0.6 23.2 %copy-start.4 = (f32[1024]{0:T(1024)S(1)}, f32[1024]{0:T(1024)}, u32[]{:S(2)}) copy-start(f32[1024]{0:T(1024)} %param.10) | copy-start | bytes 12292
  0.7 12.0 %copy-start = (bf16[1024,1024]{1,0:T(8,128)(2,1)S(1)}, bf16[1024,1024]{1,0:T(8,128)(2,1)}, u32[]{:S(2)}) copy-start(bf16[1024,1024]{1,0:T(8,128)(2,1)} %w_v.1) | copy-start | bytes 6291460
  3.3 16.7 %collective-permute-start.1 = (bf16[256,1024]{1,0:T(8,128)(2,1)}, bf16[256,1024]{1,0:T(8,128)(2,1)}, u32[]{:S(2)}, u32[]{:S(2)}) collective-permute-start(bf16[256,1024]{1,0:T(8,128)(2,1)} %get-tuple-element.31.refs_0_), channel_id=1, source_target_pairs={{0,2},{1,3},{4,0},{5,1},{8,4},{9,5},{12,8},{13,9},{14,12},{15,13},... | collective-permute-start | bytes 1572872 | tf_op jit(solution)/shard_map/ppermute | solution.py:377
  6.3 16.5 %collective-permute-start = (bf16[256,1024]{1,0:T(8,128)(2,1)}, bf16[256,1024]{1,0:T(8,128)(2,1)}, u32[]{:S(2)}, u32[]{:S(2)}) collective-permute-start(bf16[256,1024]{1,0:T(8,128)(2,1)} %get-tuple-element.31.refs_0_), channel_id=1, source_target_pairs={{0,4},{1,5},{4,8},{5,9},{8,12},{9,13},{12,14},{13,15},{14,10},{15,... | collective-permute-start | bytes 1572872 | tf_op jit(solution)/shard_map/ppermute | solution.py:377
  6.3 38.5 %all-to-all-start = ((bf16[8,272,128]{2,1,0:T(8,128)(2,1)}), bf16[8,272,128]{2,1,0:T(8,128)(2,1)S(1)}, u32[]{:S(2)}, u32[]{:S(2)}) async-start(bf16[8,272,128]{2,1,0:T(8,128)(2,1)} %get-tuple-element.32), calls=%async_computation | async-start | bytes 1114112 | tf_op jit(solution)/shard_map/all_to_all | solution.py:392
  15.3 28.2 %copy-start.8 = (bf16[1024,128]{1,0:T(8,128)(2,1)}, bf16[1024,128]{1,0:T(8,128)(2,1)S(1)}, u32[]{:S(2)}) copy-start(bf16[1024,128]{1,0:T(8,128)(2,1)S(1)} %get-tuple-element.62) | copy-start | bytes 786436
  15.3 28.2 %copy-start.10 = (bf16[1024,128]{1,0:T(8,128)(2,1)}, bf16[1024,128]{1,0:T(8,128)(2,1)S(1)}, u32[]{:S(2)}) copy-start(bf16[1024,128]{1,0:T(8,128)(2,1)S(1)} %get-tuple-element.63) | copy-start | bytes 786436
  20.0 18.8 %collective-permute-start.3 = (bf16[256,1024]{1,0:T(8,128)(2,1)}, bf16[256,1024]{1,0:T(8,128)(2,1)}, u32[]{:S(2)}, u32[]{:S(2)}) collective-permute-start(bf16[256,1024]{1,0:T(8,128)(2,1)} %collective-permute-done.1.refs_2_), channel_id=1, source_target_pairs={{0,2},{1,3},{4,0},{5,1},{8,4},{9,5},{12,8},{13,9},{14,12},{15,13},... | collective-permute-start | bytes 1572872 | tf_op jit(solution)/shard_map/ppermute | solution.py:377
  22.8 16.8 %collective-permute-start.2 = (bf16[256,1024]{1,0:T(8,128)(2,1)}, bf16[256,1024]{1,0:T(8,128)(2,1)}, u32[]{:S(2)}, u32[]{:S(2)}) collective-permute-start(bf16[256,1024]{1,0:T(8,128)(2,1)} %collective-permute-done.refs_1_), channel_id=1, source_target_pairs={{0,4},{1,5},{4,8},{5,9},{8,12},{9,13},{12,14},{13,15},{14,10},{15,... | collective-permute-start | bytes 1572872 | tf_op jit(solution)/shard_map/ppermute | solution.py:377
  23.8 41.6 %copy-start.5 = (s32[2,8]{1,0:T(2,128)}, s32[2,8]{1,0:T(2,128)S(1)}, u32[]{:S(2)}) copy-start(s32[2,8]{1,0:T(2,128)S(1)} %fusion.13.ids) | copy-start | bytes 196
  38.7 16.1 %collective-permute-start.5 = (bf16[256,1024]{1,0:T(8,128)(2,1)}, bf16[256,1024]{1,0:T(8,128)(2,1)}, u32[]{:S(2)}, u32[]{:S(2)}) collective-permute-start(bf16[256,1024]{1,0:T(8,128)(2,1)} %collective-permute-done.3.refs_4_), channel_id=1, source_target_pairs={{0,2},{1,3},{4,0},{5,1},{8,4},{9,5},{12,8},{13,9},{14,12},{15,13},... | collective-permute-start | bytes 1572872 | tf_op jit(solution)/shard_map/ppermute | solution.py:377
  39.5 16.3 %collective-permute-start.4 = (bf16[256,1024]{1,0:T(8,128)(2,1)}, bf16[256,1024]{1,0:T(8,128)(2,1)}, u32[]{:S(2)}, u32[]{:S(2)}) collective-permute-start(bf16[256,1024]{1,0:T(8,128)(2,1)} %collective-permute-done.2.refs_3_), channel_id=1, source_target_pairs={{0,4},{1,5},{4,8},{5,9},{8,12},{9,13},{12,14},{13,15},{14,10},{15,... | collective-permute-start | bytes 1572872 | tf_op jit(solution)/shard_map/ppermute | solution.py:377
  44.9 14.1 %copy-start.9 = (bf16[1024,128]{1,0:T(8,128)(2,1)S(1)}, bf16[1024,128]{1,0:T(8,128)(2,1)}, u32[]{:S(2)}) copy-start(bf16[1024,128]{1,0:T(8,128)(2,1)} %copy-done.8) | copy-start | bytes 786436
  44.9 14.1 %copy-start.11 = (bf16[1024,128]{1,0:T(8,128)(2,1)S(1)}, bf16[1024,128]{1,0:T(8,128)(2,1)}, u32[]{:S(2)}) copy-start(bf16[1024,128]{1,0:T(8,128)(2,1)} %copy-done.10) | copy-start | bytes 786436
  44.9 19.2 %collective-permute-start.11 = (bf16[8,272,128]{2,1,0:T(8,128)(2,1)S(1)}, bf16[8,272,128]{2,1,0:T(8,128)(2,1)S(1)}, u32[]{:S(2)}, u32[]{:S(2)}) collective-permute-start(bf16[8,272,128]{2,1,0:T(8,128)(2,1)S(1)} %all-to-all-done.refs_6_), channel_id=1, source_target_pairs={{0,1},{1,0},{2,3},{3,2},{4,5},{5,4},{6,7},{7,6},{8,9},{9,8},{10,11... | collective-permute-start | bytes 1671176 | tf_op jit(solution)/shard_map/ppermute | solution.py:383
  48.0 16.1 %collective-permute-start.8 = (bf16[5,256,256]{2,1,0:T(8,128)(2,1)S(1)}, bf16[5,256,256]{2,1,0:T(8,128)(2,1)S(1)}, u32[]{:S(2)}, u32[]{:S(2)}) collective-permute-start(bf16[5,256,256]{2,1,0:T(8,128)(2,1)S(1)} %fusion.9.refs_0_), channel_id=1, source_target_pairs={{0,1},{1,0},{2,3},{3,2},{4,5},{5,4},{6,7},{7,6},{8,9},{9,8},{10,11... | collective-permute-start | bytes 1966088 | tf_op jit(solution)/shard_map/ppermute | solution.py:383
  55.8 7.8 %collective-permute-start.7 = (bf16[128,1024]{1,0:T(8,128)(2,1)S(1)}, bf16[128,1024]{1,0:T(8,128)(2,1)S(1)}, u32[]{:S(2)}, u32[]{:S(2)}) collective-permute-start(bf16[128,1024]{1,0:T(8,128)(2,1)S(1)} %slice.41), channel_id=1, source_target_pairs={{0,2},{1,3},{4,0},{5,1},{8,4},{9,5},{12,8},{13,9},{14,12},{15,13},... | collective-permute-start | bytes 786440 | tf_op jit(solution)/shard_map/ppermute | solution.py:377
  56.9 6.7 %collective-permute-start.6 = (bf16[128,1024]{1,0:T(8,128)(2,1)S(1)}, bf16[128,1024]{1,0:T(8,128)(2,1)S(1)}, u32[]{:S(2)}, u32[]{:S(2)}) collective-permute-start(bf16[128,1024]{1,0:T(8,128)(2,1)S(1)} %slice.40), channel_id=1, source_target_pairs={{0,4},{1,5},{4,8},{5,9},{8,12},{9,13},{12,14},{13,15},{14,10},{15,... | collective-permute-start | bytes 786440 | tf_op jit(solution)/shard_map/ppermute | solution.py:377
  61.7 2.4 %collective-permute-start.9 = (bf16[2,256,256]{2,1,0:T(8,128)(2,1)S(1)}, bf16[2,256,256]{2,1,0:T(8,128)(2,1)S(1)}, u32[]{:S(2)}, u32[]{:S(2)}) collective-permute-start(bf16[2,256,256]{2,1,0:T(8,128)(2,1)S(1)} %pad_maximum_fusion.1.refs_1_), channel_id=1, source_target_pairs={{0,1},{1,0},{2,3},{3,2},{4,5},{5,4},{6,7},{7,6},{8,9},{9,8},{10,11... | collective-permute-start | bytes 786440 | tf_op jit(solution)/shard_map/ppermute | solution.py:383
  63.7 14.9 %copy-start.7 = (bf16[256,1024]{1,0:T(8,128)(2,1)}, bf16[256,1024]{1,0:T(8,128)(2,1)S(1)}, u32[]{:S(2)}) copy-start(bf16[256,1024]{1,0:T(8,128)(2,1)S(1)} %constant_dynamic-update-slice_fusion.refs_7_) | copy-start | bytes 1572868
  64.0 1.4 %collective-permute-start.10 = (bf16[1,256,256]{2,1,0:T(8,128)(2,1)S(1)}, bf16[1,256,256]{2,1,0:T(8,128)(2,1)S(1)}, u32[]{:S(2)}, u32[]{:S(2)}) collective-permute-start(bf16[1,256,256]{2,1,0:T(8,128)(2,1)S(1)} %fusion.12.refs_2_), channel_id=1, source_target_pairs={{0,1},{1,0},{2,3},{3,2},{4,5},{5,4},{6,7},{7,6},{8,9},{9,8},{10,11... | collective-permute-start | bytes 393224 | tf_op jit(solution)/shard_map/ppermute | solution.py:383
  78.6 2.7 %collective-permute-start.12 = (bf16[8,256,256]{2,1,0:T(8,128)(2,1)S(1)}, bf16[8,256,256]{2,1,0:T(8,128)(2,1)S(1)}, u32[]{:S(2)}, u32[]{:S(2)}) collective-permute-start(bf16[8,256,256]{2,1,0:T(8,128)(2,1)S(1)} %get-tuple-element.34), channel_id=1, source_target_pairs={{0,1},{1,0},{2,3},{3,2},{4,5},{5,4},{6,7},{7,6},{8,9},{9,8},{10,11... | collective-permute-start | bytes 3145736 | tf_op jit(solution)/shard_map/ppermute | solution.py:383
  82.6 37.9 %all-to-all-start.1 = ((bf16[8,256,256]{2,1,0:T(8,128)(2,1)}), bf16[8,256,256]{2,1,0:T(8,128)(2,1)S(1)}, u32[]{:S(2)}, u32[]{:S(2)}) async-start(bf16[8,256,256]{2,1,0:T(8,128)(2,1)} %add_convert_fusion.grads), calls=%async_computation.1 | async-start | bytes 2097152 | tf_op jit(solution)/shard_map/all_to_all | solution.py:392
  92.6 1.7 %collective-permute-start.13 = (bf16[8,64,256]{2,1,0:T(8,128)(2,1)}, bf16[8,64,256]{2,1,0:T(8,128)(2,1)S(1)}, u32[]{:S(2)}, u32[]{:S(2)}) collective-permute-start(bf16[8,64,256]{2,1,0:T(8,128)(2,1)} %get-tuple-element.36), channel_id=1, source_target_pairs={{0,1},{1,0},{2,3},{3,2},{4,5},{5,4},{6,7},{7,6},{8,9},{9,8},{10,11... | collective-permute-start | bytes 786440 | tf_op jit(solution)/shard_map/ppermute | solution.py:383
  96.0 11.3 %collective-permute-start.20 = (bf16[64,256]{1,0:T(8,128)(2,1)S(1)}, bf16[64,256]{1,0:T(8,128)(2,1)S(1)}, u32[]{:S(2)}, u32[]{:S(2)}) collective-permute-start(bf16[64,256]{1,0:T(8,128)(2,1)S(1)} %get-tuple-element.52), channel_id=1, source_target_pairs={{0,14},{1,15},{2,0},{3,1},{4,2},{5,3},{6,4},{7,5},{8,6},{9,7},{10,... | collective-permute-start | bytes 98312 | tf_op jit(solution)/shard_map/ppermute | solution.py:389
  100.7 7.3 %collective-permute-start.19 = (bf16[64,256]{1,0:T(8,128)(2,1)S(1)}, bf16[64,256]{1,0:T(8,128)(2,1)S(1)}, u32[]{:S(2)}, u32[]{:S(2)}) collective-permute-start(bf16[64,256]{1,0:T(8,128)(2,1)S(1)} %get-tuple-element.53), channel_id=1, source_target_pairs={{0,12},{1,13},{2,14},{3,15},{4,0},{5,1},{6,2},{7,3},{8,4},{9,5},{1... | collective-permute-start | bytes 98312 | tf_op jit(solution)/shard_map/ppermute | solution.py:389
  101.3 24.1 %collective-permute-start.18 = (bf16[64,256]{1,0:T(8,128)(2,1)}, bf16[64,256]{1,0:T(8,128)(2,1)S(1)}, u32[]{:S(2)}, u32[]{:S(2)}) collective-permute-start(bf16[64,256]{1,0:T(8,128)(2,1)} %get-tuple-element.54), channel_id=1, source_target_pairs={{0,10},{1,11},{2,12},{3,13},{4,14},{5,15},{6,0},{7,1},{8,2},{9,3},... | collective-permute-start | bytes 98312 | tf_op jit(solution)/shard_map/ppermute | solution.py:389
  101.3 24.1 %collective-permute-start.17 = (bf16[64,256]{1,0:T(8,128)(2,1)}, bf16[64,256]{1,0:T(8,128)(2,1)}, u32[]{:S(2)}, u32[]{:S(2)}) collective-permute-start(bf16[64,256]{1,0:T(8,128)(2,1)} %get-tuple-element.55), channel_id=1, source_target_pairs={{0,8},{1,9},{2,10},{3,11},{4,12},{5,13},{6,14},{7,15},{8,0},{9,1},... | collective-permute-start | bytes 98312 | tf_op jit(solution)/shard_map/ppermute | solution.py:389
  104.2 21.2 %collective-permute-start.16 = (bf16[64,256]{1,0:T(8,128)(2,1)}, bf16[64,256]{1,0:T(8,128)(2,1)}, u32[]{:S(2)}, u32[]{:S(2)}) collective-permute-start(bf16[64,256]{1,0:T(8,128)(2,1)} %get-tuple-element.56), channel_id=1, source_target_pairs={{0,6},{1,7},{2,8},{3,9},{4,10},{5,11},{6,12},{7,13},{8,14},{9,15},... | collective-permute-start | bytes 98312 | tf_op jit(solution)/shard_map/ppermute | solution.py:389
  107.3 18.1 %collective-permute-start.15 = (bf16[64,256]{1,0:T(8,128)(2,1)}, bf16[64,256]{1,0:T(8,128)(2,1)}, u32[]{:S(2)}, u32[]{:S(2)}) collective-permute-start(bf16[64,256]{1,0:T(8,128)(2,1)} %get-tuple-element.57), channel_id=1, source_target_pairs={{0,4},{1,5},{2,6},{3,7},{4,8},{5,9},{6,10},{7,11},{8,12},{9,13},{1... | collective-permute-start | bytes 98312 | tf_op jit(solution)/shard_map/ppermute | solution.py:389
  108.0 17.4 %copy-start.6 = (s32[2,8]{1,0:T(2,128)S(1)}, s32[2,8]{1,0:T(2,128)}, u32[]{:S(2)}) copy-start(s32[2,8]{1,0:T(2,128)} %copy-done.5) | copy-start | bytes 196
  108.0 17.4 %collective-permute-start.14 = (bf16[64,256]{1,0:T(8,128)(2,1)}, bf16[64,256]{1,0:T(8,128)(2,1)}, u32[]{:S(2)}, u32[]{:S(2)}) collective-permute-start(bf16[64,256]{1,0:T(8,128)(2,1)} %get-tuple-element.58), channel_id=1, source_target_pairs={{0,2},{1,3},{2,4},{3,5},{4,6},{5,7},{6,8},{7,9},{8,10},{9,11},{10,... | collective-permute-start | bytes 98312 | tf_op jit(solution)/shard_map/ppermute | solution.py:389
  (4 other events, 16.9 us)

commit v6 on v5

--- a/solution.py
+++ b/solution.py
@@ -244,6 +244,25 @@
     )(tokens, gain, cot, log_sums)
 
 
+def halves_kernel(first, second, upper, lower):
+    upper[...] = first[...]
+    lower[...] = second[...]
+
+
+def halves(first, second):
+    rows, width = first.shape
+    block = (rows // 2, width)
+    return pl.pallas_call(
+        halves_kernel,
+        grid=(1,),
+        out_shape=[jax.ShapeDtypeStruct(block, first.dtype)] * 2,
+        in_specs=[pl.BlockSpec(block, lambda i: (0, 0)), pl.BlockSpec(block, lambda i: (1, 0))],
+        out_specs=[pl.BlockSpec(block, lambda i: (0, 0))] * 2,
+        compiler_params=pltpu.CompilerParams(vmem_limit_bytes=SMALL_VMEM_BYTES),
+        name="halves",
+    )(first, second)
+
+
 def weight_grad_kernel(per, count, ids, grads, *refs):
     shards = refs[:count]
     outs = refs[count : count + per]
@@ -404,8 +423,9 @@
     for s in range(1, half):
         ahead, behind = hop(ahead, 1), hop(behind, -1)
         shards += [ahead, behind]
+    upper, lower = halves(ahead, behind)
     shards.append(
-        jnp.concatenate([hop(ahead[: size // 2], 1), hop(behind[size // 2 :], -1)], axis=0)
+        jnp.concatenate([hop(upper, 1), hop(lower, -1)], axis=0)
     )
     cot = exchange(chunks)
 

time: 128 us -> 128 us (level)
  local copies, waits for them, and re-layouts: 8.68 us -> 6.1 us
  Pallas kernels: 24.6 us -> 25.9 us
    slice x2 -> x0, local copies, waits for them, and re-layouts: 1.94 us -> none  [the longest x1 0.97 us: per_device(): ahead[:size // 2]]
    unnamed x27 -> x29, local copies, waits for them, and re-layouts: 2.7 us -> 2.7 us
  transfers between devices with their start and end apart: 23 -> 23, of which waited for: 9 -> 11; matrix products, arithmetic and copies ran while one was open for 13% -> 12% of each run, Pallas kernels for 6% -> 6%
where the time goes in v6:
time: 128 us
  starting transfers between devices  46.2 us (36%)
  waiting for transfers between devices  35 us (27%)
  Pallas kernels  25.9 us (20%)
  matrix products  11.2 us (9%)
  local copies, waits for them, and re-layouts  6.1 us (5%)
  other arithmetic  2.36 us (2%)
    ppermute x8, waiting for transfers between devices, hop(): return lax.ppermute(x, 'tok', route)  25.6 us
    ppermute x7, starting transfers between devices, send(): return lax.ppermute(x, 'tok', route)  20.7 us
    ppermute x8, starting transfers between devices, hop(): return lax.ppermute(x, 'tok', route)  13.5 us
    pallas_call x1, Pallas kernels, attention(): pl.pallas_call(partial(attention_kernel, per, parts, blocks, rounds, len(...  13.5 us
    dot_general x8, matrix products, project(): jnp.dot(n, my_weights, preferred_element_type=F32).astype(BF16)  11.2 us
    all_to_all x2, starting transfers between devices, exchange(): return lax.all_to_all(x, 'tok', 0, 0, tiled=True, axis_index_groups=groups)  11.2 us
    ppermute x6, waiting for transfers between devices, swap(): return lax.ppermute(x, 'tok', route)  5.58 us
    pallas_call x1, Pallas kernels, weight_grad(): pl.pallas_call(partial(weight_grad_kernel, per, len(shards)), out_shape=[...  4.76 us
  transfers between devices with their start and end apart: 23, of which 11 were waited for; matrix products, arithmetic and copies ran while one was open for 12% of the time, Pallas kernels for 6%

profile of v6, /device:TPU:0, one launch (start us, length us, event | category | flops | bytes accessed | tf_op | source)
XLA Modules:
  0.0 127.6 jit_solution(231029881136571186)
XLA Ops:
  0.7 2.6 %prepare.1 = (bf16[256,1024]{1,0:T(8,128)(2,1)}, bf16[8,272,128]{2,1,0:T(8,128)(2,1)}) custom-call(bf16[256,1024]{1,0:T(8,128)(2,1)} %tokens.3, f32[1,1024]{1,0:T(1,128)} %bitcast.57, bf16[256,1024]{1,0:T(8,128)(2,1)} %cot.1, f32[2,8,256]{2,1,0:T(8,128)} %log_sums.1), custom_call_target="tpu_custom_call" | custom-call | tf_op jit(solution)/shard_map/prepare/pallas_call | solution.py:236
  3.3 3.0 %collective-permute-start.1 = (bf16[256,1024]{1,0:T(8,128)(2,1)}, bf16[256,1024]{1,0:T(8,128)(2,1)}, u32[]{:S(2)}, u32[]{:S(2)}) collective-permute-start(bf16[256,1024]{1,0:T(8,128)(2,1)} %get-tuple-element.33.refs_0_), channel_id=1, source_target_pairs={{0,2},{1,3},{4,0},{5,1},{8,4},{9,5},{12,8},{13,9},{14,12},{15,13},... | collective-permute-start | bytes 1572872 | tf_op jit(solution)/shard_map/ppermute | solution.py:396
  6.3 6.3 %all-to-all-start = ((bf16[8,272,128]{2,1,0:T(8,128)(2,1)}), bf16[8,272,128]{2,1,0:T(8,128)(2,1)S(1)}, u32[]{:S(2)}, u32[]{:S(2)}) async-start(bf16[8,272,128]{2,1,0:T(8,128)(2,1)} %get-tuple-element.36), calls=%async_computation | async-start | bytes 1114112 | tf_op jit(solution)/shard_map/all_to_all | solution.py:411
  13.6 1.0 constant_dynamic-slice_fusion
  14.6 5.3 %collective-permute-done.1.refs_2_ = bf16[256,1024]{1,0:T(8,128)(2,1)} collective-permute-done((bf16[256,1024]{1,0:T(8,128)(2,1)}, bf16[256,1024]{1,0:T(8,128)(2,1)}, u32[]{:S(2)}, u32[]{:S(2)}) %collective-permute-start.1) | collective-permute-done | bytes 524320 | tf_op jit(solution)/shard_map/ppermute | solution.py:396
  19.9 2.8 %collective-permute-start.3 = (bf16[256,1024]{1,0:T(8,128)(2,1)}, bf16[256,1024]{1,0:T(8,128)(2,1)}, u32[]{:S(2)}, u32[]{:S(2)}) collective-permute-start(bf16[256,1024]{1,0:T(8,128)(2,1)} %collective-permute-done.1.refs_2_), channel_id=1, source_target_pairs={{0,2},{1,3},{4,0},{5,1},{8,4},{9,5},{12,8},{13,9},{14,12},{15,13},... | collective-permute-start | bytes 1572872 | tf_op jit(solution)/shard_map/ppermute | solution.py:396
  24.8 2.0 %fusion.3 = bf16[5,256,256]{2,1,0:T(8,128)(2,1)} fusion(bf16[5,256,256]{2,1,0:T(8,128)(2,1)} %fusion.1, bf16[256,1024]{1,0:T(8,128)(2,1)} %collective-permute-done.refs_1_, bf16[1024,128]{1,0:T(8,128)(2,1)S(1)} %get-tuple-element.66, bf16[1024,128]{1,0:T(8,128)(2,1)S(1)} %get-tuple-element.67), kind=kOutput, calls=%fused_computation.12 | convolution fusion | flops 135331840 | bytes 1179648 | tf_op jit(solution)/shard_map/dot_general | solution.py:447
  26.8 12.0 %collective-permute-done.3.refs_4_ = bf16[256,1024]{1,0:T(8,128)(2,1)} collective-permute-done((bf16[256,1024]{1,0:T(8,128)(2,1)}, bf16[256,1024]{1,0:T(8,128)(2,1)}, u32[]{:S(2)}, u32[]{:S(2)}) %collective-permute-start.3) | collective-permute-done | bytes 524320 | tf_op jit(solution)/shard_map/ppermute | solution.py:396
  39.5 4.0 %collective-permute-start.4 = (bf16[256,1024]{1,0:T(8,128)(2,1)}, bf16[256,1024]{1,0:T(8,128)(2,1)}, u32[]{:S(2)}, u32[]{:S(2)}) collective-permute-start(bf16[256,1024]{1,0:T(8,128)(2,1)} %collective-permute-done.2.refs_3_), channel_id=1, source_target_pairs={{0,4},{1,5},{4,8},{5,9},{8,12},{9,13},{12,14},{13,15},{14,10},{15,... | collective-permute-start | bytes 1572872 | tf_op jit(solution)/shard_map/ppermute | solution.py:396
  43.5 2.0 %fusion.5 = bf16[5,256,256]{2,1,0:T(8,128)(2,1)} fusion(bf16[5,256,256]{2,1,0:T(8,128)(2,1)} %fusion.3, bf16[256,1024]{1,0:T(8,128)(2,1)} %collective-permute-done.1.refs_2_, bf16[1024,128]{1,0:T(8,128)(2,1)S(1)} %get-tuple-element.66, bf16[1024,128]{1,0:T(8,128)(2,1)S(1)} %get-tuple-element.67), kind=kOutput, calls=%fused_computation.14 | convolution fusion | flops 135331840 | bytes 1179648 | tf_op jit(solution)/shard_map/dot_general | solution.py:447
  45.5 2.2 %fusion.7 = bf16[5,256,256]{2,1,0:T(8,128)(2,1)} fusion(bf16[5,256,256]{2,1,0:T(8,128)(2,1)} %fusion.5, bf16[256,1024]{1,0:T(8,128)(2,1)} %collective-permute-done.2.refs_3_, bf16[1024,128]{1,0:T(8,128)(2,1)} %copy-done.9, bf16[1024,128]{1,0:T(8,128)(2,1)} %copy-done.11), kind=kOutput, calls=%fused_computation.16 | convolution fusion | flops 135331840 | bytes 1179648 | tf_op jit(solution)/shard_map/dot_general | solution.py:447
  47.7 2.1 %fusion.9.refs_0_ = bf16[5,256,256]{2,1,0:T(8,128)(2,1)} fusion(bf16[5,256,256]{2,1,0:T(8,128)(2,1)} %fusion.7, bf16[256,1024]{1,0:T(8,128)(2,1)} %collective-permute-done.3.refs_4_, bf16[1024,128]{1,0:T(8,128)(2,1)} %copy-done.9, bf16[1024,128]{1,0:T(8,128)(2,1)} %copy-done.11), kind=kOutput, calls=%fused_computation.18 | convolution fusion | flops 135331840 | bytes 1179648 | tf_op jit(solution)/shard_map/dot_general | solution.py:447
  50.3 4.4 %collective-permute-done.5.second.refs_6_ = bf16[256,1024]{1,0:T(8,128)(2,1)S(1)} collective-permute-done((bf16[256,1024]{1,0:T(8,128)(2,1)}, bf16[256,1024]{1,0:T(8,128)(2,1)S(1)}, u32[]{:S(2)}, u32[]{:S(2)}) %collective-permute-start.5) | collective-permute-done | bytes 524320 | tf_op jit(solution)/shard_map/ppermute | solution.py:396
  56.1 1.6 %collective-permute-start.6 = (bf16[128,1024]{1,0:T(8,128)(2,1)S(1)}, bf16[128,1024]{1,0:T(8,128)(2,1)S(1)}, u32[]{:S(2)}, u32[]{:S(2)}) collective-permute-start(bf16[128,1024]{1,0:T(8,128)(2,1)S(1)} %get-tuple-element.34), channel_id=1, source_target_pairs={{0,4},{1,5},{4,8},{5,9},{8,12},{9,13},{12,14},{13,15},{14,10},{15,... | collective-permute-start | bytes 786440 | tf_op jit(solution)/shard_map/ppermute | solution.py:396
  57.7 1.0 collective-permute-start.7
  59.1 1.3 %fusion.10 = bf16[1,256,256]{2,1,0:T(8,128)(2,1)S(1)} fusion(bf16[256,1024]{1,0:T(8,128)(2,1)} %collective-permute-done.4.first.refs_5_, bf16[1024,128]{1,0:T(8,128)(2,1)S(1)} %copy-done.10, bf16[1024,128]{1,0:T(8,128)(2,1)S(1)} %copy-done.12), kind=kOutput, calls=%fused_computation.19 | convolution fusion | flops 135331840 | bytes 1179648 | tf_op jit(solution)/shard_map/dot_general | solution.py:447
  60.5 2.7 %collective-permute-done.6 = bf16[128,1024]{1,0:T(8,128)(2,1)S(1)} collective-permute-done((bf16[128,1024]{1,0:T(8,128)(2,1)S(1)}, bf16[128,1024]{1,0:T(8,128)(2,1)S(1)}, u32[]{:S(2)}, u32[]{:S(2)}) %collective-permute-start.6) | collective-permute-done | bytes 262176 | tf_op jit(solution)/shard_map/ppermute | solution.py:396
  64.5 1.3 %collective-permute-done.10.refs_5_ = bf16[1,256,256]{2,1,0:T(8,128)(2,1)S(1)} collective-permute-done((bf16[1,256,256]{2,1,0:T(8,128)(2,1)S(1)}, bf16[1,256,256]{2,1,0:T(8,128)(2,1)S(1)}, u32[]{:S(2)}, u32[]{:S(2)}) %collective-permute-start.10) | collective-permute-done | bytes 131104 | tf_op jit(solution)/shard_map/ppermute | solution.py:402
  65.8 13.5 %attention.1 = (bf16[8,256,256]{2,1,0:T(8,128)(2,1)S(1)}, bf16[8,256,256]{2,1,0:T(8,128)(2,1)S(1)}) custom-call(s32[2,8]{1,0:T(2,128)S(1)} %fusion.13.ids, s32[4096]{0:T(1024)S(1)} %bitcast.56, bf16[5,256,256]{2,1,0:T(8,128)(2,1)} %fusion.9.refs_0_, bf16[2,256,256]{2,1,0:T(8,128)(2,1)S(1)} %pad_maximum_fusion.1.refs_1_, ...), custom_call_target="tpu_custom_call" | custom-call | tf_op jit(solution)/shard_map/attention/pallas_call | solution.py:187
  79.5 2.5 %collective-permute-done.12 = bf16[8,256,256]{2,1,0:T(8,128)(2,1)S(1)} collective-permute-done((bf16[8,256,256]{2,1,0:T(8,128)(2,1)S(1)}, bf16[8,256,256]{2,1,0:T(8,128)(2,1)S(1)}, u32[]{:S(2)}, u32[]{:S(2)}) %collective-permute-start.12) | collective-permute-done | bytes 1048608 | tf_op jit(solution)/shard_map/ppermute | solution.py:402
  82.1 1.3 %add_convert_fusion.grads = bf16[8,256,256]{2,1,0:T(8,128)(2,1)} fusion(bf16[8,256,256]{2,1,0:T(8,128)(2,1)S(1)} %collective-permute-done.12, bf16[8,256,256]{2,1,0:T(8,128)(2,1)S(1)} %get-tuple-element.37), kind=kLoop, calls=%fused_computation | loop fusion | flops 2097152 | bytes 3145728 | tf_op jit(solution)/shard_map/convert_element_type | solution.py:458
  83.4 4.9 %all-to-all-start.1 = ((bf16[8,256,256]{2,1,0:T(8,128)(2,1)}), bf16[8,256,256]{2,1,0:T(8,128)(2,1)S(1)}, u32[]{:S(2)}, u32[]{:S(2)}) async-start(bf16[8,256,256]{2,1,0:T(8,128)(2,1)} %add_convert_fusion.grads), calls=%async_computation.1 | async-start | bytes 2097152 | tf_op jit(solution)/shard_map/all_to_all | solution.py:411
  88.3 4.8 %weight_grad.1 = (bf16[8,64,256]{2,1,0:T(8,128)(2,1)}, bf16[8,64,256]{2,1,0:T(8,128)(2,1)}) custom-call(s32[2,8]{1,0:T(2,128)} %copy-done.5, bf16[8,256,256]{2,1,0:T(8,128)(2,1)} %add_convert_fusion.grads, bf16[256,1024]{1,0:T(8,128)(2,1)} %get-tuple-element.33.refs_0_, bf16[256,1024]{1,0:T(8,128)(2,1)} %collective-permute-done.refs_1_, ...), custom_call_target="tpu_custom_call" | custom-call | tf_op jit(solution)/shard_map/weight_grad/pallas_call | solution.py:286
  93.0 1.7 %collective-permute-done.13 = bf16[8,64,256]{2,1,0:T(8,128)(2,1)S(1)} collective-permute-done((bf16[8,64,256]{2,1,0:T(8,128)(2,1)}, bf16[8,64,256]{2,1,0:T(8,128)(2,1)S(1)}, u32[]{:S(2)}, u32[]{:S(2)}) %collective-permute-start.13) | collective-permute-done | bytes 262176 | tf_op jit(solution)/shard_map/ppermute | solution.py:402
  96.4 4.7 %collective-permute-start.20 = (bf16[64,256]{1,0:T(8,128)(2,1)S(1)}, bf16[64,256]{1,0:T(8,128)(2,1)S(1)}, u32[]{:S(2)}, u32[]{:S(2)}) collective-permute-start(bf16[64,256]{1,0:T(8,128)(2,1)S(1)} %get-tuple-element.56), channel_id=1, source_target_pairs={{0,14},{1,15},{2,0},{3,1},{4,2},{5,3},{6,4},{7,5},{8,6},{9,7},{10,... | collective-permute-start | bytes 98312 | tf_op jit(solution)/shard_map/ppermute | solution.py:408
  101.7 2.9 %collective-permute-start.17 = (bf16[64,256]{1,0:T(8,128)(2,1)}, bf16[64,256]{1,0:T(8,128)(2,1)}, u32[]{:S(2)}, u32[]{:S(2)}) collective-permute-start(bf16[64,256]{1,0:T(8,128)(2,1)} %get-tuple-element.59), channel_id=1, source_target_pairs={{0,8},{1,9},{2,10},{3,11},{4,12},{5,13},{6,14},{7,15},{8,0},{9,1},... | collective-permute-start | bytes 98312 | tf_op jit(solution)/shard_map/ppermute | solution.py:408
  104.7 3.1 %collective-permute-done.20.refs_7_ = bf16[64,256]{1,0:T(8,128)(2,1)S(1)} collective-permute-done((bf16[64,256]{1,0:T(8,128)(2,1)S(1)}, bf16[64,256]{1,0:T(8,128)(2,1)S(1)}, u32[]{:S(2)}, u32[]{:S(2)}) %collective-permute-start.20) | collective-permute-done | bytes 32800 | tf_op jit(solution)/shard_map/ppermute | solution.py:408
  108.5 12.5 %collective-permute-start.14 = (bf16[64,256]{1,0:T(8,128)(2,1)}, bf16[64,256]{1,0:T(8,128)(2,1)}, u32[]{:S(2)}, u32[]{:S(2)}) collective-permute-start(bf16[64,256]{1,0:T(8,128)(2,1)} %get-tuple-element.62), channel_id=1, source_target_pairs={{0,2},{1,3},{2,4},{3,5},{4,6},{5,7},{6,8},{7,9},{8,10},{9,11},{10,... | collective-permute-start | bytes 98312 | tf_op jit(solution)/shard_map/ppermute | solution.py:408
  120.9 1.6 %copy-done.1 = bf16[1024,1024]{1,0:T(8,128)(2,1)S(1)} copy-done((bf16[1024,1024]{1,0:T(8,128)(2,1)S(1)}, bf16[1024,1024]{1,0:T(8,128)(2,1)}, u32[]{:S(2)}) %copy-start.1) | copy-done | bytes 2097176
  122.5 1.0 copy-done.2
  123.6 2.3 %home.1 = bf16[256,1024]{1,0:T(8,128)(2,1)} custom-call(bf16[8,256,256]{2,1,0:T(8,128)(2,1)S(1)} %all-to-all-done.1.grads, bf16[1024,1024]{1,0:T(8,128)(2,1)S(1)} %copy-done.1, bf16[1024,1024]{1,0:T(8,128)(2,1)S(1)} %copy-done, bf16[256,1024]{1,0:T(8,128)(2,1)S(1)} %copy-done.2, f32[1,1024]{1,0:T(1,128)S(1)} %bitcast.58), custom_call_target="tpu_custom_call" | custom-call | tf_op jit(solution)/shard_map/home/pallas_call | solution.py:313
  125.9 1.7 %weight_rows.1 = (f32[64,1024]{1,0:T(8,128)}, f32[64,1024]{1,0:T(8,128)}, f32[1,64]{1,0:T(1,128)}) custom-call(s32[2,8]{1,0:T(2,128)S(1)} %copy-done.6, bf16[64,1024]{1,0:T(8,128)(2,1)S(1)} %get-tuple-element.42.qk_own, bf16[64,1024]{1,0:T(8,128)(2,1)S(1)} %get-tuple-element.43.v_own, f32[1,64]{1,0:T(1,128)S(1)} %bitcast.59, ...), custom_call_target="tpu_custom_call" | custom-call | tf_op jit(solution)/shard_map/weight_rows/pallas_call | solution.py:344
  (67 shorter events, 10.7 us)
Async XLA Ops:
  0.6 23.2 %copy-start.4 = (f32[1024]{0:T(1024)S(1)}, f32[1024]{0:T(1024)}, u32[]{:S(2)}) copy-start(f32[1024]{0:T(1024)} %param.10) | copy-start | bytes 12292
  3.3 20.6 %copy-start.8 = (bf16[256,1024]{1,0:T(8,128)(2,1)S(1)}, bf16[256,1024]{1,0:T(8,128)(2,1)}, u32[]{:S(2)}) copy-start(bf16[256,1024]{1,0:T(8,128)(2,1)} %get-tuple-element.33.refs_0_) | copy-start | bytes 1572868
  3.3 16.6 %collective-permute-start.1 = (bf16[256,1024]{1,0:T(8,128)(2,1)}, bf16[256,1024]{1,0:T(8,128)(2,1)}, u32[]{:S(2)}, u32[]{:S(2)}) collective-permute-start(bf16[256,1024]{1,0:T(8,128)(2,1)} %get-tuple-element.33.refs_0_), channel_id=1, source_target_pairs={{0,2},{1,3},{4,0},{5,1},{8,4},{9,5},{12,8},{13,9},{14,12},{15,13},... | collective-permute-start | bytes 1572872 | tf_op jit(solution)/shard_map/ppermute | solution.py:396
  6.2 16.4 %collective-permute-start = (bf16[256,1024]{1,0:T(8,128)(2,1)}, bf16[256,1024]{1,0:T(8,128)(2,1)}, u32[]{:S(2)}, u32[]{:S(2)}) collective-permute-start(bf16[256,1024]{1,0:T(8,128)(2,1)} %get-tuple-element.33.refs_0_), channel_id=1, source_target_pairs={{0,4},{1,5},{4,8},{5,9},{8,12},{9,13},{12,14},{13,15},{14,10},{15,... | collective-permute-start | bytes 1572872 | tf_op jit(solution)/shard_map/ppermute | solution.py:396
  6.3 39.1 %all-to-all-start = ((bf16[8,272,128]{2,1,0:T(8,128)(2,1)}), bf16[8,272,128]{2,1,0:T(8,128)(2,1)S(1)}, u32[]{:S(2)}, u32[]{:S(2)}) async-start(bf16[8,272,128]{2,1,0:T(8,128)(2,1)} %get-tuple-element.36), calls=%async_computation | async-start | bytes 1114112 | tf_op jit(solution)/shard_map/all_to_all | solution.py:411
  14.6 28.8 %copy-start.9 = (bf16[1024,128]{1,0:T(8,128)(2,1)}, bf16[1024,128]{1,0:T(8,128)(2,1)S(1)}, u32[]{:S(2)}) copy-start(bf16[1024,128]{1,0:T(8,128)(2,1)S(1)} %get-tuple-element.66) | copy-start | bytes 786436
  14.6 28.8 %copy-start.11 = (bf16[1024,128]{1,0:T(8,128)(2,1)}, bf16[1024,128]{1,0:T(8,128)(2,1)S(1)}, u32[]{:S(2)}) copy-start(bf16[1024,128]{1,0:T(8,128)(2,1)S(1)} %get-tuple-element.67) | copy-start | bytes 786436
  19.9 18.9 %collective-permute-start.3 = (bf16[256,1024]{1,0:T(8,128)(2,1)}, bf16[256,1024]{1,0:T(8,128)(2,1)}, u32[]{:S(2)}, u32[]{:S(2)}) collective-permute-start(bf16[256,1024]{1,0:T(8,128)(2,1)} %collective-permute-done.1.refs_2_), channel_id=1, source_target_pairs={{0,2},{1,3},{4,0},{5,1},{8,4},{9,5},{12,8},{13,9},{14,12},{15,13},... | collective-permute-start | bytes 1572872 | tf_op jit(solution)/shard_map/ppermute | solution.py:396
  22.7 16.8 %collective-permute-start.2 = (bf16[256,1024]{1,0:T(8,128)(2,1)}, bf16[256,1024]{1,0:T(8,128)(2,1)}, u32[]{:S(2)}, u32[]{:S(2)}) collective-permute-start(bf16[256,1024]{1,0:T(8,128)(2,1)} %collective-permute-done.refs_1_), channel_id=1, source_target_pairs={{0,4},{1,5},{4,8},{5,9},{8,12},{9,13},{12,14},{13,15},{14,10},{15,... | collective-permute-start | bytes 1572872 | tf_op jit(solution)/shard_map/ppermute | solution.py:396
  23.8 42.0 %copy-start.5 = (s32[2,8]{1,0:T(2,128)}, s32[2,8]{1,0:T(2,128)S(1)}, u32[]{:S(2)}) copy-start(s32[2,8]{1,0:T(2,128)S(1)} %fusion.13.ids) | copy-start | bytes 196
  38.8 15.9 %collective-permute-start.5 = (bf16[256,1024]{1,0:T(8,128)(2,1)}, bf16[256,1024]{1,0:T(8,128)(2,1)S(1)}, u32[]{:S(2)}, u32[]{:S(2)}) collective-permute-start(bf16[256,1024]{1,0:T(8,128)(2,1)} %collective-permute-done.3.refs_4_), channel_id=1, source_target_pairs={{0,2},{1,3},{4,0},{5,1},{8,4},{9,5},{12,8},{13,9},{14,12},{15,13},... | collective-permute-start | bytes 1572872 | tf_op jit(solution)/shard_map/ppermute | solution.py:396
  39.5 15.6 %collective-permute-start.4 = (bf16[256,1024]{1,0:T(8,128)(2,1)}, bf16[256,1024]{1,0:T(8,128)(2,1)}, u32[]{:S(2)}, u32[]{:S(2)}) collective-permute-start(bf16[256,1024]{1,0:T(8,128)(2,1)} %collective-permute-done.2.refs_3_), channel_id=1, source_target_pairs={{0,4},{1,5},{4,8},{5,9},{8,12},{9,13},{12,14},{13,15},{14,10},{15,... | collective-permute-start | bytes 1572872 | tf_op jit(solution)/shard_map/ppermute | solution.py:396
  45.5 13.3 %copy-start.10 = (bf16[1024,128]{1,0:T(8,128)(2,1)S(1)}, bf16[1024,128]{1,0:T(8,128)(2,1)}, u32[]{:S(2)}) copy-start(bf16[1024,128]{1,0:T(8,128)(2,1)} %copy-done.9) | copy-start | bytes 786436
  45.5 13.3 %copy-start.12 = (bf16[1024,128]{1,0:T(8,128)(2,1)S(1)}, bf16[1024,128]{1,0:T(8,128)(2,1)}, u32[]{:S(2)}) copy-start(bf16[1024,128]{1,0:T(8,128)(2,1)} %copy-done.11) | copy-start | bytes 786436
  45.5 19.0 %collective-permute-start.11 = (bf16[8,272,128]{2,1,0:T(8,128)(2,1)S(1)}, bf16[8,272,128]{2,1,0:T(8,128)(2,1)S(1)}, u32[]{:S(2)}, u32[]{:S(2)}) collective-permute-start(bf16[8,272,128]{2,1,0:T(8,128)(2,1)S(1)} %all-to-all-done.refs_6_), channel_id=1, source_target_pairs={{0,1},{1,0},{2,3},{3,2},{4,5},{5,4},{6,7},{7,6},{8,9},{9,8},{10,11... | collective-permute-start | bytes 1671176 | tf_op jit(solution)/shard_map/ppermute | solution.py:402
  49.8 14.7 %collective-permute-start.8 = (bf16[5,256,256]{2,1,0:T(8,128)(2,1)}, bf16[5,256,256]{2,1,0:T(8,128)(2,1)S(1)}, u32[]{:S(2)}, u32[]{:S(2)}) collective-permute-start(bf16[5,256,256]{2,1,0:T(8,128)(2,1)} %fusion.9.refs_0_), channel_id=1, source_target_pairs={{0,1},{1,0},{2,3},{3,2},{4,5},{5,4},{6,7},{7,6},{8,9},{9,8},{10,11... | collective-permute-start | bytes 1966088 | tf_op jit(solution)/shard_map/ppermute | solution.py:402
  56.1 7.0 %collective-permute-start.6 = (bf16[128,1024]{1,0:T(8,128)(2,1)S(1)}, bf16[128,1024]{1,0:T(8,128)(2,1)S(1)}, u32[]{:S(2)}, u32[]{:S(2)}) collective-permute-start(bf16[128,1024]{1,0:T(8,128)(2,1)S(1)} %get-tuple-element.34), channel_id=1, source_target_pairs={{0,4},{1,5},{4,8},{5,9},{8,12},{9,13},{12,14},{13,15},{14,10},{15,... | collective-permute-start | bytes 786440 | tf_op jit(solution)/shard_map/ppermute | solution.py:396
  57.7 6.4 %collective-permute-start.7 = (bf16[128,1024]{1,0:T(8,128)(2,1)S(1)}, bf16[128,1024]{1,0:T(8,128)(2,1)S(1)}, u32[]{:S(2)}, u32[]{:S(2)}) collective-permute-start(bf16[128,1024]{1,0:T(8,128)(2,1)S(1)} %get-tuple-element.35), channel_id=1, source_target_pairs={{0,2},{1,3},{4,0},{5,1},{8,4},{9,5},{12,8},{13,9},{14,12},{15,13},... | collective-permute-start | bytes 786440 | tf_op jit(solution)/shard_map/ppermute | solution.py:396
  60.5 4.1 %collective-permute-start.9 = (bf16[2,256,256]{2,1,0:T(8,128)(2,1)S(1)}, bf16[2,256,256]{2,1,0:T(8,128)(2,1)S(1)}, u32[]{:S(2)}, u32[]{:S(2)}) collective-permute-start(bf16[2,256,256]{2,1,0:T(8,128)(2,1)S(1)} %pad_maximum_fusion.1.refs_1_), channel_id=1, source_target_pairs={{0,1},{1,0},{2,3},{3,2},{4,5},{5,4},{6,7},{7,6},{8,9},{9,8},{10,11... | collective-permute-start | bytes 786440 | tf_op jit(solution)/shard_map/ppermute | solution.py:402
  64.1 15.2 %copy-start.7 = (bf16[256,1024]{1,0:T(8,128)(2,1)}, bf16[256,1024]{1,0:T(8,128)(2,1)S(1)}, u32[]{:S(2)}) copy-start(bf16[256,1024]{1,0:T(8,128)(2,1)S(1)} %constant_dynamic-update-slice_fusion.refs_7_) | copy-start | bytes 1572868
  64.4 1.4 %collective-permute-start.10 = (bf16[1,256,256]{2,1,0:T(8,128)(2,1)S(1)}, bf16[1,256,256]{2,1,0:T(8,128)(2,1)S(1)}, u32[]{:S(2)}, u32[]{:S(2)}) collective-permute-start(bf16[1,256,256]{2,1,0:T(8,128)(2,1)S(1)} %fusion.12.refs_2_), channel_id=1, source_target_pairs={{0,1},{1,0},{2,3},{3,2},{4,5},{5,4},{6,7},{7,6},{8,9},{9,8},{10,11... | collective-permute-start | bytes 393224 | tf_op jit(solution)/shard_map/ppermute | solution.py:402
  79.3 2.7 %collective-permute-start.12 = (bf16[8,256,256]{2,1,0:T(8,128)(2,1)S(1)}, bf16[8,256,256]{2,1,0:T(8,128)(2,1)S(1)}, u32[]{:S(2)}, u32[]{:S(2)}) collective-permute-start(bf16[8,256,256]{2,1,0:T(8,128)(2,1)S(1)} %get-tuple-element.38), channel_id=1, source_target_pairs={{0,1},{1,0},{2,3},{3,2},{4,5},{5,4},{6,7},{7,6},{8,9},{9,8},{10,11... | collective-permute-start | bytes 3145736 | tf_op jit(solution)/shard_map/ppermute | solution.py:402
  83.4 37.6 %all-to-all-start.1 = ((bf16[8,256,256]{2,1,0:T(8,128)(2,1)}), bf16[8,256,256]{2,1,0:T(8,128)(2,1)S(1)}, u32[]{:S(2)}, u32[]{:S(2)}) async-start(bf16[8,256,256]{2,1,0:T(8,128)(2,1)} %add_convert_fusion.grads), calls=%async_computation.1 | async-start | bytes 2097152 | tf_op jit(solution)/shard_map/all_to_all | solution.py:411
  93.0 1.7 %collective-permute-start.13 = (bf16[8,64,256]{2,1,0:T(8,128)(2,1)}, bf16[8,64,256]{2,1,0:T(8,128)(2,1)S(1)}, u32[]{:S(2)}, u32[]{:S(2)}) collective-permute-start(bf16[8,64,256]{2,1,0:T(8,128)(2,1)} %get-tuple-element.40), channel_id=1, source_target_pairs={{0,1},{1,0},{2,3},{3,2},{4,5},{5,4},{6,7},{7,6},{8,9},{9,8},{10,11... | collective-permute-start | bytes 786440 | tf_op jit(solution)/shard_map/ppermute | solution.py:402
  96.4 11.3 %collective-permute-start.20 = (bf16[64,256]{1,0:T(8,128)(2,1)S(1)}, bf16[64,256]{1,0:T(8,128)(2,1)S(1)}, u32[]{:S(2)}, u32[]{:S(2)}) collective-permute-start(bf16[64,256]{1,0:T(8,128)(2,1)S(1)} %get-tuple-element.56), channel_id=1, source_target_pairs={{0,14},{1,15},{2,0},{3,1},{4,2},{5,3},{6,4},{7,5},{8,6},{9,7},{10,... | collective-permute-start | bytes 98312 | tf_op jit(solution)/shard_map/ppermute | solution.py:408
  101.2 7.3 %collective-permute-start.19 = (bf16[64,256]{1,0:T(8,128)(2,1)S(1)}, bf16[64,256]{1,0:T(8,128)(2,1)S(1)}, u32[]{:S(2)}, u32[]{:S(2)}) collective-permute-start(bf16[64,256]{1,0:T(8,128)(2,1)S(1)} %get-tuple-element.57), channel_id=1, source_target_pairs={{0,12},{1,13},{2,14},{3,15},{4,0},{5,1},{6,2},{7,3},{8,4},{9,5},{1... | collective-permute-start | bytes 98312 | tf_op jit(solution)/shard_map/ppermute | solution.py:408
  101.7 24.1 %collective-permute-start.18 = (bf16[64,256]{1,0:T(8,128)(2,1)}, bf16[64,256]{1,0:T(8,128)(2,1)S(1)}, u32[]{:S(2)}, u32[]{:S(2)}) collective-permute-start(bf16[64,256]{1,0:T(8,128)(2,1)} %get-tuple-element.58), channel_id=1, source_target_pairs={{0,10},{1,11},{2,12},{3,13},{4,14},{5,15},{6,0},{7,1},{8,2},{9,3},... | collective-permute-start | bytes 98312 | tf_op jit(solution)/shard_map/ppermute | solution.py:408
  101.7 24.1 %collective-permute-start.17 = (bf16[64,256]{1,0:T(8,128)(2,1)}, bf16[64,256]{1,0:T(8,128)(2,1)}, u32[]{:S(2)}, u32[]{:S(2)}) collective-permute-start(bf16[64,256]{1,0:T(8,128)(2,1)} %get-tuple-element.59), channel_id=1, source_target_pairs={{0,8},{1,9},{2,10},{3,11},{4,12},{5,13},{6,14},{7,15},{8,0},{9,1},... | collective-permute-start | bytes 98312 | tf_op jit(solution)/shard_map/ppermute | solution.py:408
  104.7 21.2 %collective-permute-start.16 = (bf16[64,256]{1,0:T(8,128)(2,1)}, bf16[64,256]{1,0:T(8,128)(2,1)}, u32[]{:S(2)}, u32[]{:S(2)}) collective-permute-start(bf16[64,256]{1,0:T(8,128)(2,1)} %get-tuple-element.60), channel_id=1, source_target_pairs={{0,6},{1,7},{2,8},{3,9},{4,10},{5,11},{6,12},{7,13},{8,14},{9,15},... | collective-permute-start | bytes 98312 | tf_op jit(solution)/shard_map/ppermute | solution.py:408
  107.8 18.1 %collective-permute-start.15 = (bf16[64,256]{1,0:T(8,128)(2,1)}, bf16[64,256]{1,0:T(8,128)(2,1)}, u32[]{:S(2)}, u32[]{:S(2)}) collective-permute-start(bf16[64,256]{1,0:T(8,128)(2,1)} %get-tuple-element.61), channel_id=1, source_target_pairs={{0,4},{1,5},{2,6},{3,7},{4,8},{5,9},{6,10},{7,11},{8,12},{9,13},{1... | collective-permute-start | bytes 98312 | tf_op jit(solution)/shard_map/ppermute | solution.py:408
  108.5 17.4 %copy-start.6 = (s32[2,8]{1,0:T(2,128)S(1)}, s32[2,8]{1,0:T(2,128)}, u32[]{:S(2)}) copy-start(s32[2,8]{1,0:T(2,128)} %copy-done.5) | copy-start | bytes 196
  108.5 17.4 %collective-permute-start.14 = (bf16[64,256]{1,0:T(8,128)(2,1)}, bf16[64,256]{1,0:T(8,128)(2,1)}, u32[]{:S(2)}, u32[]{:S(2)}) collective-permute-start(bf16[64,256]{1,0:T(8,128)(2,1)} %get-tuple-element.62), channel_id=1, source_target_pairs={{0,2},{1,3},{2,4},{3,5},{4,6},{5,7},{6,8},{7,9},{8,10},{9,11},{10,... | collective-permute-start | bytes 98312 | tf_op jit(solution)/shard_map/ppermute | solution.py:408
  (5 other events, 32.3 us)
